TPU v7x, 256 devices: a whole 4x4x8 slice. The times are simulated.
256 devices in a mesh: ch: 4 (over z_hi, core), ha: 16 (over z_lo, x), dp: 4 (over y).
Axes of the slice: x: 4, y: 4, z: 8 (z_hi: 2, z_lo: 4; z = z_hi * 4 + z_lo), core: 2. Of those that a mesh axis runs over, the one named last changes fastest.
Arguments:
- features: bfloat16 [384, 4, 4, 32, 128], P('ch', 'dp', None, 'ha'), may hold values from -26 to 26
- frame_count: int32 [4], P('dp'), may hold values from 1 to 4, as said below
- norm1_gain: float32 [384], P('ch'), may hold values from 0.5 to 2
- norm1_shift: float32 [384], P('ch'), may hold values from -3 to 3
- qkv_weight: bfloat16 [384, 1152], replicated, may hold values from -0.51031036 to 0.51031036
- qkv_bias: float32 [1152], replicated, may hold values from -3 to 3
- out_weight: bfloat16 [384, 384], replicated, may hold values from -0.3125 to 0.3125
- out_bias: float32 [384], replicated, may hold values from -3 to 3
- norm2_gain: float32 [384], P('ch'), may hold values from 0.5 to 2
- norm2_shift: float32 [384], P('ch'), may hold values from -3 to 3
- conv_weight: bfloat16 [3, 3, 3, 384, 384], P(None, None, None, 'ch'), may hold values from -0.0625 to 0.0625
- conv_bias: float32 [384], P('ch'), may hold values from -3 to 3
- cotangent: bfloat16 [384, 4, 4, 32, 128], P('ch', 'dp', None, 'ha'), may hold values from -0.0234375 to 0.0234375
Outputs:
- mixed: bfloat16 [384, 4, 4, 32, 128], P('ch', 'dp', None, 'ha')
- weight_grad: float32 [3, 3, 3, 384, 384], P(None, None, None, 'ch')
Inputs may be any that keep to these rules, and one draw needn't show every extreme that they name: `frame_count`: some clip has all 4 frames valid and some clip only one.
All inputs are finite; a program needn't handle non-finite values.
Results may differ from a plain program's by a relative error of at most 0.015.
Values may be sent and summed in bfloat16 or wider, within the bound.
No kernel may reach another device: no remote copies, remote signals or barrier semaphores. Data moves between devices by JAX's collectives and lax.ppermute only.
A program may use at most 64 MiB of HBM per device.

v0:
```python
import itertools
import jax
import jax.numpy as jnp
from jax import lax
from jax.experimental import pallas as pl
from jax.experimental.pallas import tpu as pltpu
from jax.sharding import Mesh, PartitionSpec as P

EPS = 1e-06
SIZES = {"zh": 2, "co": 2, "zl": 4, "x": 4, "y": 4}
BF, F32 = jnp.bfloat16, jnp.float32
VMEM = 56 * 1024 * 1024


def permute(value, axes, target):
    sizes = [SIZES[a] for a in axes]

    def flat(index):
        at = 0
        for i, n in zip(index, sizes):
            at = at * n + i
        return at

    pairs = []
    for index in itertools.product(*[range(n) for n in sizes]):
        to = target(*index)
        if to is not None:
            pairs.append((flat(index), flat(to)))
    return lax.ppermute(value, axes, pairs)


def ring(value, axis):
    return [value] + [permute(value, (axis,), lambda i: ((i + s) % 4,)) for s in (1, 2, 3)]


def halo(last, first):
    def up(zl, x):
        at = zl * 4 + x + 1
        return (at // 4, at % 4) if at < 16 else None

    def down(zl, x):
        at = zl * 4 + x - 1
        return (at // 4, at % 4) if at >= 0 else None

    return permute(last, ("zl", "x"), up), permute(first, ("zl", "x"), down)


def spread(value, axes, count):
    copies = jnp.broadcast_to(value[None], (count,) + value.shape)
    return lax.all_to_all(copies, axes, 0, 0, tiled=True)


def cost(flops, size):
    return pl.CostEstimate(flops=flops, bytes_accessed=size, transcendentals=0)


def column(rows, place):
    lane = lax.broadcasted_iota(jnp.int32, (96, 128), 1)
    return jnp.sum(jnp.where(lane == place, rows, 0.0), axis=1, keepdims=True)


def pack_kernel(valid, frames, gain, shift, out):
    first = jnp.zeros((96, 128), F32)
    second = jnp.zeros((96, 128), F32)
    for f in range(4):
        data = frames[:, f * 256 : f * 256 + 256].astype(F32)
        data = jnp.where(f < valid[0], data, 0.0)
        square = data * data
        first += data[:, :128] + data[:, 128:]
        second += square[:, :128] + square[:, 128:]
    row = lax.broadcasted_iota(jnp.int32, (96, 128), 0) // 12
    lane = lax.broadcasted_iota(jnp.int32, (96, 128), 1)
    first = jnp.sum(first, axis=1, keepdims=True)
    second = jnp.sum(second, axis=1, keepdims=True)
    sums = jnp.where(row == lane, first, jnp.where(row + 8 == lane, second, 0.0))
    sums = jnp.sum(sums, axis=0, keepdims=True)
    pad = jnp.zeros((1, 32), F32)
    rows = jnp.concatenate(
        [
            sums,
            jnp.concatenate([gain[...], pad], axis=1),
            jnp.concatenate([shift[...], pad], axis=1),
            jnp.zeros((1, 128), F32),
        ],
        axis=0,
    )
    out[...] = jnp.broadcast_to(rows[None], out.shape)


def attend_kernel(
    at,
    packed,
    own0,
    own1,
    own2,
    own3,
    other0,
    other1,
    other2,
    other3,
    qkv,
    qkv_bias,
    out_weight,
    out_bias,
    hidden,
    sums,
    tokens,
    scores,
):
    co, slot, valid, frame = at[0], at[1], at[2], at[3]
    count = valid.astype(F32) * (12 * 32 * 128)
    group = lax.broadcasted_iota(jnp.int32, (96, 128), 0) // 12
    entry = lax.broadcasted_iota(jnp.int32, (96, 128), 0)
    for which, parts in ((co, (own0, own1, own2, own3)), (1 - co, (other0, other1, other2, other3))):
        for zh in range(2):
            c = 2 * zh + which
            table = jnp.sum(packed[c], axis=0)
            mean = column(table[0:1], group) / count
            var = column(table[0:1], group + 8) / count - mean * mean
            scale = lax.rsqrt(var + EPS)
            gain = column(packed[c, 0, 1:2], entry)
            shift = column(packed[c, 0, 2:3], entry)
            rows = pl.ds(pl.multiple_of(c * 96, 32), 96)
            for s in range(4):
                data = parts[s][zh * 96 : zh * 96 + 96, :].astype(F32)
                data = (data - mean) * scale * gain + shift
                tokens[rows, s * 1024 : s * 1024 + 1024] = data.astype(BF)
    lanes = pl.ds(pl.multiple_of(slot, 256), 256)
    queries = lax.dot_general(
        tokens[:, lanes], qkv[:, :384], (((0,), (0,)), ((), ())), preferred_element_type=F32
    )
    queries = (queries + qkv_bias[:, :384]).astype(BF)
    lifted = lax.dot_general(
        queries, qkv[:, 384:768], (((1,), (1,)), ((), ())), preferred_element_type=F32
    ).astype(BF)
    offset = jnp.sum(queries.astype(F32) * qkv_bias[:, 384:768], axis=1, keepdims=True)
    top = jnp.full((256, 128), -jnp.inf, F32)
    for j in range(8):
        piece = jnp.dot(lifted, tokens[:, j * 512 : j * 512 + 512], preferred_element_type=F32)
        piece = (piece + offset) * (384 ** (-0.5))
        scores[:, j * 512 : j * 512 + 512] = piece
        for i in range(4):
            top = jnp.maximum(top, piece[:, i * 128 : i * 128 + 128])
    top = jnp.max(top, axis=1, keepdims=True)
    total = jnp.zeros((256, 128), F32)
    acc = jnp.zeros((256, 384), F32)
    for j in range(8):
        ew = jnp.exp(scores[:, j * 512 : j * 512 + 512] - top)
        for i in range(4):
            total += ew[:, i * 128 : i * 128 + 128]
        acc += lax.dot_general(
            ew.astype(BF),
            tokens[:, j * 512 : j * 512 + 512],
            (((1,), (1,)), ((), ())),
            preferred_element_type=F32,
        )
    total = jnp.sum(total, axis=1, keepdims=True)
    acc = (acc / total).astype(BF)
    attended = jnp.dot(acc, qkv[:, 768:], preferred_element_type=F32)
    attended = (attended + qkv_bias[:, 768:]).astype(BF)
    update = lax.dot_general(
        out_weight[...], attended, (((0,), (1,)), ((), ())), preferred_element_type=F32
    )
    hidden[...] = (update + out_bias[...]).astype(BF)
    for which, part in ((co, own0), (1 - co, other0)):
        for zh in range(2):
            rows = pl.ds(pl.multiple_of((2 * zh + which) * 96, 32), 96)
            raw = part[zh * 96 : zh * 96 + 96, lanes].astype(F32)
            hidden[rows, :] = (raw + hidden[rows, :].astype(F32)).astype(BF)
    data = jnp.where(frame < valid, hidden[...].astype(F32), 0.0)
    first = jnp.sum(data, axis=1, keepdims=True)
    second = jnp.sum(data * data, axis=1, keepdims=True)
    row = lax.broadcasted_iota(jnp.int32, (384, 128), 0) // 12
    lane = lax.broadcasted_iota(jnp.int32, (384, 128), 1)
    table = jnp.where(row == lane, first, jnp.where(row + 32 == lane, second, 0.0))
    table = jnp.sum(table, axis=0, keepdims=True)
    sums[...] = jnp.broadcast_to(table[None], sums.shape)


def gate_kernel(at, packed, piece0, piece1, piece2, piece3, gain, shift, gated, hidden, held):
    ch, valid = at[0], at[1]
    count = valid.astype(F32) * (12 * 32 * 128)
    table = jnp.sum(packed[...], axis=0)
    group = lax.broadcasted_iota(jnp.int32, (96, 128), 0) // 12 + ch * 8
    mean = column(table, group) / count
    var = column(table, group + 32) / count - mean * mean
    scale = lax.rsqrt(var + EPS)
    for k, piece in enumerate((piece0, piece1, piece2, piece3)):
        held[ch ^ k] = piece[...]
    for f in range(4):
        data = held[f]
        hidden[:, f * 256 : f * 256 + 256] = data
        u = (data.astype(F32) - mean) * scale * gain[...] + shift[...]
        gated[:, f * 256 : f * 256 + 256] = (u / (1.0 + jnp.exp(-u))).astype(BF)


def shifted(g, kx):
    if kx == 1:
        return g
    lane = lax.broadcasted_iota(jnp.int32, g.shape, 1)
    if kx == 0:
        return jnp.where(lane == 0, 0.0, pltpu.roll(g, 1, 1))
    return jnp.where(lane == 127, 0.0, pltpu.roll(g, 127, 1))


def grad_kernel(at, clip0, clip1, clip2, clip3, cot, before, after, out, gs, cs):
    gs[864:, :] = jnp.zeros((32, 4096), BF)
    for s, clip in enumerate((clip0, clip1, clip2, clip3)):
        for kt in range(2):
            gs[kt * 288 : kt * 288 + 288, s * 1024 : s * 1024 + (2 - kt) * 256] = jnp.zeros(
                (288, (2 - kt) * 256), BF
            )
        for b in range(8):
            g = clip[:, b * 128 : b * 128 + 128].astype(F32)
            for kx in range(3):
                piece = shifted(g, kx).astype(BF)
                for kt in range(3):
                    to = b * 128 + (2 - kt) * 256
                    if to < 1024:
                        row = (kt * 3 + kx) * 96
                        gs[row : row + 96, s * 1024 + to : s * 1024 + to + 128] = piece
        k = lax.rem(s + at[0], 4)
        cs[96:192, s * 1024 : s * 1024 + 1024] = cot[k]
        for f in range(4):
            to = s * 1024 + f * 256
            cs[0:96, to : to + 128] = cot[k, :, f * 256 + 128 : f * 256 + 256]
            cs[0:96, to + 128 : to + 256] = after[k, :, f * 128 : f * 128 + 128]
            cs[192:288, to : to + 128] = before[k, :, f * 128 : f * 128 + 128]
            cs[192:288, to + 128 : to + 256] = cot[k, :, f * 256 : f * 256 + 128]
    table = lax.dot_general(
        cs[...], gs[...], (((1,), (1,)), ((), ())), preferred_element_type=F32
    ).astype(BF)
    for t in range(18):
        for l in range(7):
            out[t * 7 + l] = table[t * 16 : t * 16 + 16, l * 128 : l * 128 + 128]
    out[126:] = jnp.zeros((2, 16, 128), BF)


def join_kernel(at, table0, table1, table2, table3, out, held):
    for s, table in enumerate((table0, table1, table2, table3)):
        held[lax.rem(at[0] - s + 4, 4)] = table[...]
    for ky in range(3):
        for l in range(7):
            blocks = [
                held[j, (ky * 6 + t) * 7 + l] for j in range(4) for t in range(6)
            ]
            flipped = jnp.concatenate(blocks, axis=0).astype(F32).T
            lane = l * 128
            while lane < min(l * 128 + 128, 864):
                block = lane // 96
                end = min((block + 1) * 96, l * 128 + 128)
                row = ((block // 3 * 3 + ky) * 3 + block % 3) * 96 + lane % 96
                out[row : row + end - lane, :] = flipped[lane - l * 128 : end - l * 128, :]
                lane = end


def conv_kernel(clip, before, after, weight, out, stack):
    stack[:, :512] = jnp.zeros((864, 512), BF)
    for f in range(4):
        for p in range(4):
            if p == 0:
                g = before[:, f * 128 : f * 128 + 128]
            elif p == 3:
                g = after[:, f * 128 : f * 128 + 128]
            else:
                g = clip[:, f * 256 + p * 128 - 128 : f * 256 + p * 128]
            g = g.astype(F32)
            for kx in range(3):
                piece = shifted(g, kx).astype(BF)
                for ky in range(3):
                    r = p - ky
                    if 0 <= r < 2:
                        to = 512 + f * 256 + r * 128
                        row = (ky * 3 + kx) * 96
                        stack[row : row + 96, to : to + 128] = piece
    total = jnp.zeros((384, 1024), F32)
    for kt in range(3):
        total = total + jnp.dot(
            weight[kt], stack[:, kt * 256 : kt * 256 + 1024], preferred_element_type=F32
        )
    out[...] = total.astype(BF).reshape(4, 96, 1024)


def body(
    features,
    frame_count,
    norm1_gain,
    norm1_shift,
    qkv_weight,
    qkv_bias,
    out_weight,
    out_bias,
    norm2_gain,
    norm2_shift,
    conv_weight,
    conv_bias,
    cotangent,
):
    zh, co, zl = lax.axis_index("zh"), lax.axis_index("co"), lax.axis_index("zl")
    x, y = lax.axis_index("x"), lax.axis_index("y")
    ch = zh * 2 + co
    params = pltpu.CompilerParams(vmem_limit_bytes=VMEM)
    scalars = pl.BlockSpec(memory_space=pltpu.SMEM)
    whole = pl.BlockSpec(memory_space=pltpu.VMEM)
    frames = features.reshape(96, 4, 256)
    valid = frame_count[0]
    mask = (lax.iota(jnp.int32, 4) < valid).astype(F32)

    by_frame = jnp.repeat(frames.transpose(1, 0, 2), 2, axis=0)
    got = lax.all_to_all(by_frame, ("zh", "zl"), 0, 0, tiled=True)
    mine = got.reshape(2, 4, 96, 256).transpose(0, 2, 1, 3).reshape(192, 1024)
    parts = ring(mine, "x")
    others = [permute(p, ("co",), lambda i: (1 - i,)) for p in parts]

    packed = pl.pallas_call(
        pack_kernel,
        out_shape=jax.ShapeDtypeStruct((64, 4, 128), F32),
        in_specs=[scalars, whole, whole, whole],
        out_specs=whole,
        compiler_params=params,
        cost_estimate=cost(10**6, 200000),
        name="pack",
    )(frame_count, frames.reshape(96, 1024), norm1_gain[None], norm1_shift[None])
    packed = lax.all_to_all(packed, ("zh", "co", "zl", "x"), 0, 0, tiled=True)

    frame = 2 * zh + zl // 2
    at = jnp.stack([co, (2 * (zl % 2) + co) * 256, valid, frame]).astype(jnp.int32)
    hidden_q, packed = pl.pallas_call(
        attend_kernel,
        out_shape=(
            jax.ShapeDtypeStruct((384, 256), BF),
            jax.ShapeDtypeStruct((64, 1, 128), F32),
        ),
        in_specs=[scalars] + [whole] * 13,
        out_specs=(whole, whole),
        scratch_shapes=[pltpu.VMEM((384, 4096), BF), pltpu.VMEM((256, 4096), F32)],
        compiler_params=params,
        cost_estimate=cost(4 * 10**9, 20 * 10**6),
        name="attention",
    )(
        at,
        packed.reshape(4, 16, 4, 128),
        *parts,
        *others,
        qkv_weight,
        qkv_bias[None],
        out_weight,
        out_bias[:, None],
    )

    pieces = []
    for k in range(4):
        piece = lax.dynamic_slice(hidden_q, ((frame ^ k) * 96, 0), (96, 256))

        def to_channels(zh, co, zl, k=k):
            c = (2 * zh + zl // 2) ^ k
            return (c // 2, c % 2, 2 * (zl % 2) + co)

        pieces.append(permute(piece, ("zh", "co", "zl"), to_channels))

    packed = lax.all_to_all(packed, ("zh", "co", "zl", "x"), 0, 0, tiled=True)
    gated, hidden = pl.pallas_call(
        gate_kernel,
        out_shape=(jax.ShapeDtypeStruct((96, 1024), BF), jax.ShapeDtypeStruct((96, 1024), BF)),
        in_specs=[scalars] + [whole] * 7,
        out_specs=(whole, whole),
        scratch_shapes=[pltpu.VMEM((4, 96, 256), BF)],
        compiler_params=params,
        cost_estimate=cost(10**7, 10**6),
        name="gate",
    )(
        jnp.stack([ch, valid]).astype(jnp.int32),
        packed,
        *pieces,
        norm2_gain[:, None],
        norm2_shift[:, None],
    )

    masked = (cotangent.reshape(96, 4, 256) * mask.astype(BF)[None, :, None]).reshape(96, 1024)
    masked, _ = lax.optimization_barrier((masked, mine))
    blocks = jnp.stack(
        [
            permute(
                masked,
                ("zh", "co", "y"),
                lambda zh, co, y: (((y + k) % 4) // 2, (y + k) % 2, 2 * zh + co),
            )
            for k in range(4)
        ]
    )
    lines = blocks.reshape(4, 96, 4, 2, 128)
    before, after = halo(
        lines[:, :, :, 1].reshape(4, 96, 512), lines[:, :, :, 0].reshape(4, 96, 512)
    )

    clips = ring(gated, "y")
    table = pl.pallas_call(
        grad_kernel,
        out_shape=jax.ShapeDtypeStruct((128, 16, 128), BF),
        in_specs=[scalars] + [whole] * 7,
        out_specs=whole,
        scratch_shapes=[pltpu.VMEM((896, 4096), BF), pltpu.VMEM((288, 4096), BF)],
        compiler_params=params,
        cost_estimate=cost(4 * 10**9, 20 * 10**6),
        name="weight_grad",
    )((ch - y + 4).astype(jnp.int32)[None], *clips, blocks, before, after)
    shares = lax.all_to_all(table.reshape(16, 8, 16, 128), ("zl", "x"), 0, 0, tiled=True)
    share = jnp.sum(shares.astype(F32), axis=0).astype(BF)
    table = spread(share, ("zl", "x"), 16).reshape(128, 16, 128)
    weight_grad = pl.pallas_call(
        join_kernel,
        out_shape=jax.ShapeDtypeStruct((2592, 384), F32),
        in_specs=[scalars] + [whole] * 4,
        out_specs=whole,
        scratch_shapes=[pltpu.VMEM((4, 128, 16, 128), BF)],
        compiler_params=params,
        cost_estimate=cost(10**6, 6 * 10**6),
        name="join",
    )(y.astype(jnp.int32)[None], *ring(table, "y"))
    weight_grad = weight_grad.reshape(3, 3, 3, 96, 384)

    rows = gated.reshape(96, 4, 2, 128)
    before, after = halo(rows[:, :, 1].reshape(96, 512), rows[:, :, 0].reshape(96, 512))
    kernels = conv_weight.transpose(0, 4, 1, 2, 3).reshape(3, 384, 864)
    partial = pl.pallas_call(
        conv_kernel,
        out_shape=jax.ShapeDtypeStruct((4, 96, 1024), BF),
        scratch_shapes=[pltpu.VMEM((864, 1536), BF)],
        compiler_params=params,
        cost_estimate=cost(3 * 10**9, 12 * 10**6),
        name="convolution",
    )(gated, before, after, kernels)
    conv = lax.dynamic_index_in_dim(partial, ch, 0, keepdims=False).astype(F32)
    for k in range(1, 4):
        piece = lax.dynamic_index_in_dim(partial, ch ^ k, 0, keepdims=False)
        piece = permute(
            piece, ("zh", "co"), lambda zh, co, k=k: (zh ^ (k >> 1), co ^ (k & 1))
        )
        conv = conv + piece.astype(F32)
    mixed = hidden.astype(F32) + conv + conv_bias[:, None]
    mixed = (mixed.reshape(96, 4, 256) * mask[None, :, None]).astype(BF)
    return mixed.reshape(96, 1, 4, 2, 128), weight_grad


def solution(mesh):
    cut = Mesh(mesh.devices.reshape(2, 2, 4, 4, 4), ("zh", "co", "zl", "x", "y"))
    ch, ha = ("zh", "co"), ("zl", "x")
    maps = P(ch, "y", None, ha, None)
    placed = (
        maps,
        P("y"),
        P(ch),
        P(ch),
        P(),
        P(),
        P(),
        P(),
        P(ch),
        P(ch),
        P(None, None, None, ch, None),
        P(ch),
        maps,
    )
    return jax.shard_map(
        body,
        mesh=cut,
        in_specs=placed,
        out_specs=(maps, P(None, None, None, ch, None)),
        check_vma=False,
    )
```

profile of v0, /device:TPU:65, one launch (start us, length us, event | category | flops | bytes accessed | tf_op | source)
XLA Modules:
  0.0 224.8 jit_solution(5141468028627184171)
XLA Ops:
  0.6 1.1 reshape.79
  1.8 0.8 broadcast_in_dim.38
  2.6 7.7 %all-to-all-start.1 = ((bf16[8,96,256]{2,1,0:T(8,128)(2,1)}), bf16[8,96,256]{2,1,0:T(8,128)(2,1)S(1)}, u32[]{:S(2)}, u32[]{:S(2)}) async-start(bf16[8,96,256]{2,1,0:T(8,128)(2,1)} %bitcast.8), calls=%async_computation.1 | async-start | bytes 786432 | tf_op jit(solution)/shard_map/all_to_all | solution.py:310
  11.1 9.9 %all-to-all-done.1 = bf16[8,96,256]{2,1,0:T(8,128)(2,1)S(1)} async-done(((bf16[8,96,256]{2,1,0:T(8,128)(2,1)}), bf16[8,96,256]{2,1,0:T(8,128)(2,1)S(1)}, u32[]{:S(2)}, u32[]{:S(2)}) %all-to-all-start.1) | async-done | bytes 393248 | tf_op jit(solution)/shard_map/all_to_all | solution.py:310
  21.4 4.9 %collective-permute-start.19 = (bf16[96,1024]{1,0:T(8,128)(2,1)S(1)}, bf16[96,1024]{1,0:T(8,128)(2,1)S(1)}, u32[]{:S(2)}, u32[]{:S(2)}) collective-permute-start(bf16[96,1024]{1,0:T(8,128)(2,1)S(1)} %broadcast_multiply_fusion), channel_id=1, source_target_pairs={{0,0},{1,64},{2,128},{3,192},{64,1},{65,65},{66,129},{67,193},{128... | collective-permute-start | bytes 589832 | tf_op jit(solution)/shard_map/ppermute | solution.py:29
  26.4 4.8 %collective-permute-start.21 = (bf16[96,1024]{1,0:T(8,128)(2,1)S(1)}, bf16[96,1024]{1,0:T(8,128)(2,1)S(1)}, u32[]{:S(2)}, u32[]{:S(2)}) collective-permute-start(bf16[96,1024]{1,0:T(8,128)(2,1)S(1)} %broadcast_multiply_fusion), channel_id=1, source_target_pairs={{0,128},{1,192},{2,0},{3,64},{64,129},{65,193},{66,1},{67,65},{128... | collective-permute-start | bytes 589832 | tf_op jit(solution)/shard_map/ppermute | solution.py:29
  31.2 0.8 reshape_reshape.3.frames
  32.0 1.8 pack.1
  33.7 12.2 %all-to-all-start = ((f32[64,4,128]{2,1,0:T(4,128)}), f32[64,4,128]{2,1,0:T(4,128)S(1)}, u32[]{:S(2)}, u32[]{:S(2)}) async-start(f32[64,4,128]{2,1,0:T(4,128)} %pack.1), calls=%async_computation | async-start | bytes 262144 | tf_op jit(solution)/shard_map/all_to_all | solution.py:324
  46.6 0.8 broadcast_in_dim.46.out_bias
  48.0 1.2 collective-permute-start
  49.2 2.4 %collective-permute-start.1 = (bf16[192,1024]{1,0:T(8,128)(2,1)S(1)}, bf16[192,1024]{1,0:T(8,128)(2,1)}, u32[]{:S(2)}, u32[]{:S(2)}) collective-permute-start(bf16[192,1024]{1,0:T(8,128)(2,1)S(1)} %bitcast.75), channel_id=1, source_target_pairs={{0,8},{4,12},{8,0},{12,4},{1,9},{5,13},{9,1},{13,5},{2,10},{6,14},... | collective-permute-start | bytes 1179656 | tf_op jit(solution)/shard_map/ppermute | solution.py:29
  51.6 1.2 collective-permute-start.2
  52.9 1.3 collective-permute-start.3
  54.3 3.6 %collective-permute-start.22 = (bf16[96,1024]{1,0:T(8,128)(2,1)S(1)}, bf16[96,1024]{1,0:T(8,128)(2,1)S(1)}, u32[]{:S(2)}, u32[]{:S(2)}) collective-permute-start(bf16[96,1024]{1,0:T(8,128)(2,1)S(1)} %broadcast_multiply_fusion), channel_id=1, source_target_pairs={{0,192},{1,0},{2,64},{3,128},{64,193},{65,1},{66,65},{67,129},{128... | collective-permute-start | bytes 589832 | tf_op jit(solution)/shard_map/ppermute | solution.py:29
  58.0 8.3 %collective-permute-done.22 = bf16[96,1024]{1,0:T(8,128)(2,1)S(1)} collective-permute-done((bf16[96,1024]{1,0:T(8,128)(2,1)S(1)}, bf16[96,1024]{1,0:T(8,128)(2,1)S(1)}, u32[]{:S(2)}, u32[]{:S(2)}) %collective-permute-start.22) | collective-permute-done | bytes 196640 | tf_op jit(solution)/shard_map/ppermute | solution.py:29
  66.6 1.0 collective-permute-start.4
  67.6 2.3 %collective-permute-done.1.own2 = bf16[192,1024]{1,0:T(8,128)(2,1)} collective-permute-done((bf16[192,1024]{1,0:T(8,128)(2,1)S(1)}, bf16[192,1024]{1,0:T(8,128)(2,1)}, u32[]{:S(2)}, u32[]{:S(2)}) %collective-permute-start.1) | collective-permute-done | bytes 393248 | tf_op jit(solution)/shard_map/ppermute | solution.py:29
  69.9 1.1 collective-permute-start.5
  71.5 3.0 %collective-permute-start.23 = (bf16[4,96,512]{2,1,0:T(8,128)(2,1)S(1)}, bf16[4,96,512]{2,1,0:T(8,128)(2,1)S(1)}, u32[]{:S(2)}, u32[]{:S(2)}) collective-permute-start(bf16[4,96,512]{2,1,0:T(8,128)(2,1)S(1)} %reshape_squeeze.14), channel_id=1, source_target_pairs={{0,4},{4,8},{8,12},{12,16},{16,20},{20,24},{24,28},{28,32},{32,36}... | collective-permute-start | bytes 1179656 | tf_op jit(solution)/shard_map/ppermute | solution.py:29
  74.7 4.6 %collective-permute-start.24 = (bf16[4,96,512]{2,1,0:T(8,128)(2,1)S(1)}, bf16[4,96,512]{2,1,0:T(8,128)(2,1)S(1)}, u32[]{:S(2)}, u32[]{:S(2)}) collective-permute-start(bf16[4,96,512]{2,1,0:T(8,128)(2,1)S(1)} %reshape_squeeze.15), channel_id=1, source_target_pairs={{4,0},{8,4},{12,8},{16,12},{20,16},{24,20},{28,24},{32,28},{36,32}... | collective-permute-start | bytes 1179656 | tf_op jit(solution)/shard_map/ppermute | solution.py:29
  79.3 0.6 copy-done.11
  80.0 9.1 %attention.1 = (bf16[384,256]{1,0:T(8,128)(2,1)}, f32[64,1,128]{2,1,0:T(1,128)}) custom-call(s32[4]{0:T(128)} %pad_add_fusion.1.at, f32[4,16,4,128]{3,2,1,0:T(4,128)} %bitcast.81, bf16[192,1024]{1,0:T(8,128)(2,1)} %bitcast.78, bf16[192,1024]{1,0:T(8,128)(2,1)} %copy-done.23, bf16[192,1024]{1,0:T(8,128)(2,1)} %collective-permute-done.1.own2, ...), custom_call_target="tpu_custom_call" | custom-call | flops 4000000000 | bytes 20000000 | tf_op jit(solution)/shard_map/attention/pallas_call | solution.py:328
  89.1 0.9 constant_dynamic-slice_fusion
  90.0 2.4 %collective-permute-start.7 = (bf16[96,256]{1,0:T(8,128)(2,1)S(1)}, bf16[96,256]{1,0:T(8,128)(2,1)S(1)}, u32[]{:S(2)}, u32[]{:S(2)}) collective-permute-start(bf16[96,256]{1,0:T(8,128)(2,1)S(1)} %get-tuple-element.22), channel_id=1, source_target_pairs={{0,0},{16,32},{32,64},{48,96},{64,16},{80,48},{96,80},{112,112},{1... | collective-permute-start | bytes 147464 | tf_op jit(solution)/shard_map/ppermute | solution.py:29
  92.3 9.8 %all-to-all-start.2 = ((f32[64,1,128]{2,1,0:T(1,128)}), f32[64,1,128]{2,1,0:T(1,128)S(1)}, u32[]{:S(2)}, u32[]{:S(2)}) async-start(f32[64,1,128]{2,1,0:T(1,128)} %get-tuple-element.7), calls=%async_computation.2 | async-start | bytes 65536 | tf_op jit(solution)/shard_map/all_to_all | solution.py:361
  102.8 3.3 %collective-permute-start.9 = (bf16[96,256]{1,0:T(8,128)(2,1)S(1)}, bf16[96,256]{1,0:T(8,128)(2,1)S(1)}, u32[]{:S(2)}, u32[]{:S(2)}) collective-permute-start(bf16[96,256]{1,0:T(8,128)(2,1)S(1)} %get-tuple-element.20), channel_id=1, source_target_pairs={{0,128},{16,160},{32,192},{48,224},{64,144},{80,176},{96,208},{112... | collective-permute-start | bytes 147464 | tf_op jit(solution)/shard_map/ppermute | solution.py:29
  106.1 1.6 collective-permute-start.10
  107.7 0.7 pad_add_fusion.at
  108.4 0.7 copy.29.gain
  109.1 0.7 copy.30.shift
  109.8 3.1 %collective-permute-done.10.piece3 = bf16[96,256]{1,0:T(8,128)(2,1)S(1)} collective-permute-done((bf16[96,256]{1,0:T(8,128)(2,1)S(1)}, bf16[96,256]{1,0:T(8,128)(2,1)S(1)}, u32[]{:S(2)}, u32[]{:S(2)}) %collective-permute-start.10) | collective-permute-done | bytes 49184 | tf_op jit(solution)/shard_map/ppermute | solution.py:29
  114.1 1.9 gate.1
  116.5 3.4 %collective-permute-start.17 = (bf16[96,1024]{1,0:T(8,128)(2,1)}, bf16[96,1024]{1,0:T(8,128)(2,1)S(1)}, u32[]{:S(2)}, u32[]{:S(2)}) collective-permute-start(bf16[96,1024]{1,0:T(8,128)(2,1)} %get-tuple-element.10.clip.clip0), channel_id=1, source_target_pairs={{0,2},{1,3},{2,0},{3,1},{4,6},{5,7},{6,4},{7,5},{8,10},{9,11},{10,... | collective-permute-start | bytes 589832 | tf_op jit(solution)/shard_map/ppermute | solution.py:29
  119.9 2.1 collective-permute-start.18
  122.0 1.0 pad_maximum_fusion.cot
  123.3 5.7 %collective-permute-done.17.clip2 = bf16[96,1024]{1,0:T(8,128)(2,1)S(1)} collective-permute-done((bf16[96,1024]{1,0:T(8,128)(2,1)}, bf16[96,1024]{1,0:T(8,128)(2,1)S(1)}, u32[]{:S(2)}, u32[]{:S(2)}) %collective-permute-start.17) | collective-permute-done | bytes 196640 | tf_op jit(solution)/shard_map/ppermute | solution.py:29
  129.1 0.6 copy-done.25
  129.8 5.2 %weight_grad.1 = bf16[128,16,128]{2,1,0:T(8,128)(2,1)} custom-call(s32[1]{0:T(128)} %bitcast.22.at, bf16[96,1024]{1,0:T(8,128)(2,1)} %get-tuple-element.10.clip.clip0, bf16[96,1024]{1,0:T(8,128)(2,1)} %copy-done.24, bf16[96,1024]{1,0:T(8,128)(2,1)} %copy-done.25, bf16[96,1024]{1,0:T(8,128)(2,1)} %copy-done.26, bf16[4,96,1024]{2,1,0:T(8,128)(2,1)} %pad_maximum_fusion.cot, ...), custom_call_target="tpu_custom_call" | custom-call | flops 4000000000 | bytes 20000000 | tf_op jit(solution)/shard_map/weight_grad/pallas_call | solution.py:397
  135.0 21.3 %all_to_all.25 = bf16[16,8,16,128]{3,2,1,0:T(8,128)(2,1)S(1)} all-to-all(bf16[16,8,16,128]{3,2,1,0:T(8,128)(2,1)} %bitcast.73), channel_id=1, replica_groups=mesh['zh'=2,'co'=2,'zl'=4,'x'=4,'y'=4] {'zl','x'}, dimensions={0} | all-to-all | bytes 1048576 | tf_op jit(solution)/shard_map/all_to_all | solution.py:407
  156.4 0.9 broadcast_in_dim.45
  157.3 4.5 %all-to-all-start.4 = ((bf16[16,8,16,128]{3,2,1,0:T(8,128)(2,1)}), bf16[16,8,16,128]{3,2,1,0:T(8,128)(2,1)S(1)}, u32[]{:S(2)}, u32[]{:S(2)}) async-start(bf16[16,8,16,128]{3,2,1,0:T(8,128)(2,1)} %broadcast_in_dim.45), calls=%async_computation.4 | async-start | bytes 1048576 | tf_op jit(solution)/shard_map/all_to_all | solution.py:50
  161.8 1.1 slice_reduce_fusion
  163.0 3.1 %collective-permute-start.11 = (bf16[96,512]{1,0:T(8,128)(2,1)S(1)}, bf16[96,512]{1,0:T(8,128)(2,1)S(1)}, u32[]{:S(2)}, u32[]{:S(2)}) collective-permute-start(bf16[96,512]{1,0:T(8,128)(2,1)S(1)} %bitcast.82), channel_id=1, source_target_pairs={{0,4},{4,8},{8,12},{12,16},{16,20},{20,24},{24,28},{28,32},{32,36}... | collective-permute-start | bytes 294920 | tf_op jit(solution)/shard_map/ppermute | solution.py:29
  166.1 4.3 %collective-permute-start.12 = (bf16[96,512]{1,0:T(8,128)(2,1)S(1)}, bf16[96,512]{1,0:T(8,128)(2,1)S(1)}, u32[]{:S(2)}, u32[]{:S(2)}) collective-permute-start(bf16[96,512]{1,0:T(8,128)(2,1)S(1)} %bitcast.83), channel_id=1, source_target_pairs={{4,0},{8,4},{12,8},{16,12},{20,16},{24,20},{28,24},{32,28},{36,32}... | collective-permute-start | bytes 294920 | tf_op jit(solution)/shard_map/ppermute | solution.py:29
  170.4 2.4 %copy.33.weight = bf16[3,384,864]{2,1,0:T(8,128)(2,1)} copy(bf16[3,384,864]{1,2,0:T(8,128)(2,1)S(1)} %bitcast.65) | data formatting | bytes 3981312 | tf_op jit(solution)/shard_map/reshape | solution.py:424
  172.8 5.2 %collective-permute-done.11.before = bf16[96,512]{1,0:T(8,128)(2,1)S(1)} collective-permute-done((bf16[96,512]{1,0:T(8,128)(2,1)S(1)}, bf16[96,512]{1,0:T(8,128)(2,1)S(1)}, u32[]{:S(2)}, u32[]{:S(2)}) %collective-permute-start.11) | collective-permute-done | bytes 98336 | tf_op jit(solution)/shard_map/ppermute | solution.py:29
  178.0 0.6 copy-done.27
  178.7 0.6 copy-done.28
  179.3 5.4 %convolution.1 = bf16[4,96,1024]{2,1,0:T(8,128)(2,1)} custom-call(bf16[96,1024]{1,0:T(8,128)(2,1)} %get-tuple-element.10.clip.clip0, bf16[96,512]{1,0:T(8,128)(2,1)} %copy-done.27, bf16[96,512]{1,0:T(8,128)(2,1)} %copy-done.28, bf16[3,384,864]{2,1,0:T(8,128)(2,1)} %copy.33.weight), custom_call_target="tpu_custom_call" | custom-call | flops 3000000000 | bytes 12000000 | tf_op jit(solution)/shard_map/convolution/pallas_call | solution.py:425
  184.7 1.2 dynamic-slice_bitcast_fusion.2
  185.9 3.8 %collective-permute-start.15 = (bf16[96,1024]{1,0:T(8,128)(2,1)S(1)}, bf16[96,1024]{1,0:T(8,128)(2,1)S(1)}, u32[]{:S(2)}, u32[]{:S(2)}) collective-permute-start(bf16[96,1024]{1,0:T(8,128)(2,1)S(1)} %get-tuple-element.17), channel_id=1, source_target_pairs={{0,192},{64,128},{128,64},{192,0},{1,193},{65,129},{129,65},{193,1... | collective-permute-start | bytes 589832 | tf_op jit(solution)/shard_map/ppermute | solution.py:29
  189.7 2.9 %collective-permute-start.14 = (bf16[96,1024]{1,0:T(8,128)(2,1)S(1)}, bf16[96,1024]{1,0:T(8,128)(2,1)S(1)}, u32[]{:S(2)}, u32[]{:S(2)}) collective-permute-start(bf16[96,1024]{1,0:T(8,128)(2,1)S(1)} %get-tuple-element.18), channel_id=1, source_target_pairs={{0,128},{64,192},{128,0},{192,64},{1,129},{65,193},{129,1},{193,65... | collective-permute-start | bytes 589832 | tf_op jit(solution)/shard_map/ppermute | solution.py:29
  192.5 1.8 collective-permute-start.25
  194.3 2.2 collective-permute-start.26
  196.5 3.0 %collective-permute-done.15 = bf16[96,1024]{1,0:T(8,128)(2,1)S(1)} collective-permute-done((bf16[96,1024]{1,0:T(8,128)(2,1)S(1)}, bf16[96,1024]{1,0:T(8,128)(2,1)S(1)}, u32[]{:S(2)}, u32[]{:S(2)}) %collective-permute-start.15) | collective-permute-done | bytes 196640 | tf_op jit(solution)/shard_map/ppermute | solution.py:29
  199.6 2.5 %collective-permute-start.27 = (bf16[128,16,128]{2,1,0:T(8,128)(2,1)S(1)}, bf16[128,16,128]{2,1,0:T(8,128)(2,1)S(1)}, u32[]{:S(2)}, u32[]{:S(2)}) collective-permute-start(bf16[128,16,128]{2,1,0:T(8,128)(2,1)S(1)} %bitcast.63), channel_id=1, source_target_pairs={{0,3},{1,0},{2,1},{3,2},{4,7},{5,4},{6,5},{7,6},{8,11},{9,8},{10,9... | collective-permute-start | bytes 1572872 | tf_op jit(solution)/shard_map/ppermute | solution.py:29
  202.1 1.7 collective-permute-done.14
  203.8 1.1 fusion.3
  205.2 0.9 fusion.4
  206.1 0.8 collective-permute-done.25.table1
  206.9 12.5 %collective-permute-done.26.table2 = bf16[128,16,128]{2,1,0:T(8,128)(2,1)S(1)} collective-permute-done((bf16[128,16,128]{2,1,0:T(8,128)(2,1)S(1)}, bf16[128,16,128]{2,1,0:T(8,128)(2,1)S(1)}, u32[]{:S(2)}, u32[]{:S(2)}) %collective-permute-start.26) | collective-permute-done | bytes 524320 | tf_op jit(solution)/shard_map/ppermute | solution.py:29
  219.4 0.8 copy-done.4
  220.4 4.4 %join.1 = f32[2592,384]{1,0:T(8,128)} custom-call(s32[1]{0:T(128)} %bitcast.21.at, bf16[128,16,128]{2,1,0:T(8,128)(2,1)} %bitcast.64, bf16[128,16,128]{2,1,0:T(8,128)(2,1)} %copy-done.3, bf16[128,16,128]{2,1,0:T(8,128)(2,1)} %copy-done.4, bf16[128,16,128]{2,1,0:T(8,128)(2,1)} %copy-done.5), custom_call_target="tpu_custom_call" | custom-call | flops 1000000 | bytes 6000000 | tf_op jit(solution)/shard_map/join/pallas_call | solution.py:410
  (107 shorter events, 6.7 us)
Async XLA Ops:
  0.6 10.3 %copy-start.8 = (bf16[96,1,4,2,128]{4,3,2,1,0:T(2,128)(2,1)S(1)}, bf16[96,1,4,2,128]{4,3,2,1,0:T(2,128)(2,1)}, u32[]{:S(2)}) copy-start(bf16[96,1,4,2,128]{4,3,2,1,0:T(2,128)(2,1)} %param.25) | copy-start | bytes 589828
  1.7 29.5 %copy-start.2 = (bf16[96,1,4,2,128]{4,3,2,1,0:T(2,128)(2,1)S(1)}, bf16[96,1,4,2,128]{4,3,2,1,0:T(2,128)(2,1)}, u32[]{:S(2)}) copy-start(bf16[96,1,4,2,128]{4,3,2,1,0:T(2,128)(2,1)} %param.13) | copy-start | bytes 589828
  2.6 43.4 %copy-start.16 = (f32[1152]{0:T(1024)S(1)}, f32[1152]{0:T(1024)}, u32[]{:S(2)}) copy-start(f32[1152]{0:T(1024)} %param.18) | copy-start | bytes 13828
  2.6 44.0 %copy-start.17 = (f32[384]{0:T(512)S(1)}, f32[384]{0:T(512)}, u32[]{:S(2)}) copy-start(f32[384]{0:T(512)} %param.20) | copy-start | bytes 4612
  2.6 18.5 %all-to-all-start.1 = ((bf16[8,96,256]{2,1,0:T(8,128)(2,1)}), bf16[8,96,256]{2,1,0:T(8,128)(2,1)S(1)}, u32[]{:S(2)}, u32[]{:S(2)}) async-start(bf16[8,96,256]{2,1,0:T(8,128)(2,1)} %bitcast.8), calls=%async_computation.1 | async-start | bytes 786432 | tf_op jit(solution)/shard_map/all_to_all | solution.py:310
  21.4 49.7 %copy-start.6 = (bf16[24,8,4,256]{3,1,2,0:T(8,128)(2,1)}, bf16[24,8,4,256]{3,1,2,0:T(8,128)(2,1)S(1)}, u32[]{:S(2)}) copy-start(bf16[24,8,4,256]{3,1,2,0:T(8,128)(2,1)S(1)} %copy.41) | copy-start | bytes 1179652
  21.4 30.2 %collective-permute-start.19 = (bf16[96,1024]{1,0:T(8,128)(2,1)S(1)}, bf16[96,1024]{1,0:T(8,128)(2,1)S(1)}, u32[]{:S(2)}, u32[]{:S(2)}) collective-permute-start(bf16[96,1024]{1,0:T(8,128)(2,1)S(1)} %broadcast_multiply_fusion), channel_id=1, source_target_pairs={{0,0},{1,64},{2,128},{3,192},{64,1},{65,65},{66,129},{67,193},{128... | collective-permute-start | bytes 589832 | tf_op jit(solution)/shard_map/ppermute | solution.py:29
  26.3 26.6 %collective-permute-start.20 = (bf16[96,1024]{1,0:T(8,128)(2,1)S(1)}, bf16[96,1024]{1,0:T(8,128)(2,1)S(1)}, u32[]{:S(2)}, u32[]{:S(2)}) collective-permute-start(bf16[96,1024]{1,0:T(8,128)(2,1)S(1)} %broadcast_multiply_fusion), channel_id=1, source_target_pairs={{0,64},{1,128},{2,192},{3,0},{64,65},{65,129},{66,193},{67,1},{128... | collective-permute-start | bytes 589832 | tf_op jit(solution)/shard_map/ppermute | solution.py:29
  26.4 27.9 %collective-permute-start.21 = (bf16[96,1024]{1,0:T(8,128)(2,1)S(1)}, bf16[96,1024]{1,0:T(8,128)(2,1)S(1)}, u32[]{:S(2)}, u32[]{:S(2)}) collective-permute-start(bf16[96,1024]{1,0:T(8,128)(2,1)S(1)} %broadcast_multiply_fusion), channel_id=1, source_target_pairs={{0,128},{1,192},{2,0},{3,64},{64,129},{65,193},{66,1},{67,65},{128... | collective-permute-start | bytes 589832 | tf_op jit(solution)/shard_map/ppermute | solution.py:29
  33.7 45.5 %all-to-all-start = ((f32[64,4,128]{2,1,0:T(4,128)}), f32[64,4,128]{2,1,0:T(4,128)S(1)}, u32[]{:S(2)}, u32[]{:S(2)}) async-start(f32[64,4,128]{2,1,0:T(4,128)} %pack.1), calls=%async_computation | async-start | bytes 262144 | tf_op jit(solution)/shard_map/all_to_all | solution.py:324
  48.0 18.6 %collective-permute-start = (bf16[192,1024]{1,0:T(8,128)(2,1)S(1)}, bf16[192,1024]{1,0:T(8,128)(2,1)S(1)}, u32[]{:S(2)}, u32[]{:S(2)}) collective-permute-start(bf16[192,1024]{1,0:T(8,128)(2,1)S(1)} %bitcast.74), channel_id=1, source_target_pairs={{0,4},{4,8},{8,12},{12,0},{1,5},{5,9},{9,13},{13,1},{2,6},{6,10},{... | collective-permute-start | bytes 1179656 | tf_op jit(solution)/shard_map/ppermute | solution.py:29
  49.2 20.7 %collective-permute-start.1 = (bf16[192,1024]{1,0:T(8,128)(2,1)S(1)}, bf16[192,1024]{1,0:T(8,128)(2,1)}, u32[]{:S(2)}, u32[]{:S(2)}) collective-permute-start(bf16[192,1024]{1,0:T(8,128)(2,1)S(1)} %bitcast.75), channel_id=1, source_target_pairs={{0,8},{4,12},{8,0},{12,4},{1,9},{5,13},{9,1},{13,5},{2,10},{6,14},... | collective-permute-start | bytes 1179656 | tf_op jit(solution)/shard_map/ppermute | solution.py:29
  51.6 19.4 %collective-permute-start.2 = (bf16[192,1024]{1,0:T(8,128)(2,1)S(1)}, bf16[192,1024]{1,0:T(8,128)(2,1)}, u32[]{:S(2)}, u32[]{:S(2)}) collective-permute-start(bf16[192,1024]{1,0:T(8,128)(2,1)S(1)} %bitcast.76), channel_id=1, source_target_pairs={{0,12},{4,0},{8,4},{12,8},{1,13},{5,1},{9,5},{13,9},{2,14},{6,2},{... | collective-permute-start | bytes 1179656 | tf_op jit(solution)/shard_map/ppermute | solution.py:29
  52.9 21.8 %collective-permute-start.3 = (bf16[192,1024]{1,0:T(8,128)(2,1)S(1)}, bf16[192,1024]{1,0:T(8,128)(2,1)}, u32[]{:S(2)}, u32[]{:S(2)}) collective-permute-start(bf16[192,1024]{1,0:T(8,128)(2,1)S(1)} %bitcast.77), channel_id=1, source_target_pairs={{0,64},{64,0},{1,65},{65,1},{2,66},{66,2},{3,67},{67,3},{4,68},{68... | collective-permute-start | bytes 1179656 | tf_op jit(solution)/shard_map/ppermute | solution.py:29
  54.3 12.0 %collective-permute-start.22 = (bf16[96,1024]{1,0:T(8,128)(2,1)S(1)}, bf16[96,1024]{1,0:T(8,128)(2,1)S(1)}, u32[]{:S(2)}, u32[]{:S(2)}) collective-permute-start(bf16[96,1024]{1,0:T(8,128)(2,1)S(1)} %broadcast_multiply_fusion), channel_id=1, source_target_pairs={{0,192},{1,0},{2,64},{3,128},{64,193},{65,1},{66,65},{67,129},{128... | collective-permute-start | bytes 589832 | tf_op jit(solution)/shard_map/ppermute | solution.py:29
  66.6 12.8 %copy-start.23 = (bf16[192,1024]{1,0:T(8,128)(2,1)}, bf16[192,1024]{1,0:T(8,128)(2,1)S(1)}, u32[]{:S(2)}) copy-start(bf16[192,1024]{1,0:T(8,128)(2,1)S(1)} %collective-permute-done.own1) | copy-start | bytes 1179652
  66.6 12.7 %collective-permute-start.4 = (bf16[192,1024]{1,0:T(8,128)(2,1)S(1)}, bf16[192,1024]{1,0:T(8,128)(2,1)}, u32[]{:S(2)}, u32[]{:S(2)}) collective-permute-start(bf16[192,1024]{1,0:T(8,128)(2,1)S(1)} %collective-permute-done.own1), channel_id=1, source_target_pairs={{0,64},{64,0},{1,65},{65,1},{2,66},{66,2},{3,67},{67,3},{4,68},{68... | collective-permute-start | bytes 1179656 | tf_op jit(solution)/shard_map/ppermute | solution.py:29
  69.9 9.4 %collective-permute-start.5 = (bf16[192,1024]{1,0:T(8,128)(2,1)}, bf16[192,1024]{1,0:T(8,128)(2,1)}, u32[]{:S(2)}, u32[]{:S(2)}) collective-permute-start(bf16[192,1024]{1,0:T(8,128)(2,1)} %collective-permute-done.1.own2), channel_id=1, source_target_pairs={{0,64},{64,0},{1,65},{65,1},{2,66},{66,2},{3,67},{67,3},{4,68},{68... | collective-permute-start | bytes 1179656 | tf_op jit(solution)/shard_map/ppermute | solution.py:29
  71.0 8.3 %collective-permute-start.6 = (bf16[192,1024]{1,0:T(8,128)(2,1)}, bf16[192,1024]{1,0:T(8,128)(2,1)}, u32[]{:S(2)}, u32[]{:S(2)}) collective-permute-start(bf16[192,1024]{1,0:T(8,128)(2,1)} %collective-permute-done.2.own3), channel_id=1, source_target_pairs={{0,64},{64,0},{1,65},{65,1},{2,66},{66,2},{3,67},{67,3},{4,68},{68... | collective-permute-start | bytes 1179656 | tf_op jit(solution)/shard_map/ppermute | solution.py:29
  71.5 51.5 %collective-permute-start.23 = (bf16[4,96,512]{2,1,0:T(8,128)(2,1)S(1)}, bf16[4,96,512]{2,1,0:T(8,128)(2,1)S(1)}, u32[]{:S(2)}, u32[]{:S(2)}) collective-permute-start(bf16[4,96,512]{2,1,0:T(8,128)(2,1)S(1)} %reshape_squeeze.14), channel_id=1, source_target_pairs={{0,4},{4,8},{8,12},{12,16},{16,20},{20,24},{24,28},{28,32},{32,36}... | collective-permute-start | bytes 1179656 | tf_op jit(solution)/shard_map/ppermute | solution.py:29
  74.7 48.3 %collective-permute-start.24 = (bf16[4,96,512]{2,1,0:T(8,128)(2,1)S(1)}, bf16[4,96,512]{2,1,0:T(8,128)(2,1)S(1)}, u32[]{:S(2)}, u32[]{:S(2)}) collective-permute-start(bf16[4,96,512]{2,1,0:T(8,128)(2,1)S(1)} %reshape_squeeze.15), channel_id=1, source_target_pairs={{4,0},{8,4},{12,8},{16,12},{20,16},{24,20},{28,24},{32,28},{36,32}... | collective-permute-start | bytes 1179656 | tf_op jit(solution)/shard_map/ppermute | solution.py:29
  79.3 0.7 copy-start.11
  80.0 28.4 %copy-start.18 = (f32[96]{0:T(128)S(1)}, f32[96]{0:T(128)}, u32[]{:S(2)}) copy-start(f32[96]{0:T(128)} %param.21) | copy-start | bytes 1156
  80.0 29.1 %copy-start.19 = (f32[96]{0:T(128)S(1)}, f32[96]{0:T(128)}, u32[]{:S(2)}) copy-start(f32[96]{0:T(128)} %param.22) | copy-start | bytes 1156
  90.0 16.1 %collective-permute-start.7 = (bf16[96,256]{1,0:T(8,128)(2,1)S(1)}, bf16[96,256]{1,0:T(8,128)(2,1)S(1)}, u32[]{:S(2)}, u32[]{:S(2)}) collective-permute-start(bf16[96,256]{1,0:T(8,128)(2,1)S(1)} %get-tuple-element.22), channel_id=1, source_target_pairs={{0,0},{16,32},{32,64},{48,96},{64,16},{80,48},{96,80},{112,112},{1... | collective-permute-start | bytes 147464 | tf_op jit(solution)/shard_map/ppermute | solution.py:29
  92.3 20.6 %all-to-all-start.2 = ((f32[64,1,128]{2,1,0:T(1,128)}), f32[64,1,128]{2,1,0:T(1,128)S(1)}, u32[]{:S(2)}, u32[]{:S(2)}) async-start(f32[64,1,128]{2,1,0:T(1,128)} %get-tuple-element.7), calls=%async_computation.2 | async-start | bytes 65536 | tf_op jit(solution)/shard_map/all_to_all | solution.py:361
  102.2 7.6 %collective-permute-start.8 = (bf16[96,256]{1,0:T(8,128)(2,1)S(1)}, bf16[96,256]{1,0:T(8,128)(2,1)S(1)}, u32[]{:S(2)}, u32[]{:S(2)}) collective-permute-start(bf16[96,256]{1,0:T(8,128)(2,1)S(1)} %get-tuple-element.21), channel_id=1, source_target_pairs={{0,64},{16,96},{32,0},{48,32},{64,80},{80,112},{96,16},{112,48},{1... | collective-permute-start | bytes 147464 | tf_op jit(solution)/shard_map/ppermute | solution.py:29
  102.8 7.1 %collective-permute-start.9 = (bf16[96,256]{1,0:T(8,128)(2,1)S(1)}, bf16[96,256]{1,0:T(8,128)(2,1)S(1)}, u32[]{:S(2)}, u32[]{:S(2)}) collective-permute-start(bf16[96,256]{1,0:T(8,128)(2,1)S(1)} %get-tuple-element.20), channel_id=1, source_target_pairs={{0,128},{16,160},{32,192},{48,224},{64,144},{80,176},{96,208},{112... | collective-permute-start | bytes 147464 | tf_op jit(solution)/shard_map/ppermute | solution.py:29
  106.1 6.8 %copy-start.12 = (bf16[96,256]{1,0:T(8,128)(2,1)}, bf16[96,256]{1,0:T(8,128)(2,1)S(1)}, u32[]{:S(2)}) copy-start(bf16[96,256]{1,0:T(8,128)(2,1)S(1)} %collective-permute-done.7.piece0) | copy-start | bytes 147460
  106.1 6.8 %collective-permute-start.10 = (bf16[96,256]{1,0:T(8,128)(2,1)S(1)}, bf16[96,256]{1,0:T(8,128)(2,1)S(1)}, u32[]{:S(2)}, u32[]{:S(2)}) collective-permute-start(bf16[96,256]{1,0:T(8,128)(2,1)S(1)} %get-tuple-element.19), channel_id=1, source_target_pairs={{0,192},{16,224},{32,128},{48,160},{64,208},{80,240},{96,144},{112... | collective-permute-start | bytes 147464 | tf_op jit(solution)/shard_map/ppermute | solution.py:29
  109.8 3.1 %copy-start.13 = (bf16[96,256]{1,0:T(8,128)(2,1)}, bf16[96,256]{1,0:T(8,128)(2,1)S(1)}, u32[]{:S(2)}) copy-start(bf16[96,256]{1,0:T(8,128)(2,1)S(1)} %collective-permute-done.8.piece1) | copy-start | bytes 147460
  109.8 3.1 %copy-start.14 = (bf16[96,256]{1,0:T(8,128)(2,1)}, bf16[96,256]{1,0:T(8,128)(2,1)S(1)}, u32[]{:S(2)}) copy-start(bf16[96,256]{1,0:T(8,128)(2,1)S(1)} %collective-permute-done.9.piece2) | copy-start | bytes 147460
  112.9 0.6 copy-start.15
  113.5 0.6 copy-start.10
  116.1 7.3 %collective-permute-start.16 = (bf16[96,1024]{1,0:T(8,128)(2,1)}, bf16[96,1024]{1,0:T(8,128)(2,1)S(1)}, u32[]{:S(2)}, u32[]{:S(2)}) collective-permute-start(bf16[96,1024]{1,0:T(8,128)(2,1)} %get-tuple-element.10.clip.clip0), channel_id=1, source_target_pairs={{0,1},{1,2},{2,3},{3,0},{4,5},{5,6},{6,7},{7,4},{8,9},{9,10},{10,1... | collective-permute-start | bytes 589832 | tf_op jit(solution)/shard_map/ppermute | solution.py:29
  116.5 12.6 %collective-permute-start.17 = (bf16[96,1024]{1,0:T(8,128)(2,1)}, bf16[96,1024]{1,0:T(8,128)(2,1)S(1)}, u32[]{:S(2)}, u32[]{:S(2)}) collective-permute-start(bf16[96,1024]{1,0:T(8,128)(2,1)} %get-tuple-element.10.clip.clip0), channel_id=1, source_target_pairs={{0,2},{1,3},{2,0},{3,1},{4,6},{5,7},{6,4},{7,5},{8,10},{9,11},{10,... | collective-permute-start | bytes 589832 | tf_op jit(solution)/shard_map/ppermute | solution.py:29
  119.9 9.1 %collective-permute-start.18 = (bf16[96,1024]{1,0:T(8,128)(2,1)}, bf16[96,1024]{1,0:T(8,128)(2,1)S(1)}, u32[]{:S(2)}, u32[]{:S(2)}) collective-permute-start(bf16[96,1024]{1,0:T(8,128)(2,1)} %get-tuple-element.10.clip.clip0), channel_id=1, source_target_pairs={{0,3},{1,0},{2,1},{3,2},{4,7},{5,4},{6,5},{7,6},{8,11},{9,8},{10,9... | collective-permute-start | bytes 589832 | tf_op jit(solution)/shard_map/ppermute | solution.py:29
  123.0 6.1 %copy-start.21 = (bf16[4,96,512]{2,1,0:T(8,128)(2,1)}, bf16[4,96,512]{2,1,0:T(8,128)(2,1)S(1)}, u32[]{:S(2)}) copy-start(bf16[4,96,512]{2,1,0:T(8,128)(2,1)S(1)} %collective-permute-done.23.before) | copy-start | bytes 1179652
  123.0 6.1 %copy-start.22 = (bf16[4,96,512]{2,1,0:T(8,128)(2,1)}, bf16[4,96,512]{2,1,0:T(8,128)(2,1)S(1)}, u32[]{:S(2)}) copy-start(bf16[4,96,512]{2,1,0:T(8,128)(2,1)S(1)} %collective-permute-done.24.after) | copy-start | bytes 1179652
  123.3 5.7 %copy-start.24 = (bf16[96,1024]{1,0:T(8,128)(2,1)}, bf16[96,1024]{1,0:T(8,128)(2,1)S(1)}, u32[]{:S(2)}) copy-start(bf16[96,1024]{1,0:T(8,128)(2,1)S(1)} %collective-permute-done.16.clip1) | copy-start | bytes 589828
  129.1 0.7 copy-start.25
  129.1 0.8 copy-start.26
  135.0 26.7 %copy-start.9 = (bf16[96,1024]{1,0:T(8,128)(2,1)S(1)}, bf16[96,1024]{1,0:T(8,128)(2,1)}, u32[]{:S(2)}) copy-start(bf16[96,1024]{1,0:T(8,128)(2,1)} %get-tuple-element.10.clip.clip0) | copy-start | bytes 589828
  135.0 35.4 %copy-start.1 = (bf16[3,3,3,96,384]{4,3,2,1,0:T(8,128)(2,1)S(1)}, bf16[3,3,3,96,384]{4,3,2,1,0:T(8,128)(2,1)}, u32[]{:S(2)}) copy-start(bf16[3,3,3,96,384]{4,3,2,1,0:T(8,128)(2,1)} %param.23) | copy-start | bytes 5971972
  157.3 35.3 %all-to-all-start.4 = ((bf16[16,8,16,128]{3,2,1,0:T(8,128)(2,1)}), bf16[16,8,16,128]{3,2,1,0:T(8,128)(2,1)S(1)}, u32[]{:S(2)}, u32[]{:S(2)}) async-start(bf16[16,8,16,128]{3,2,1,0:T(8,128)(2,1)} %broadcast_in_dim.45), calls=%async_computation.4 | async-start | bytes 1048576 | tf_op jit(solution)/shard_map/all_to_all | solution.py:50
  163.0 15.1 %collective-permute-start.11 = (bf16[96,512]{1,0:T(8,128)(2,1)S(1)}, bf16[96,512]{1,0:T(8,128)(2,1)S(1)}, u32[]{:S(2)}, u32[]{:S(2)}) collective-permute-start(bf16[96,512]{1,0:T(8,128)(2,1)S(1)} %bitcast.82), channel_id=1, source_target_pairs={{0,4},{4,8},{8,12},{12,16},{16,20},{20,24},{24,28},{28,32},{32,36}... | collective-permute-start | bytes 294920 | tf_op jit(solution)/shard_map/ppermute | solution.py:29
  166.1 11.9 %collective-permute-start.12 = (bf16[96,512]{1,0:T(8,128)(2,1)S(1)}, bf16[96,512]{1,0:T(8,128)(2,1)S(1)}, u32[]{:S(2)}, u32[]{:S(2)}) collective-permute-start(bf16[96,512]{1,0:T(8,128)(2,1)S(1)} %bitcast.83), channel_id=1, source_target_pairs={{4,0},{8,4},{12,8},{16,12},{20,16},{24,20},{28,24},{32,28},{36,32}... | collective-permute-start | bytes 294920 | tf_op jit(solution)/shard_map/ppermute | solution.py:29
  172.8 31.0 %copy-start.7 = (bf16[96,1024]{1,0:T(8,128)(2,1)S(1)}, bf16[96,1024]{1,0:T(8,128)(2,1)}, u32[]{:S(2)}) copy-start(bf16[96,1024]{1,0:T(8,128)(2,1)} %get-tuple-element.9) | copy-start | bytes 589828
  172.8 31.0 %copy-start.20 = (f32[96]{0:T(128)S(1)}, f32[96]{0:T(128)}, u32[]{:S(2)}) copy-start(f32[96]{0:T(128)} %param.24) | copy-start | bytes 1156
  178.0 0.7 copy-start.27
  178.7 0.6 copy-start.28
  185.9 13.7 %collective-permute-start.15 = (bf16[96,1024]{1,0:T(8,128)(2,1)S(1)}, bf16[96,1024]{1,0:T(8,128)(2,1)S(1)}, u32[]{:S(2)}, u32[]{:S(2)}) collective-permute-start(bf16[96,1024]{1,0:T(8,128)(2,1)S(1)} %get-tuple-element.17), channel_id=1, source_target_pairs={{0,192},{64,128},{128,64},{192,0},{1,193},{65,129},{129,65},{193,1... | collective-permute-start | bytes 589832 | tf_op jit(solution)/shard_map/ppermute | solution.py:29
  189.7 14.1 %collective-permute-start.14 = (bf16[96,1024]{1,0:T(8,128)(2,1)S(1)}, bf16[96,1024]{1,0:T(8,128)(2,1)S(1)}, u32[]{:S(2)}, u32[]{:S(2)}) collective-permute-start(bf16[96,1024]{1,0:T(8,128)(2,1)S(1)} %get-tuple-element.18), channel_id=1, source_target_pairs={{0,128},{64,192},{128,0},{192,64},{1,129},{65,193},{129,1},{193,65... | collective-permute-start | bytes 589832 | tf_op jit(solution)/shard_map/ppermute | solution.py:29
  192.5 11.3 %collective-permute-start.13 = (bf16[96,1024]{1,0:T(8,128)(2,1)S(1)}, bf16[96,1024]{1,0:T(8,128)(2,1)S(1)}, u32[]{:S(2)}, u32[]{:S(2)}) collective-permute-start(bf16[96,1024]{1,0:T(8,128)(2,1)S(1)} %get-tuple-element.16), channel_id=1, source_target_pairs={{0,64},{64,0},{128,192},{192,128},{1,65},{65,1},{129,193},{193,129... | collective-permute-start | bytes 589832 | tf_op jit(solution)/shard_map/ppermute | solution.py:29
  192.5 26.9 %copy-start = (bf16[16,8,16,128]{3,2,1,0:T(8,128)(2,1)}, bf16[16,8,16,128]{3,2,1,0:T(8,128)(2,1)S(1)}, u32[]{:S(2)}) copy-start(bf16[16,8,16,128]{3,2,1,0:T(8,128)(2,1)S(1)} %all-to-all-done.4) | copy-start | bytes 1572868
  192.5 14.4 %collective-permute-start.25 = (bf16[128,16,128]{2,1,0:T(8,128)(2,1)S(1)}, bf16[128,16,128]{2,1,0:T(8,128)(2,1)S(1)}, u32[]{:S(2)}, u32[]{:S(2)}) collective-permute-start(bf16[128,16,128]{2,1,0:T(8,128)(2,1)S(1)} %bitcast.61), channel_id=1, source_target_pairs={{0,1},{1,2},{2,3},{3,0},{4,5},{5,6},{6,7},{7,4},{8,9},{9,10},{10,1... | collective-permute-start | bytes 1572872 | tf_op jit(solution)/shard_map/ppermute | solution.py:29
  194.3 25.1 %collective-permute-start.26 = (bf16[128,16,128]{2,1,0:T(8,128)(2,1)S(1)}, bf16[128,16,128]{2,1,0:T(8,128)(2,1)S(1)}, u32[]{:S(2)}, u32[]{:S(2)}) collective-permute-start(bf16[128,16,128]{2,1,0:T(8,128)(2,1)S(1)} %bitcast.62), channel_id=1, source_target_pairs={{0,2},{1,3},{2,0},{3,1},{4,6},{5,7},{6,4},{7,5},{8,10},{9,11},{10,... | collective-permute-start | bytes 1572872 | tf_op jit(solution)/shard_map/ppermute | solution.py:29
  199.6 19.8 %collective-permute-start.27 = (bf16[128,16,128]{2,1,0:T(8,128)(2,1)S(1)}, bf16[128,16,128]{2,1,0:T(8,128)(2,1)S(1)}, u32[]{:S(2)}, u32[]{:S(2)}) collective-permute-start(bf16[128,16,128]{2,1,0:T(8,128)(2,1)S(1)} %bitcast.63), channel_id=1, source_target_pairs={{0,3},{1,0},{2,1},{3,2},{4,7},{5,4},{6,5},{7,6},{8,11},{9,8},{10,9... | collective-permute-start | bytes 1572872 | tf_op jit(solution)/shard_map/ppermute | solution.py:29
  206.9 12.5 %copy-start.3 = (bf16[128,16,128]{2,1,0:T(8,128)(2,1)}, bf16[128,16,128]{2,1,0:T(8,128)(2,1)S(1)}, u32[]{:S(2)}) copy-start(bf16[128,16,128]{2,1,0:T(8,128)(2,1)S(1)} %collective-permute-done.25.table1) | copy-start | bytes 1572868
  219.4 0.8 copy-start.4
  219.4 1.0 copy-start.5
where the time goes:
time: 228 us; the launch traced here: 225 us
  starting transfers between devices  97.5 us (43%)
  waiting for transfers between devices  52.9 us (23%)
  Pallas kernels  27.8 us (12%)
  blocking collectives  21.3 us (9%)
  local copies, waits for them, and re-layouts  19.2 us (8%)
  other arithmetic  4.29 us (2%)
    ppermute x28, starting transfers between devices, permute(): return lax.ppermute(value, axes, pairs)  63.4 us
    ppermute x28, waiting for transfers between devices, permute(): return lax.ppermute(value, axes, pairs)  43 us
    all_to_all x2, starting transfers between devices, body(): packed = lax.all_to_all(packed, ('zh', 'co', 'zl', 'x'), 0, 0, tiled=True)  22 us
    all_to_all x1, blocking collectives, body(): lax.all_to_all(table.reshape(16, 8, 16, 128), ('zl', 'x'), 0, 0, tiled=True)  21.3 us
    all_to_all x1, waiting for transfers between devices, body(): got = lax.all_to_all(by_frame, ('zh', 'zl'), 0, 0, tiled=True)  9.89 us
    pallas_call x1, Pallas kernels, body(): pl.pallas_call(attend_kernel, out_shape=(jax.ShapeDtypeStruct((384, 256),...  9.12 us
    all_to_all x1, starting transfers between devices, body(): got = lax.all_to_all(by_frame, ('zh', 'zl'), 0, 0, tiled=True)  7.69 us
    pallas_call x1, Pallas kernels, body(): pl.pallas_call(conv_kernel, out_shape=jax.ShapeDtypeStruct((4, 96, 1024),...  5.4 us
  transfers between devices with their start and end apart: 32, of which 11 were waited for; matrix products, arithmetic and copies ran while one was open for 7% of the time, Pallas kernels for 8%

commit v1 on v0

--- a/solution.py
+++ b/solution.py
@@ -63,8 +63,10 @@
     first = jnp.zeros((96, 128), F32)
     second = jnp.zeros((96, 128), F32)
     for f in range(4):
-        data = frames[:, f * 256 : f * 256 + 256].astype(F32)
-        data = jnp.where(f < valid[0], data, 0.0)
+        data = frames[:, f * 256 : f * 256 + 256]
+        out[2 * f, :96] = data
+        out[2 * f + 1, :96] = data
+        data = jnp.where(f < valid[0], data.astype(F32), 0.0)
         square = data * data
         first += data[:, :128] + data[:, 128:]
         second += square[:, :128] + square[:, 128:]
@@ -72,24 +74,23 @@
     lane = lax.broadcasted_iota(jnp.int32, (96, 128), 1)
     first = jnp.sum(first, axis=1, keepdims=True)
     second = jnp.sum(second, axis=1, keepdims=True)
-    sums = jnp.where(row == lane, first, jnp.where(row + 8 == lane, second, 0.0))
+    sums = jnp.where(row + 96 == lane, first, jnp.where(row + 104 == lane, second, 0.0))
     sums = jnp.sum(sums, axis=0, keepdims=True)
-    pad = jnp.zeros((1, 32), F32)
-    rows = jnp.concatenate(
-        [
-            sums,
-            jnp.concatenate([gain[...], pad], axis=1),
-            jnp.concatenate([shift[...], pad], axis=1),
-            jnp.zeros((1, 128), F32),
-        ],
-        axis=0,
-    )
-    out[...] = jnp.broadcast_to(rows[None], out.shape)
+    left = jnp.concatenate([gain[...], jnp.zeros((1, 32), F32)], axis=1) + sums
+    right = jnp.concatenate([shift[...], jnp.zeros((1, 32), F32)], axis=1)
+    rest = jnp.concatenate([left, right], axis=1)
+    rows = []
+    for _ in range(3):
+        rounded = rest.astype(BF).astype(F32)
+        rows.append(rounded)
+        rest = rest - rounded
+    rows = jnp.concatenate(rows + [jnp.zeros((13, 256), F32)], axis=0).astype(BF)
+    for z in range(8):
+        out[z, 96:] = rows
 
 
 def attend_kernel(
     at,
-    packed,
     own0,
     own1,
     own2,
@@ -113,19 +114,28 @@
     entry = lax.broadcasted_iota(jnp.int32, (96, 128), 0)
     for which, parts in ((co, (own0, own1, own2, own3)), (1 - co, (other0, other1, other2, other3))):
         for zh in range(2):
-            c = 2 * zh + which
-            table = jnp.sum(packed[c], axis=0)
-            mean = column(table[0:1], group) / count
-            var = column(table[0:1], group + 8) / count - mean * mean
+            tables = []
+            for s in range(4):
+                for zl in range(4):
+                    rows = parts[s][zh * 4 + zl, 96:].astype(F32)
+                    tables.append(rows[0:1] + rows[1:2] + rows[2:3])
+            table = tables[0]
+            for other in tables[1:]:
+                table = table + other
+            left, right = tables[0][:, :128], tables[0][:, 128:]
+            mean = column(table[:, :128], group + 96) / count
+            var = column(table[:, :128], group + 104) / count - mean * mean
             scale = lax.rsqrt(var + EPS)
-            gain = column(packed[c, 0, 1:2], entry)
-            shift = column(packed[c, 0, 2:3], entry)
-            rows = pl.ds(pl.multiple_of(c * 96, 32), 96)
+            gain = column(left, entry)
+            shift = column(right, entry)
+            rows = pl.ds(pl.multiple_of((2 * zh + which) * 96, 32), 96)
             for s in range(4):
-                data = parts[s][zh * 96 : zh * 96 + 96, :].astype(F32)
-                data = (data - mean) * scale * gain + shift
-                tokens[rows, s * 1024 : s * 1024 + 1024] = data.astype(BF)
-    lanes = pl.ds(pl.multiple_of(slot, 256), 256)
+                for zl in range(4):
+                    data = parts[s][zh * 4 + zl, :96].astype(F32)
+                    data = (data - mean) * scale * gain + shift
+                    to = s * 1024 + zl * 256
+                    tokens[rows, to : to + 256] = data.astype(BF)
+    lanes = pl.ds(pl.multiple_of(slot * 256, 256), 256)
     queries = lax.dot_general(
         tokens[:, lanes], qkv[:, :384], (((0,), (0,)), ((), ())), preferred_element_type=F32
     )
@@ -165,7 +175,7 @@
     for which, part in ((co, own0), (1 - co, other0)):
         for zh in range(2):
             rows = pl.ds(pl.multiple_of((2 * zh + which) * 96, 32), 96)
-            raw = part[zh * 96 : zh * 96 + 96, lanes].astype(F32)
+            raw = part[zh * 4 + slot, :96].astype(F32)
             hidden[rows, :] = (raw + hidden[rows, :].astype(F32)).astype(BF)
     data = jnp.where(frame < valid, hidden[...].astype(F32), 0.0)
     first = jnp.sum(data, axis=1, keepdims=True)
@@ -203,15 +213,40 @@
     return jnp.where(lane == 127, 0.0, pltpu.roll(g, 127, 1))
 
 
-def grad_kernel(at, clip0, clip1, clip2, clip3, cot, before, after, out, gs, cs):
+def grad_kernel(
+    at,
+    clip0,
+    clip1,
+    clip2,
+    clip3,
+    near,
+    near_before,
+    near_after,
+    far,
+    far_before,
+    far_after,
+    out,
+    gs,
+    cs,
+    cot,
+    before,
+    after,
+):
+    for to, first, second in (
+        (cot, near, far),
+        (before, near_before, far_before),
+        (after, near_after, far_after),
+    ):
+        to[0:2] = first[...]
+        to[2:4] = second[...]
     gs[864:, :] = jnp.zeros((32, 4096), BF)
-    for s, clip in enumerate((clip0, clip1, clip2, clip3)):
+    for s, gated in enumerate((clip0, clip1, clip2, clip3)):
         for kt in range(2):
             gs[kt * 288 : kt * 288 + 288, s * 1024 : s * 1024 + (2 - kt) * 256] = jnp.zeros(
                 (288, (2 - kt) * 256), BF
             )
         for b in range(8):
-            g = clip[:, b * 128 : b * 128 + 128].astype(F32)
+            g = gated[:, b * 128 : b * 128 + 128].astype(F32)
             for kx in range(3):
                 piece = shifted(g, kx).astype(BF)
                 for kt in range(3):
@@ -219,7 +254,8 @@
                     if to < 1024:
                         row = (kt * 3 + kx) * 96
                         gs[row : row + 96, s * 1024 + to : s * 1024 + to + 128] = piece
-        k = lax.rem(s + at[0], 4)
+        clip = lax.rem(at[0] - s + 4, 4)
+        k = jnp.where(lax.rem(clip, 2) == at[1], 0, 2) + (clip // 2 ^ at[2])
         cs[96:192, s * 1024 : s * 1024 + 1024] = cot[k]
         for f in range(4):
             to = s * 1024 + f * 256
@@ -302,36 +338,31 @@
     params = pltpu.CompilerParams(vmem_limit_bytes=VMEM)
     scalars = pl.BlockSpec(memory_space=pltpu.SMEM)
     whole = pl.BlockSpec(memory_space=pltpu.VMEM)
-    frames = features.reshape(96, 4, 256)
     valid = frame_count[0]
     mask = (lax.iota(jnp.int32, 4) < valid).astype(F32)
 
-    by_frame = jnp.repeat(frames.transpose(1, 0, 2), 2, axis=0)
-    got = lax.all_to_all(by_frame, ("zh", "zl"), 0, 0, tiled=True)
-    mine = got.reshape(2, 4, 96, 256).transpose(0, 2, 1, 3).reshape(192, 1024)
-    parts = ring(mine, "x")
-    others = [permute(p, ("co",), lambda i: (1 - i,)) for p in parts]
-
-    packed = pl.pallas_call(
+    by_frame = pl.pallas_call(
         pack_kernel,
-        out_shape=jax.ShapeDtypeStruct((64, 4, 128), F32),
+        out_shape=jax.ShapeDtypeStruct((8, 112, 256), BF),
         in_specs=[scalars, whole, whole, whole],
         out_specs=whole,
         compiler_params=params,
         cost_estimate=cost(10**6, 200000),
         name="pack",
-    )(frame_count, frames.reshape(96, 1024), norm1_gain[None], norm1_shift[None])
-    packed = lax.all_to_all(packed, ("zh", "co", "zl", "x"), 0, 0, tiled=True)
+    )(frame_count, features.reshape(96, 1024), norm1_gain[None], norm1_shift[None])
+    mine = lax.all_to_all(by_frame, ("zh", "zl"), 0, 0, tiled=True)
+    parts = ring(mine, "x")
+    others = [permute(p, ("co",), lambda i: (1 - i,)) for p in parts]
 
     frame = 2 * zh + zl // 2
-    at = jnp.stack([co, (2 * (zl % 2) + co) * 256, valid, frame]).astype(jnp.int32)
+    at = jnp.stack([co, 2 * (zl % 2) + co, valid, frame]).astype(jnp.int32)
     hidden_q, packed = pl.pallas_call(
         attend_kernel,
         out_shape=(
             jax.ShapeDtypeStruct((384, 256), BF),
             jax.ShapeDtypeStruct((64, 1, 128), F32),
         ),
-        in_specs=[scalars] + [whole] * 13,
+        in_specs=[scalars] + [whole] * 12,
         out_specs=(whole, whole),
         scratch_shapes=[pltpu.VMEM((384, 4096), BF), pltpu.VMEM((256, 4096), F32)],
         compiler_params=params,
@@ -339,7 +370,6 @@
         name="attention",
     )(
         at,
-        packed.reshape(4, 16, 4, 128),
         *parts,
         *others,
         qkv_weight,
@@ -358,7 +388,27 @@
 
         pieces.append(permute(piece, ("zh", "co", "zl"), to_channels))
 
+    masked = (cotangent.reshape(96, 4, 256) * mask.astype(BF)[None, :, None]).reshape(96, 1024)
+    masked, _ = lax.optimization_barrier((masked, parts[1]))
+    blocks = jnp.stack(
+        [
+            permute(
+                masked,
+                ("zh", "co", "y"),
+                lambda zh, co, y: ((y // 2 + k) % 2, y % 2, 2 * zh + co),
+            )
+            for k in range(2)
+        ]
+    )
+    lines = blocks.reshape(2, 96, 4, 2, 128)
+    before, after = halo(
+        lines[:, :, :, 1].reshape(2, 96, 512), lines[:, :, :, 0].reshape(2, 96, 512)
+    )
+    near = (blocks, before, after)
+    far = [permute(v, ("co",), lambda i: (1 - i,)) for v in near]
+
     packed = lax.all_to_all(packed, ("zh", "co", "zl", "x"), 0, 0, tiled=True)
+    packed, near, far = lax.optimization_barrier((packed, near, far))
     gated, hidden = pl.pallas_call(
         gate_kernel,
         out_shape=(jax.ShapeDtypeStruct((96, 1024), BF), jax.ShapeDtypeStruct((96, 1024), BF)),
@@ -376,35 +426,38 @@
         norm2_shift[:, None],
     )
 
-    masked = (cotangent.reshape(96, 4, 256) * mask.astype(BF)[None, :, None]).reshape(96, 1024)
-    masked, _ = lax.optimization_barrier((masked, mine))
-    blocks = jnp.stack(
-        [
-            permute(
-                masked,
-                ("zh", "co", "y"),
-                lambda zh, co, y: (((y + k) % 4) // 2, (y + k) % 2, 2 * zh + co),
-            )
-            for k in range(4)
-        ]
-    )
-    lines = blocks.reshape(4, 96, 4, 2, 128)
-    before, after = halo(
-        lines[:, :, :, 1].reshape(4, 96, 512), lines[:, :, :, 0].reshape(4, 96, 512)
-    )
-
+    rows = gated.reshape(96, 4, 2, 128)
+    above, below = halo(rows[:, :, 1].reshape(96, 512), rows[:, :, 0].reshape(96, 512))
     clips = ring(gated, "y")
+    kernels = conv_weight.transpose(0, 4, 1, 2, 3).reshape(3, 384, 864)
+    clips, above, below, kernels = lax.optimization_barrier((clips, above, below, kernels))
     table = pl.pallas_call(
         grad_kernel,
         out_shape=jax.ShapeDtypeStruct((128, 16, 128), BF),
-        in_specs=[scalars] + [whole] * 7,
+        in_specs=[scalars] + [whole] * 10,
         out_specs=whole,
-        scratch_shapes=[pltpu.VMEM((896, 4096), BF), pltpu.VMEM((288, 4096), BF)],
+        scratch_shapes=[
+            pltpu.VMEM((896, 4096), BF),
+            pltpu.VMEM((288, 4096), BF),
+            pltpu.VMEM((4, 96, 1024), BF),
+            pltpu.VMEM((4, 96, 512), BF),
+            pltpu.VMEM((4, 96, 512), BF),
+        ],
         compiler_params=params,
         cost_estimate=cost(4 * 10**9, 20 * 10**6),
         name="weight_grad",
-    )((ch - y + 4).astype(jnp.int32)[None], *clips, blocks, before, after)
+    )(jnp.stack([y, co, zh]).astype(jnp.int32), *clips, *near, *far)
+    table, above, below = lax.optimization_barrier((table, above, below))
     shares = lax.all_to_all(table.reshape(16, 8, 16, 128), ("zl", "x"), 0, 0, tiled=True)
+    partial = pl.pallas_call(
+        conv_kernel,
+        out_shape=jax.ShapeDtypeStruct((4, 96, 1024), BF),
+        scratch_shapes=[pltpu.VMEM((864, 1536), BF)],
+        compiler_params=params,
+        cost_estimate=cost(3 * 10**9, 12 * 10**6),
+        name="convolution",
+    )(clips[0], above, below, kernels)
+    shares, partial = lax.optimization_barrier((shares, partial))
     share = jnp.sum(shares.astype(F32), axis=0).astype(BF)
     table = spread(share, ("zl", "x"), 16).reshape(128, 16, 128)
     weight_grad = pl.pallas_call(
@@ -419,17 +472,6 @@
     )(y.astype(jnp.int32)[None], *ring(table, "y"))
     weight_grad = weight_grad.reshape(3, 3, 3, 96, 384)
 
-    rows = gated.reshape(96, 4, 2, 128)
-    before, after = halo(rows[:, :, 1].reshape(96, 512), rows[:, :, 0].reshape(96, 512))
-    kernels = conv_weight.transpose(0, 4, 1, 2, 3).reshape(3, 384, 864)
-    partial = pl.pallas_call(
-        conv_kernel,
-        out_shape=jax.ShapeDtypeStruct((4, 96, 1024), BF),
-        scratch_shapes=[pltpu.VMEM((864, 1536), BF)],
-        compiler_params=params,
-        cost_estimate=cost(3 * 10**9, 12 * 10**6),
-        name="convolution",
-    )(gated, before, after, kernels)
     conv = lax.dynamic_index_in_dim(partial, ch, 0, keepdims=False).astype(F32)
     for k in range(1, 4):
         piece = lax.dynamic_index_in_dim(partial, ch ^ k, 0, keepdims=False)

time: 228 us -> 222 us (0.974)
  waiting for transfers between devices: 52.9 us -> 60.5 us
  starting transfers between devices: 97.5 us -> 91.6 us
  local copies, waits for them, and re-layouts: 19.2 us -> 15 us
    all_to_all x1, waiting for transfers between devices: 0.01 us -> 22.6 us  [spread(): return lax.all_to_all(copies, axes, 0, 0, tiled=True)]
    ppermute x28 -> x29, waiting for transfers between devices: 43 us -> 31.7 us  [permute(): return lax.ppermute(value, axes, pairs)]
    all_to_all x2 -> x1, starting transfers between devices: 22 us -> 14.2 us  [body(): packed = lax.all_to_all(packed, ('zh', 'co', 'zl', 'x'), 0, 0, tiled=True)]
    all_to_all x1, waiting for transfers between devices: 9.89 us -> 6.27 us  [body(): lax.all_to_all(table.reshape(16, 8, 16, 128), ('zl', 'x'), 0, 0, tiled=True)]
    ppermute x28 -> x29, starting transfers between devices: 63.4 us -> 66.9 us  [permute(): return lax.ppermute(value, axes, pairs)]
    optimization_barrier x0 -> x1, local copies, waits for them, and re-layouts: none -> 2.4 us  [body(): lax.optimization_barrier((clips, above, below, kernels))]
    unnamed x66 -> x71, local copies, waits for them, and re-layouts: 5.23 us -> 3 us
  transfers between devices with their start and end apart: 32 -> 32, of which waited for: 11 -> 10; matrix products, arithmetic and copies ran while one was open for 7% -> 6% of each run, Pallas kernels for 8% -> 7%
where the time goes in v1:
time: 222 us; the launch traced here: 221 us
  starting transfers between devices  91.6 us (41%)
  waiting for transfers between devices  60.5 us (27%)
  Pallas kernels  28.2 us (13%)
  blocking collectives  19.4 us (9%)
  local copies, waits for them, and re-layouts  15 us (7%)
  other arithmetic  4.23 us (2%)
    ppermute x29, starting transfers between devices, permute(): return lax.ppermute(value, axes, pairs)  66.9 us
    ppermute x29, waiting for transfers between devices, permute(): return lax.ppermute(value, axes, pairs)  31.7 us
    all_to_all x1, waiting for transfers between devices, spread(): return lax.all_to_all(copies, axes, 0, 0, tiled=True)  22.6 us
    all_to_all x1, blocking collectives, body(): mine = lax.all_to_all(by_frame, ('zh', 'zl'), 0, 0, tiled=True)  19.4 us
    all_to_all x1, starting transfers between devices, body(): packed = lax.all_to_all(packed, ('zh', 'co', 'zl', 'x'), 0, 0, tiled=True)  14.2 us
    pallas_call x1, Pallas kernels, body(): pl.pallas_call(attend_kernel, out_shape=(jax.ShapeDtypeStruct((384, 256),...  9.13 us
    all_to_all x1, waiting for transfers between devices, body(): lax.all_to_all(table.reshape(16, 8, 16, 128), ('zl', 'x'), 0, 0, tiled=True)  6.27 us
    all_to_all x1, starting transfers between devices, body(): lax.all_to_all(table.reshape(16, 8, 16, 128), ('zl', 'x'), 0, 0, tiled=True)  6.07 us
  transfers between devices with their start and end apart: 32, of which 10 were waited for; matrix products, arithmetic and copies ran while one was open for 6% of the time, Pallas kernels for 7%

profile of v1, /device:TPU:65, one launch (start us, length us, event | category | flops | bytes accessed | tf_op | source)
XLA Modules:
  0.0 220.8 jit_solution(7744152471536479266)
XLA Ops:
  1.3 1.7 reshape.62.frames
  3.1 1.9 pack.1
  4.9 19.4 %all_to_all.20.own0 = bf16[8,112,256]{2,1,0:T(8,128)(2,1)S(1)} all-to-all(bf16[8,112,256]{2,1,0:T(8,128)(2,1)} %pack.1), channel_id=1, replica_groups=mesh['zh'=2,'co'=2,'zl'=4,'x'=4,'y'=4] {'zh','zl'}, dimensions={0} | all-to-all | bytes 917504 | tf_op jit(solution)/shard_map/all_to_all | solution.py:353
  24.4 1.2 collective-permute-start
  25.6 1.5 collective-permute-start.2
  27.0 1.5 collective-permute-start.1
  28.8 6.3 %collective-permute-done.own1 = bf16[8,112,256]{2,1,0:T(8,128)(2,1)S(1)} collective-permute-done((bf16[8,112,256]{2,1,0:T(8,128)(2,1)S(1)}, bf16[8,112,256]{2,1,0:T(8,128)(2,1)S(1)}, u32[]{:S(2)}, u32[]{:S(2)}) %collective-permute-start) | collective-permute-done | bytes 458784 | tf_op jit(solution)/shard_map/ppermute | solution.py:29
  35.1 8.4 %collective-permute-start.7 = (bf16[96,1024]{1,0:T(8,128)(2,1)S(1)}, bf16[96,1024]{1,0:T(8,128)(2,1)S(1)}, u32[]{:S(2)}, u32[]{:S(2)}) collective-permute-start(bf16[96,1024]{1,0:T(8,128)(2,1)S(1)} %broadcast_multiply_fusion), channel_id=1, source_target_pairs={{0,0},{1,64},{2,128},{3,192},{64,1},{65,65},{66,129},{67,193},{128... | collective-permute-start | bytes 589832 | tf_op jit(solution)/shard_map/ppermute | solution.py:29
  43.6 0.6 broadcast_in_dim.30.qkv_bias
  44.2 0.8 broadcast_in_dim.35.out_bias
  45.0 2.2 collective-permute-start.8
  47.2 5.2 %collective-permute-start.4 = (bf16[8,112,256]{2,1,0:T(8,128)(2,1)S(1)}, bf16[8,112,256]{2,1,0:T(8,128)(2,1)}, u32[]{:S(2)}, u32[]{:S(2)}) collective-permute-start(bf16[8,112,256]{2,1,0:T(8,128)(2,1)S(1)} %collective-permute-done.own1), channel_id=1, source_target_pairs={{0,64},{64,0},{1,65},{65,1},{2,66},{66,2},{3,67},{67,3},{4,68},{68... | collective-permute-start | bytes 1376264 | tf_op jit(solution)/shard_map/ppermute | solution.py:29
  52.5 0.4 collective-permute-start.5
  53.1 0.3 collective-permute-done.8
  54.0 2.9 %collective-permute-start.9 = (bf16[2,96,512]{2,1,0:T(8,128)(2,1)S(1)}, bf16[2,96,512]{2,1,0:T(8,128)(2,1)S(1)}, u32[]{:S(2)}, u32[]{:S(2)}) collective-permute-start(bf16[2,96,512]{2,1,0:T(8,128)(2,1)S(1)} %reshape_squeeze.12), channel_id=1, source_target_pairs={{0,4},{4,8},{8,12},{12,16},{16,20},{20,24},{24,28},{28,32},{32,36}... | collective-permute-start | bytes 589832 | tf_op jit(solution)/shard_map/ppermute | solution.py:29
  56.9 4.8 %collective-permute-start.10 = (bf16[2,96,512]{2,1,0:T(8,128)(2,1)S(1)}, bf16[2,96,512]{2,1,0:T(8,128)(2,1)S(1)}, u32[]{:S(2)}, u32[]{:S(2)}) collective-permute-start(bf16[2,96,512]{2,1,0:T(8,128)(2,1)S(1)} %reshape_squeeze.13), channel_id=1, source_target_pairs={{4,0},{8,4},{12,8},{16,12},{20,16},{24,20},{28,24},{32,28},{36,32}... | collective-permute-start | bytes 589832 | tf_op jit(solution)/shard_map/ppermute | solution.py:29
  61.6 0.7 pad_add_fusion.1.at
  62.4 0.7 collective-permute-done.9.near_before
  63.2 6.3 %collective-permute-start.11 = (bf16[2,96,1024]{2,1,0:T(8,128)(2,1)S(1)}, bf16[2,96,1024]{2,1,0:T(8,128)(2,1)S(1)}, u32[]{:S(2)}, u32[]{:S(2)}) collective-permute-start(bf16[2,96,1024]{2,1,0:T(8,128)(2,1)S(1)} %pad_maximum_fusion.near), channel_id=1, source_target_pairs={{0,64},{64,0},{1,65},{65,1},{2,66},{66,2},{3,67},{67,3},{4,68},{68... | collective-permute-start | bytes 1179656 | tf_op jit(solution)/shard_map/ppermute | solution.py:29
  69.4 1.5 collective-permute-start.12
  70.9 0.3 collective-permute-start.13
  71.2 9.1 %attention.1 = (bf16[384,256]{1,0:T(8,128)(2,1)}, f32[64,1,128]{2,1,0:T(1,128)}) custom-call(s32[4]{0:T(128)} %pad_add_fusion.1.at, bf16[8,112,256]{2,1,0:T(8,128)(2,1)} %copy-done.6, bf16[8,112,256]{2,1,0:T(8,128)(2,1)} %copy-done.20, bf16[8,112,256]{2,1,0:T(8,128)(2,1)} %collective-permute-done.1.own2, bf16[8,112,256]{2,1,0:T(8,128)(2,1)} %copy-done.21, ...), custom_call_target="tpu_custom_call" | custom-call | flops 4000000000 | bytes 20000000 | tf_op jit(solution)/shard_map/attention/pallas_call | solution.py:359
  80.3 14.2 %all-to-all-start.1 = ((f32[64,1,128]{2,1,0:T(1,128)}), f32[64,1,128]{2,1,0:T(1,128)S(1)}, u32[]{:S(2)}, u32[]{:S(2)}) async-start(f32[64,1,128]{2,1,0:T(1,128)} %get-tuple-element.26), calls=%async_computation.1 | async-start | bytes 65536 | tf_op jit(solution)/shard_map/all_to_all | solution.py:410
  94.5 0.9 constant_dynamic-slice_fusion
  95.4 3.7 %collective-permute-start.17 = (bf16[96,256]{1,0:T(8,128)(2,1)S(1)}, bf16[96,256]{1,0:T(8,128)(2,1)S(1)}, u32[]{:S(2)}, u32[]{:S(2)}) collective-permute-start(bf16[96,256]{1,0:T(8,128)(2,1)S(1)} %get-tuple-element.57), channel_id=1, source_target_pairs={{0,192},{16,224},{32,128},{48,160},{64,208},{80,240},{96,144},{112... | collective-permute-start | bytes 147464 | tf_op jit(solution)/shard_map/ppermute | solution.py:29
  99.2 0.9 collective-permute-start.16
  100.1 5.3 %collective-permute-start.14 = (bf16[96,256]{1,0:T(8,128)(2,1)S(1)}, bf16[96,256]{1,0:T(8,128)(2,1)S(1)}, u32[]{:S(2)}, u32[]{:S(2)}) collective-permute-start(bf16[96,256]{1,0:T(8,128)(2,1)S(1)} %get-tuple-element.60), channel_id=1, source_target_pairs={{0,0},{16,32},{32,64},{48,96},{64,16},{80,48},{96,80},{112,112},{1... | collective-permute-start | bytes 147464 | tf_op jit(solution)/shard_map/ppermute | solution.py:29
  105.4 0.6 pad_add_fusion.at
  106.1 0.7 copy.26.gain
  106.8 0.7 copy.27.shift
  107.6 0.5 copy-done.10
  108.3 0.6 copy-done.14
  108.9 1.9 gate.1
  110.8 1.0 reshape.64
  112.1 1.4 collective-permute-start.18
  113.4 1.1 slice_reduce_fusion
  114.6 3.1 %collective-permute-start.21 = (bf16[96,512]{1,0:T(8,128)(2,1)S(1)}, bf16[96,512]{1,0:T(8,128)(2,1)S(1)}, u32[]{:S(2)}, u32[]{:S(2)}) collective-permute-start(bf16[96,512]{1,0:T(8,128)(2,1)S(1)} %bitcast.61), channel_id=1, source_target_pairs={{0,4},{4,8},{8,12},{12,16},{16,20},{20,24},{24,28},{28,32},{32,36}... | collective-permute-start | bytes 294920 | tf_op jit(solution)/shard_map/ppermute | solution.py:29
  117.7 4.3 %collective-permute-start.22 = (bf16[96,512]{1,0:T(8,128)(2,1)S(1)}, bf16[96,512]{1,0:T(8,128)(2,1)S(1)}, u32[]{:S(2)}, u32[]{:S(2)}) collective-permute-start(bf16[96,512]{1,0:T(8,128)(2,1)S(1)} %bitcast.60), channel_id=1, source_target_pairs={{4,0},{8,4},{12,8},{16,12},{20,16},{24,20},{28,24},{32,28},{36,32}... | collective-permute-start | bytes 294920 | tf_op jit(solution)/shard_map/ppermute | solution.py:29
  122.0 0.6 pad_add_fusion.2.at
  122.6 1.0 collective-permute-done.22.after
  123.6 1.2 collective-permute-done.18.clip1
  124.9 0.6 copy-done.30
  125.5 5.5 %weight_grad.1 = bf16[128,16,128]{2,1,0:T(8,128)(2,1)} custom-call(s32[3]{0:T(128)} %pad_add_fusion.2.at, bf16[96,1024]{1,0:T(8,128)(2,1)} %get-tuple-element.32.clip0.clip, bf16[96,1024]{1,0:T(8,128)(2,1)} %copy-done.30, bf16[96,1024]{1,0:T(8,128)(2,1)} %copy-done.29, bf16[96,1024]{1,0:T(8,128)(2,1)} %copy-done.28, bf16[2,96,1024]{2,1,0:T(8,128)(2,1)} %copy-done.7, ...), custom_call_target="tpu_custom_call" | custom-call | flops 4000000000 | bytes 20000000 | tf_op jit(solution)/shard_map/weight_grad/pallas_call | solution.py:434
  131.0 6.1 %all-to-all-start.2 = ((bf16[16,8,16,128]{3,2,1,0:T(8,128)(2,1)}), bf16[16,8,16,128]{3,2,1,0:T(8,128)(2,1)S(1)}, u32[]{:S(2)}, u32[]{:S(2)}) async-start(bf16[16,8,16,128]{3,2,1,0:T(8,128)(2,1)} %bitcast.57), calls=%async_computation.2 | async-start | bytes 1048576 | tf_op jit(solution)/shard_map/all_to_all | solution.py:451
  137.1 2.4 %copy.30.weight = bf16[3,384,864]{2,1,0:T(8,128)(2,1)} copy(bf16[3,384,864]{1,2,0:T(8,128)(2,1)S(1)} %bitcast.54) | data formatting | bytes 3981312 | tf_op jit(solution)/shard_map/optimization_barrier | solution.py:433
  139.5 5.4 %convolution.1 = bf16[4,96,1024]{2,1,0:T(8,128)(2,1)} custom-call(bf16[96,1024]{1,0:T(8,128)(2,1)} %get-tuple-element.32.clip0.clip, bf16[96,512]{1,0:T(8,128)(2,1)} %copy-done.31, bf16[96,512]{1,0:T(8,128)(2,1)} %copy-done.32, bf16[3,384,864]{2,1,0:T(8,128)(2,1)} %copy.30.weight), custom_call_target="tpu_custom_call" | custom-call | flops 3000000000 | bytes 12000000 | tf_op jit(solution)/shard_map/convolution/pallas_call | solution.py:452
  144.9 6.3 %all-to-all-done.2 = bf16[16,8,16,128]{3,2,1,0:T(8,128)(2,1)S(1)} async-done(((bf16[16,8,16,128]{3,2,1,0:T(8,128)(2,1)}), bf16[16,8,16,128]{3,2,1,0:T(8,128)(2,1)S(1)}, u32[]{:S(2)}, u32[]{:S(2)}) %all-to-all-start.2) | async-done | bytes 524320 | tf_op jit(solution)/shard_map/all_to_all | solution.py:451
  151.2 0.9 broadcast_in_dim.34
  152.1 4.5 %all-to-all-start.3 = ((bf16[16,8,16,128]{3,2,1,0:T(8,128)(2,1)}), bf16[16,8,16,128]{3,2,1,0:T(8,128)(2,1)S(1)}, u32[]{:S(2)}, u32[]{:S(2)}) async-start(bf16[16,8,16,128]{3,2,1,0:T(8,128)(2,1)} %broadcast_in_dim.34), calls=%async_computation.3 | async-start | bytes 1048576 | tf_op jit(solution)/shard_map/all_to_all | solution.py:50
  156.7 2.7 %collective-permute-start.23 = (bf16[96,1024]{1,0:T(8,128)(2,1)S(1)}, bf16[96,1024]{1,0:T(8,128)(2,1)}, u32[]{:S(2)}, u32[]{:S(2)}) collective-permute-start(bf16[96,1024]{1,0:T(8,128)(2,1)S(1)} %get-tuple-element.52), channel_id=1, source_target_pairs={{0,64},{64,0},{128,192},{192,128},{1,65},{65,1},{129,193},{193,129... | collective-permute-start | bytes 589832 | tf_op jit(solution)/shard_map/ppermute | solution.py:29
  159.4 3.0 %collective-permute-start.25 = (bf16[96,1024]{1,0:T(8,128)(2,1)S(1)}, bf16[96,1024]{1,0:T(8,128)(2,1)}, u32[]{:S(2)}, u32[]{:S(2)}) collective-permute-start(bf16[96,1024]{1,0:T(8,128)(2,1)S(1)} %get-tuple-element.53), channel_id=1, source_target_pairs={{0,192},{64,128},{128,64},{192,0},{1,193},{65,129},{129,65},{193,1... | collective-permute-start | bytes 589832 | tf_op jit(solution)/shard_map/ppermute | solution.py:29
  162.4 2.3 %collective-permute-start.24 = (bf16[96,1024]{1,0:T(8,128)(2,1)S(1)}, bf16[96,1024]{1,0:T(8,128)(2,1)}, u32[]{:S(2)}, u32[]{:S(2)}) collective-permute-start(bf16[96,1024]{1,0:T(8,128)(2,1)S(1)} %get-tuple-element.54), channel_id=1, source_target_pairs={{0,128},{64,192},{128,0},{192,64},{1,129},{65,193},{129,1},{193,65... | collective-permute-start | bytes 589832 | tf_op jit(solution)/shard_map/ppermute | solution.py:29
  164.7 22.6 %all-to-all-done.3 = bf16[16,8,16,128]{3,2,1,0:T(8,128)(2,1)S(1)} async-done(((bf16[16,8,16,128]{3,2,1,0:T(8,128)(2,1)}), bf16[16,8,16,128]{3,2,1,0:T(8,128)(2,1)S(1)}, u32[]{:S(2)}, u32[]{:S(2)}) %all-to-all-start.3) | async-done | bytes 524320 | tf_op jit(solution)/shard_map/all_to_all | solution.py:50
  187.3 1.7 collective-permute-start.28
  189.0 1.2 collective-permute-start.27
  190.2 0.9 collective-permute-start.26
  191.1 1.3 fusion.3
  192.3 0.3 reshape.67
  192.7 0.9 fusion.4
  193.6 5.3 %collective-permute-done.28.table3 = bf16[128,16,128]{2,1,0:T(8,128)(2,1)S(1)} collective-permute-done((bf16[128,16,128]{2,1,0:T(8,128)(2,1)S(1)}, bf16[128,16,128]{2,1,0:T(8,128)(2,1)S(1)}, u32[]{:S(2)}, u32[]{:S(2)}) %collective-permute-start.28) | collective-permute-done | bytes 524320 | tf_op jit(solution)/shard_map/ppermute | solution.py:29
  198.9 3.0 %collective-permute-done.27.table2 = bf16[128,16,128]{2,1,0:T(8,128)(2,1)S(1)} collective-permute-done((bf16[128,16,128]{2,1,0:T(8,128)(2,1)S(1)}, bf16[128,16,128]{2,1,0:T(8,128)(2,1)S(1)}, u32[]{:S(2)}, u32[]{:S(2)}) %collective-permute-start.27) | collective-permute-done | bytes 524320 | tf_op jit(solution)/shard_map/ppermute | solution.py:29
  201.8 13.8 %collective-permute-done.26.table1 = bf16[128,16,128]{2,1,0:T(8,128)(2,1)S(1)} collective-permute-done((bf16[128,16,128]{2,1,0:T(8,128)(2,1)S(1)}, bf16[128,16,128]{2,1,0:T(8,128)(2,1)S(1)}, u32[]{:S(2)}, u32[]{:S(2)}) %collective-permute-start.26) | collective-permute-done | bytes 524320 | tf_op jit(solution)/shard_map/ppermute | solution.py:29
  215.6 0.8 copy-done.5
  216.4 4.4 %join.1 = f32[2592,384]{1,0:T(8,128)} custom-call(s32[1]{0:T(128)} %bitcast.11.at, bf16[128,16,128]{2,1,0:T(8,128)(2,1)} %bitcast.53, bf16[128,16,128]{2,1,0:T(8,128)(2,1)} %copy-done.5, bf16[128,16,128]{2,1,0:T(8,128)(2,1)} %copy-done.4, bf16[128,16,128]{2,1,0:T(8,128)(2,1)} %copy-done.3), custom_call_target="tpu_custom_call" | custom-call | flops 1000000 | bytes 6000000 | tf_op jit(solution)/shard_map/join/pallas_call | solution.py:463
  (107 shorter events, 1.8 us)
Async XLA Ops:
  0.6 28.0 %copy-start.9 = (bf16[96,1,4,2,128]{4,3,2,1,0:T(2,128)(2,1)S(1)}, bf16[96,1,4,2,128]{4,3,2,1,0:T(2,128)(2,1)}, u32[]{:S(2)}) copy-start(bf16[96,1,4,2,128]{4,3,2,1,0:T(2,128)(2,1)} %param.25) | copy-start | bytes 589828
  0.6 43.0 %copy-start.15 = (f32[1152]{0:T(1024)S(1)}, f32[1152]{0:T(1024)}, u32[]{:S(2)}) copy-start(f32[1152]{0:T(1024)} %param.18) | copy-start | bytes 13828
  0.7 43.6 %copy-start.16 = (f32[384]{0:T(512)S(1)}, f32[384]{0:T(512)}, u32[]{:S(2)}) copy-start(f32[384]{0:T(512)} %param.20) | copy-start | bytes 4612
  24.3 29.6 %copy-start.6 = (bf16[8,112,256]{2,1,0:T(8,128)(2,1)}, bf16[8,112,256]{2,1,0:T(8,128)(2,1)S(1)}, u32[]{:S(2)}) copy-start(bf16[8,112,256]{2,1,0:T(8,128)(2,1)S(1)} %all_to_all.20.own0) | copy-start | bytes 1376260
  24.4 10.8 %collective-permute-start = (bf16[8,112,256]{2,1,0:T(8,128)(2,1)S(1)}, bf16[8,112,256]{2,1,0:T(8,128)(2,1)S(1)}, u32[]{:S(2)}, u32[]{:S(2)}) collective-permute-start(bf16[8,112,256]{2,1,0:T(8,128)(2,1)S(1)} %all_to_all.20.own0), channel_id=1, source_target_pairs={{0,4},{4,8},{8,12},{12,0},{1,5},{5,9},{9,13},{13,1},{2,6},{6,10},{... | collective-permute-start | bytes 1376264 | tf_op jit(solution)/shard_map/ppermute | solution.py:29
  25.6 21.7 %collective-permute-start.2 = (bf16[8,112,256]{2,1,0:T(8,128)(2,1)S(1)}, bf16[8,112,256]{2,1,0:T(8,128)(2,1)S(1)}, u32[]{:S(2)}, u32[]{:S(2)}) collective-permute-start(bf16[8,112,256]{2,1,0:T(8,128)(2,1)S(1)} %all_to_all.20.own0), channel_id=1, source_target_pairs={{0,12},{4,0},{8,4},{12,8},{1,13},{5,1},{9,5},{13,9},{2,14},{6,2},{... | collective-permute-start | bytes 1376264 | tf_op jit(solution)/shard_map/ppermute | solution.py:29
  27.0 25.4 %collective-permute-start.1 = (bf16[8,112,256]{2,1,0:T(8,128)(2,1)S(1)}, bf16[8,112,256]{2,1,0:T(8,128)(2,1)}, u32[]{:S(2)}, u32[]{:S(2)}) collective-permute-start(bf16[8,112,256]{2,1,0:T(8,128)(2,1)S(1)} %all_to_all.20.own0), channel_id=1, source_target_pairs={{0,8},{4,12},{8,0},{12,4},{1,9},{5,13},{9,1},{13,5},{2,10},{6,14},... | collective-permute-start | bytes 1376264 | tf_op jit(solution)/shard_map/ppermute | solution.py:29
  35.1 27.2 %copy-start.20 = (bf16[8,112,256]{2,1,0:T(8,128)(2,1)}, bf16[8,112,256]{2,1,0:T(8,128)(2,1)S(1)}, u32[]{:S(2)}) copy-start(bf16[8,112,256]{2,1,0:T(8,128)(2,1)S(1)} %collective-permute-done.own1) | copy-start | bytes 1376260
  35.1 17.4 %collective-permute-start.7 = (bf16[96,1024]{1,0:T(8,128)(2,1)S(1)}, bf16[96,1024]{1,0:T(8,128)(2,1)S(1)}, u32[]{:S(2)}, u32[]{:S(2)}) collective-permute-start(bf16[96,1024]{1,0:T(8,128)(2,1)S(1)} %broadcast_multiply_fusion), channel_id=1, source_target_pairs={{0,0},{1,64},{2,128},{3,192},{64,1},{65,65},{66,129},{67,193},{128... | collective-permute-start | bytes 589832 | tf_op jit(solution)/shard_map/ppermute | solution.py:29
  45.0 11.9 %collective-permute-start.3 = (bf16[8,112,256]{2,1,0:T(8,128)(2,1)S(1)}, bf16[8,112,256]{2,1,0:T(8,128)(2,1)S(1)}, u32[]{:S(2)}, u32[]{:S(2)}) collective-permute-start(bf16[8,112,256]{2,1,0:T(8,128)(2,1)S(1)} %all_to_all.20.own0), channel_id=1, source_target_pairs={{0,64},{64,0},{1,65},{65,1},{2,66},{66,2},{3,67},{67,3},{4,68},{68... | collective-permute-start | bytes 1376264 | tf_op jit(solution)/shard_map/ppermute | solution.py:29
  45.0 8.4 %collective-permute-start.8 = (bf16[96,1024]{1,0:T(8,128)(2,1)S(1)}, bf16[96,1024]{1,0:T(8,128)(2,1)S(1)}, u32[]{:S(2)}, u32[]{:S(2)}) collective-permute-start(bf16[96,1024]{1,0:T(8,128)(2,1)S(1)} %broadcast_multiply_fusion), channel_id=1, source_target_pairs={{0,128},{1,192},{2,0},{3,64},{64,129},{65,193},{66,1},{67,65},{128... | collective-permute-start | bytes 589832 | tf_op jit(solution)/shard_map/ppermute | solution.py:29
  47.2 24.0 %copy-start.21 = (bf16[8,112,256]{2,1,0:T(8,128)(2,1)}, bf16[8,112,256]{2,1,0:T(8,128)(2,1)S(1)}, u32[]{:S(2)}) copy-start(bf16[8,112,256]{2,1,0:T(8,128)(2,1)S(1)} %collective-permute-done.2.own3) | copy-start | bytes 1376260
  47.2 24.0 %collective-permute-start.4 = (bf16[8,112,256]{2,1,0:T(8,128)(2,1)S(1)}, bf16[8,112,256]{2,1,0:T(8,128)(2,1)}, u32[]{:S(2)}, u32[]{:S(2)}) collective-permute-start(bf16[8,112,256]{2,1,0:T(8,128)(2,1)S(1)} %collective-permute-done.own1), channel_id=1, source_target_pairs={{0,64},{64,0},{1,65},{65,1},{2,66},{66,2},{3,67},{67,3},{4,68},{68... | collective-permute-start | bytes 1376264 | tf_op jit(solution)/shard_map/ppermute | solution.py:29
  52.4 18.5 %collective-permute-start.6 = (bf16[8,112,256]{2,1,0:T(8,128)(2,1)S(1)}, bf16[8,112,256]{2,1,0:T(8,128)(2,1)}, u32[]{:S(2)}, u32[]{:S(2)}) collective-permute-start(bf16[8,112,256]{2,1,0:T(8,128)(2,1)S(1)} %collective-permute-done.2.own3), channel_id=1, source_target_pairs={{0,64},{64,0},{1,65},{65,1},{2,66},{66,2},{3,67},{67,3},{4,68},{68... | collective-permute-start | bytes 1376264 | tf_op jit(solution)/shard_map/ppermute | solution.py:29
  52.5 18.7 %collective-permute-start.5 = (bf16[8,112,256]{2,1,0:T(8,128)(2,1)}, bf16[8,112,256]{2,1,0:T(8,128)(2,1)}, u32[]{:S(2)}, u32[]{:S(2)}) collective-permute-start(bf16[8,112,256]{2,1,0:T(8,128)(2,1)} %collective-permute-done.1.own2), channel_id=1, source_target_pairs={{0,64},{64,0},{1,65},{65,1},{2,66},{66,2},{3,67},{67,3},{4,68},{68... | collective-permute-start | bytes 1376264 | tf_op jit(solution)/shard_map/ppermute | solution.py:29
  54.0 9.2 %collective-permute-start.9 = (bf16[2,96,512]{2,1,0:T(8,128)(2,1)S(1)}, bf16[2,96,512]{2,1,0:T(8,128)(2,1)S(1)}, u32[]{:S(2)}, u32[]{:S(2)}) collective-permute-start(bf16[2,96,512]{2,1,0:T(8,128)(2,1)S(1)} %reshape_squeeze.12), channel_id=1, source_target_pairs={{0,4},{4,8},{8,12},{12,16},{16,20},{20,24},{24,28},{28,32},{32,36}... | collective-permute-start | bytes 589832 | tf_op jit(solution)/shard_map/ppermute | solution.py:29
  56.9 5.4 %copy-start.22 = (bf16[8,112,256]{2,1,0:T(8,128)(2,1)}, bf16[8,112,256]{2,1,0:T(8,128)(2,1)S(1)}, u32[]{:S(2)}) copy-start(bf16[8,112,256]{2,1,0:T(8,128)(2,1)S(1)} %collective-permute-done.3.other0) | copy-start | bytes 1376260
  56.9 12.6 %collective-permute-start.10 = (bf16[2,96,512]{2,1,0:T(8,128)(2,1)S(1)}, bf16[2,96,512]{2,1,0:T(8,128)(2,1)S(1)}, u32[]{:S(2)}, u32[]{:S(2)}) collective-permute-start(bf16[2,96,512]{2,1,0:T(8,128)(2,1)S(1)} %reshape_squeeze.13), channel_id=1, source_target_pairs={{4,0},{8,4},{12,8},{16,12},{20,16},{24,20},{28,24},{32,28},{36,32}... | collective-permute-start | bytes 589832 | tf_op jit(solution)/shard_map/ppermute | solution.py:29
  62.4 18.0 %copy-start.7 = (bf16[2,96,1024]{2,1,0:T(8,128)(2,1)}, bf16[2,96,1024]{2,1,0:T(8,128)(2,1)S(1)}, u32[]{:S(2)}) copy-start(bf16[2,96,1024]{2,1,0:T(8,128)(2,1)S(1)} %pad_maximum_fusion.near) | copy-start | bytes 1179652
  62.4 43.7 %copy-start.17 = (f32[96]{0:T(128)S(1)}, f32[96]{0:T(128)}, u32[]{:S(2)}) copy-start(f32[96]{0:T(128)} %param.21) | copy-start | bytes 1156
  62.4 44.4 %copy-start.18 = (f32[96]{0:T(128)S(1)}, f32[96]{0:T(128)}, u32[]{:S(2)}) copy-start(f32[96]{0:T(128)} %param.22) | copy-start | bytes 1156
  63.2 17.2 %copy-start.24 = (bf16[2,96,512]{2,1,0:T(8,128)(2,1)}, bf16[2,96,512]{2,1,0:T(8,128)(2,1)S(1)}, u32[]{:S(2)}) copy-start(bf16[2,96,512]{2,1,0:T(8,128)(2,1)S(1)} %collective-permute-done.9.near_before) | copy-start | bytes 589828
  63.2 44.4 %collective-permute-start.11 = (bf16[2,96,1024]{2,1,0:T(8,128)(2,1)S(1)}, bf16[2,96,1024]{2,1,0:T(8,128)(2,1)S(1)}, u32[]{:S(2)}, u32[]{:S(2)}) collective-permute-start(bf16[2,96,1024]{2,1,0:T(8,128)(2,1)S(1)} %pad_maximum_fusion.near), channel_id=1, source_target_pairs={{0,64},{64,0},{1,65},{65,1},{2,66},{66,2},{3,67},{67,3},{4,68},{68... | collective-permute-start | bytes 1179656 | tf_op jit(solution)/shard_map/ppermute | solution.py:29
  69.4 10.9 %copy-start.25 = (bf16[2,96,512]{2,1,0:T(8,128)(2,1)}, bf16[2,96,512]{2,1,0:T(8,128)(2,1)S(1)}, u32[]{:S(2)}) copy-start(bf16[2,96,512]{2,1,0:T(8,128)(2,1)S(1)} %collective-permute-done.10.near_after) | copy-start | bytes 589828
  69.4 30.6 %collective-permute-start.12 = (bf16[2,96,512]{2,1,0:T(8,128)(2,1)S(1)}, bf16[2,96,512]{2,1,0:T(8,128)(2,1)S(1)}, u32[]{:S(2)}, u32[]{:S(2)}) collective-permute-start(bf16[2,96,512]{2,1,0:T(8,128)(2,1)S(1)} %collective-permute-done.9.near_before), channel_id=1, source_target_pairs={{0,64},{64,0},{1,65},{65,1},{2,66},{66,2},{3,67},{67,3},{4,68},{68... | collective-permute-start | bytes 589832 | tf_op jit(solution)/shard_map/ppermute | solution.py:29
  70.9 29.2 %collective-permute-start.13 = (bf16[2,96,512]{2,1,0:T(8,128)(2,1)S(1)}, bf16[2,96,512]{2,1,0:T(8,128)(2,1)S(1)}, u32[]{:S(2)}, u32[]{:S(2)}) collective-permute-start(bf16[2,96,512]{2,1,0:T(8,128)(2,1)S(1)} %collective-permute-done.10.near_after), channel_id=1, source_target_pairs={{0,64},{64,0},{1,65},{65,1},{2,66},{66,2},{3,67},{67,3},{4,68},{68... | collective-permute-start | bytes 589832 | tf_op jit(solution)/shard_map/ppermute | solution.py:29
  80.3 27.2 %all-to-all-start.1 = ((f32[64,1,128]{2,1,0:T(1,128)}), f32[64,1,128]{2,1,0:T(1,128)S(1)}, u32[]{:S(2)}, u32[]{:S(2)}) async-start(f32[64,1,128]{2,1,0:T(1,128)} %get-tuple-element.26), calls=%async_computation.1 | async-start | bytes 65536 | tf_op jit(solution)/shard_map/all_to_all | solution.py:410
  95.4 12.1 %collective-permute-start.17 = (bf16[96,256]{1,0:T(8,128)(2,1)S(1)}, bf16[96,256]{1,0:T(8,128)(2,1)S(1)}, u32[]{:S(2)}, u32[]{:S(2)}) collective-permute-start(bf16[96,256]{1,0:T(8,128)(2,1)S(1)} %get-tuple-element.57), channel_id=1, source_target_pairs={{0,192},{16,224},{32,128},{48,160},{64,208},{80,240},{96,144},{112... | collective-permute-start | bytes 147464 | tf_op jit(solution)/shard_map/ppermute | solution.py:29
  99.2 8.4 %collective-permute-start.16 = (bf16[96,256]{1,0:T(8,128)(2,1)S(1)}, bf16[96,256]{1,0:T(8,128)(2,1)S(1)}, u32[]{:S(2)}, u32[]{:S(2)}) collective-permute-start(bf16[96,256]{1,0:T(8,128)(2,1)S(1)} %get-tuple-element.58), channel_id=1, source_target_pairs={{0,128},{16,160},{32,192},{48,224},{64,144},{80,176},{96,208},{112... | collective-permute-start | bytes 147464 | tf_op jit(solution)/shard_map/ppermute | solution.py:29
  100.0 24.8 %copy-start.26 = (bf16[2,96,512]{2,1,0:T(8,128)(2,1)}, bf16[2,96,512]{2,1,0:T(8,128)(2,1)S(1)}, u32[]{:S(2)}) copy-start(bf16[2,96,512]{2,1,0:T(8,128)(2,1)S(1)} %collective-permute-done.12.far_before) | copy-start | bytes 589828
  100.0 7.5 %collective-permute-start.15 = (bf16[96,256]{1,0:T(8,128)(2,1)S(1)}, bf16[96,256]{1,0:T(8,128)(2,1)S(1)}, u32[]{:S(2)}, u32[]{:S(2)}) collective-permute-start(bf16[96,256]{1,0:T(8,128)(2,1)S(1)} %get-tuple-element.59), channel_id=1, source_target_pairs={{0,64},{16,96},{32,0},{48,32},{64,80},{80,112},{96,16},{112,48},{1... | collective-permute-start | bytes 147464 | tf_op jit(solution)/shard_map/ppermute | solution.py:29
  100.1 24.8 %copy-start.27 = (bf16[2,96,512]{2,1,0:T(8,128)(2,1)}, bf16[2,96,512]{2,1,0:T(8,128)(2,1)S(1)}, u32[]{:S(2)}) copy-start(bf16[2,96,512]{2,1,0:T(8,128)(2,1)S(1)} %collective-permute-done.13.far_after) | copy-start | bytes 589828
  100.1 7.5 %collective-permute-start.14 = (bf16[96,256]{1,0:T(8,128)(2,1)S(1)}, bf16[96,256]{1,0:T(8,128)(2,1)S(1)}, u32[]{:S(2)}, u32[]{:S(2)}) collective-permute-start(bf16[96,256]{1,0:T(8,128)(2,1)S(1)} %get-tuple-element.60), channel_id=1, source_target_pairs={{0,0},{16,32},{32,64},{48,96},{64,16},{80,48},{96,80},{112,112},{1... | collective-permute-start | bytes 147464 | tf_op jit(solution)/shard_map/ppermute | solution.py:29
  107.5 17.3 %copy-start.23 = (bf16[2,96,1024]{2,1,0:T(8,128)(2,1)}, bf16[2,96,1024]{2,1,0:T(8,128)(2,1)S(1)}, u32[]{:S(2)}) copy-start(bf16[2,96,1024]{2,1,0:T(8,128)(2,1)S(1)} %collective-permute-done.11.far) | copy-start | bytes 1179652
  107.5 0.7 copy-start.11
  107.6 0.7 copy-start.12
  107.6 0.7 copy-start.13
  108.3 0.6 copy-start.14
  111.9 11.7 %collective-permute-start.20 = (bf16[96,1024]{1,0:T(8,128)(2,1)}, bf16[96,1024]{1,0:T(8,128)(2,1)S(1)}, u32[]{:S(2)}, u32[]{:S(2)}) collective-permute-start(bf16[96,1024]{1,0:T(8,128)(2,1)} %get-tuple-element.32.clip0.clip), channel_id=1, source_target_pairs={{0,3},{1,0},{2,1},{3,2},{4,7},{5,4},{6,5},{7,6},{8,11},{9,8},{10,9... | collective-permute-start | bytes 589832 | tf_op jit(solution)/shard_map/ppermute | solution.py:29
  112.0 11.6 %collective-permute-start.19 = (bf16[96,1024]{1,0:T(8,128)(2,1)}, bf16[96,1024]{1,0:T(8,128)(2,1)S(1)}, u32[]{:S(2)}, u32[]{:S(2)}) collective-permute-start(bf16[96,1024]{1,0:T(8,128)(2,1)} %get-tuple-element.32.clip0.clip), channel_id=1, source_target_pairs={{0,2},{1,3},{2,0},{3,1},{4,6},{5,7},{6,4},{7,5},{8,10},{9,11},{10,... | collective-permute-start | bytes 589832 | tf_op jit(solution)/shard_map/ppermute | solution.py:29
  112.1 12.8 %collective-permute-start.18 = (bf16[96,1024]{1,0:T(8,128)(2,1)}, bf16[96,1024]{1,0:T(8,128)(2,1)S(1)}, u32[]{:S(2)}, u32[]{:S(2)}) collective-permute-start(bf16[96,1024]{1,0:T(8,128)(2,1)} %get-tuple-element.32.clip0.clip), channel_id=1, source_target_pairs={{0,1},{1,2},{2,3},{3,0},{4,5},{5,6},{6,7},{7,4},{8,9},{9,10},{10,1... | collective-permute-start | bytes 589832 | tf_op jit(solution)/shard_map/ppermute | solution.py:29
  114.6 8.1 %collective-permute-start.21 = (bf16[96,512]{1,0:T(8,128)(2,1)S(1)}, bf16[96,512]{1,0:T(8,128)(2,1)S(1)}, u32[]{:S(2)}, u32[]{:S(2)}) collective-permute-start(bf16[96,512]{1,0:T(8,128)(2,1)S(1)} %bitcast.61), channel_id=1, source_target_pairs={{0,4},{4,8},{8,12},{12,16},{16,20},{20,24},{24,28},{28,32},{32,36}... | collective-permute-start | bytes 294920 | tf_op jit(solution)/shard_map/ppermute | solution.py:29
  117.7 5.9 %collective-permute-start.22 = (bf16[96,512]{1,0:T(8,128)(2,1)S(1)}, bf16[96,512]{1,0:T(8,128)(2,1)S(1)}, u32[]{:S(2)}, u32[]{:S(2)}) collective-permute-start(bf16[96,512]{1,0:T(8,128)(2,1)S(1)} %bitcast.60), channel_id=1, source_target_pairs={{4,0},{8,4},{12,8},{16,12},{20,16},{24,20},{28,24},{32,28},{36,32}... | collective-permute-start | bytes 294920 | tf_op jit(solution)/shard_map/ppermute | solution.py:29
  122.6 8.4 %copy-start.31 = (bf16[96,512]{1,0:T(8,128)(2,1)}, bf16[96,512]{1,0:T(8,128)(2,1)S(1)}, u32[]{:S(2)}) copy-start(bf16[96,512]{1,0:T(8,128)(2,1)S(1)} %collective-permute-done.21.before) | copy-start | bytes 294916
  123.6 7.4 %copy-start.32 = (bf16[96,512]{1,0:T(8,128)(2,1)}, bf16[96,512]{1,0:T(8,128)(2,1)S(1)}, u32[]{:S(2)}) copy-start(bf16[96,512]{1,0:T(8,128)(2,1)S(1)} %collective-permute-done.22.after) | copy-start | bytes 294916
  123.6 1.3 copy-start.28
  123.6 1.3 copy-start.29
  124.9 0.7 copy-start.30
  125.5 11.6 %copy-start.1 = (bf16[3,3,3,96,384]{4,3,2,1,0:T(8,128)(2,1)S(1)}, bf16[3,3,3,96,384]{4,3,2,1,0:T(8,128)(2,1)}, u32[]{:S(2)}) copy-start(bf16[3,3,3,96,384]{4,3,2,1,0:T(8,128)(2,1)} %param.23) | copy-start | bytes 5971972
  131.0 20.1 %all-to-all-start.2 = ((bf16[16,8,16,128]{3,2,1,0:T(8,128)(2,1)}), bf16[16,8,16,128]{3,2,1,0:T(8,128)(2,1)S(1)}, u32[]{:S(2)}, u32[]{:S(2)}) async-start(bf16[16,8,16,128]{3,2,1,0:T(8,128)(2,1)} %bitcast.57), calls=%async_computation.2 | async-start | bytes 1048576 | tf_op jit(solution)/shard_map/all_to_all | solution.py:451
  144.9 11.7 %copy-start.2 = (bf16[4,96,1024]{2,1,0:T(8,128)(2,1)S(1)}, bf16[4,96,1024]{2,1,0:T(8,128)(2,1)}, u32[]{:S(2)}) copy-start(bf16[4,96,1024]{2,1,0:T(8,128)(2,1)} %convolution.1) | copy-start | bytes 2359300
  144.9 46.2 %copy-start.8 = (bf16[96,1024]{1,0:T(8,128)(2,1)S(1)}, bf16[96,1024]{1,0:T(8,128)(2,1)}, u32[]{:S(2)}) copy-start(bf16[96,1024]{1,0:T(8,128)(2,1)} %get-tuple-element.30) | copy-start | bytes 589828
  144.9 46.2 %copy-start.19 = (f32[96]{0:T(128)S(1)}, f32[96]{0:T(128)}, u32[]{:S(2)}) copy-start(f32[96]{0:T(128)} %param.24) | copy-start | bytes 1156
  152.1 35.2 %all-to-all-start.3 = ((bf16[16,8,16,128]{3,2,1,0:T(8,128)(2,1)}), bf16[16,8,16,128]{3,2,1,0:T(8,128)(2,1)S(1)}, u32[]{:S(2)}, u32[]{:S(2)}) async-start(bf16[16,8,16,128]{3,2,1,0:T(8,128)(2,1)} %broadcast_in_dim.34), calls=%async_computation.3 | async-start | bytes 1048576 | tf_op jit(solution)/shard_map/all_to_all | solution.py:50
  156.7 33.5 %collective-permute-start.23 = (bf16[96,1024]{1,0:T(8,128)(2,1)S(1)}, bf16[96,1024]{1,0:T(8,128)(2,1)}, u32[]{:S(2)}, u32[]{:S(2)}) collective-permute-start(bf16[96,1024]{1,0:T(8,128)(2,1)S(1)} %get-tuple-element.52), channel_id=1, source_target_pairs={{0,64},{64,0},{128,192},{192,128},{1,65},{65,1},{129,193},{193,129... | collective-permute-start | bytes 589832 | tf_op jit(solution)/shard_map/ppermute | solution.py:29
  159.4 31.7 %collective-permute-start.25 = (bf16[96,1024]{1,0:T(8,128)(2,1)S(1)}, bf16[96,1024]{1,0:T(8,128)(2,1)}, u32[]{:S(2)}, u32[]{:S(2)}) collective-permute-start(bf16[96,1024]{1,0:T(8,128)(2,1)S(1)} %get-tuple-element.53), channel_id=1, source_target_pairs={{0,192},{64,128},{128,64},{192,0},{1,193},{65,129},{129,65},{193,1... | collective-permute-start | bytes 589832 | tf_op jit(solution)/shard_map/ppermute | solution.py:29
  162.4 28.6 %collective-permute-start.24 = (bf16[96,1024]{1,0:T(8,128)(2,1)S(1)}, bf16[96,1024]{1,0:T(8,128)(2,1)}, u32[]{:S(2)}, u32[]{:S(2)}) collective-permute-start(bf16[96,1024]{1,0:T(8,128)(2,1)S(1)} %get-tuple-element.54), channel_id=1, source_target_pairs={{0,128},{64,192},{128,0},{192,64},{1,129},{65,193},{129,1},{193,65... | collective-permute-start | bytes 589832 | tf_op jit(solution)/shard_map/ppermute | solution.py:29
  187.3 28.2 %copy-start = (bf16[16,8,16,128]{3,2,1,0:T(8,128)(2,1)}, bf16[16,8,16,128]{3,2,1,0:T(8,128)(2,1)S(1)}, u32[]{:S(2)}) copy-start(bf16[16,8,16,128]{3,2,1,0:T(8,128)(2,1)S(1)} %all-to-all-done.3) | copy-start | bytes 1572868
  187.3 11.5 %collective-permute-start.28 = (bf16[128,16,128]{2,1,0:T(8,128)(2,1)S(1)}, bf16[128,16,128]{2,1,0:T(8,128)(2,1)S(1)}, u32[]{:S(2)}, u32[]{:S(2)}) collective-permute-start(bf16[128,16,128]{2,1,0:T(8,128)(2,1)S(1)} %bitcast.50), channel_id=1, source_target_pairs={{0,3},{1,0},{2,1},{3,2},{4,7},{5,4},{6,5},{7,6},{8,11},{9,8},{10,9... | collective-permute-start | bytes 1572872 | tf_op jit(solution)/shard_map/ppermute | solution.py:29
  189.0 12.8 %collective-permute-start.27 = (bf16[128,16,128]{2,1,0:T(8,128)(2,1)S(1)}, bf16[128,16,128]{2,1,0:T(8,128)(2,1)S(1)}, u32[]{:S(2)}, u32[]{:S(2)}) collective-permute-start(bf16[128,16,128]{2,1,0:T(8,128)(2,1)S(1)} %bitcast.51), channel_id=1, source_target_pairs={{0,2},{1,3},{2,0},{3,1},{4,6},{5,7},{6,4},{7,5},{8,10},{9,11},{10,... | collective-permute-start | bytes 1572872 | tf_op jit(solution)/shard_map/ppermute | solution.py:29
  190.2 25.4 %collective-permute-start.26 = (bf16[128,16,128]{2,1,0:T(8,128)(2,1)S(1)}, bf16[128,16,128]{2,1,0:T(8,128)(2,1)S(1)}, u32[]{:S(2)}, u32[]{:S(2)}) collective-permute-start(bf16[128,16,128]{2,1,0:T(8,128)(2,1)S(1)} %bitcast.52), channel_id=1, source_target_pairs={{0,1},{1,2},{2,3},{3,0},{4,5},{5,6},{6,7},{7,4},{8,9},{9,10},{10,1... | collective-permute-start | bytes 1572872 | tf_op jit(solution)/shard_map/ppermute | solution.py:29
  198.9 16.7 %copy-start.3 = (bf16[128,16,128]{2,1,0:T(8,128)(2,1)}, bf16[128,16,128]{2,1,0:T(8,128)(2,1)S(1)}, u32[]{:S(2)}) copy-start(bf16[128,16,128]{2,1,0:T(8,128)(2,1)S(1)} %collective-permute-done.28.table3) | copy-start | bytes 1572868
  201.8 13.8 %copy-start.4 = (bf16[128,16,128]{2,1,0:T(8,128)(2,1)}, bf16[128,16,128]{2,1,0:T(8,128)(2,1)S(1)}, u32[]{:S(2)}) copy-start(bf16[128,16,128]{2,1,0:T(8,128)(2,1)S(1)} %collective-permute-done.27.table2) | copy-start | bytes 1572868
  215.6 0.8 copy-start.5
  (1 other events, 0.6 us)

commit v2 on v1

--- a/solution.py
+++ b/solution.py
@@ -190,7 +190,7 @@
 def gate_kernel(at, packed, piece0, piece1, piece2, piece3, gain, shift, gated, hidden, held):
     ch, valid = at[0], at[1]
     count = valid.astype(F32) * (12 * 32 * 128)
-    table = jnp.sum(packed[...], axis=0)
+    table = jnp.sum(packed[...], axis=0, keepdims=True)
     group = lax.broadcasted_iota(jnp.int32, (96, 128), 0) // 12 + ch * 8
     mean = column(table, group) / count
     var = column(table, group + 32) / count - mean * mean
@@ -214,31 +214,12 @@
 
 
 def grad_kernel(
-    at,
-    clip0,
-    clip1,
-    clip2,
-    clip3,
-    near,
-    near_before,
-    near_after,
-    far,
-    far_before,
-    far_after,
-    out,
-    gs,
-    cs,
-    cot,
-    before,
-    after,
+    at, clip0, clip1, clip2, clip3, near0, near1, far0, far1, out, gs, cs, cot, before, after
 ):
-    for to, first, second in (
-        (cot, near, far),
-        (before, near_before, far_before),
-        (after, near_after, far_after),
-    ):
-        to[0:2] = first[...]
-        to[2:4] = second[...]
+    for i, part in enumerate((near0, near1, far0, far1)):
+        cot[i] = part[:, :1024]
+        before[i] = part[:, 1024:1536]
+        after[i] = part[:, 1536:]
     gs[864:, :] = jnp.zeros((32, 4096), BF)
     for s, gated in enumerate((clip0, clip1, clip2, clip3)):
         for kt in range(2):
@@ -290,7 +271,7 @@
                 lane = end
 
 
-def conv_kernel(clip, before, after, weight, out, stack):
+def conv_kernel(at, clip, before, after, weight, keep, send, stack, held):
     stack[:, :512] = jnp.zeros((864, 512), BF)
     for f in range(4):
         for p in range(4):
@@ -314,7 +295,10 @@
         total = total + jnp.dot(
             weight[kt], stack[:, kt * 256 : kt * 256 + 1024], preferred_element_type=F32
         )
-    out[...] = total.astype(BF).reshape(4, 96, 1024)
+    held[...] = total.astype(BF).reshape(4, 96, 1024)
+    for zh in range(2):
+        keep[zh] = held[2 * zh + at[0]]
+        send[zh] = held[2 * zh + 1 - at[0]]
 
 
 def body(
@@ -354,13 +338,25 @@
     parts = ring(mine, "x")
     others = [permute(p, ("co",), lambda i: (1 - i,)) for p in parts]
 
+    masked = (cotangent.reshape(96, 4, 256) * mask.astype(BF)[None, :, None]).reshape(96, 1024)
+    lines = masked.reshape(96, 4, 2, 128)
+    before, after = halo(lines[:, :, 1].reshape(96, 512), lines[:, :, 0].reshape(96, 512))
+    bundle = jnp.concatenate([masked, before, after], axis=1)
+    bundle, _ = lax.optimization_barrier((bundle, parts[1]))
+    near = [
+        permute(
+            bundle, ("zh", "co", "y"), lambda zh, co, y: ((y // 2 + k) % 2, y % 2, 2 * zh + co)
+        )
+        for k in range(2)
+    ]
+
     frame = 2 * zh + zl // 2
     at = jnp.stack([co, 2 * (zl % 2) + co, valid, frame]).astype(jnp.int32)
     hidden_q, packed = pl.pallas_call(
         attend_kernel,
         out_shape=(
             jax.ShapeDtypeStruct((384, 256), BF),
-            jax.ShapeDtypeStruct((64, 1, 128), F32),
+            jax.ShapeDtypeStruct((16, 1, 128), F32),
         ),
         in_specs=[scalars] + [whole] * 12,
         out_specs=(whole, whole),
@@ -388,27 +384,11 @@
 
         pieces.append(permute(piece, ("zh", "co", "zl"), to_channels))
 
-    masked = (cotangent.reshape(96, 4, 256) * mask.astype(BF)[None, :, None]).reshape(96, 1024)
-    masked, _ = lax.optimization_barrier((masked, parts[1]))
-    blocks = jnp.stack(
-        [
-            permute(
-                masked,
-                ("zh", "co", "y"),
-                lambda zh, co, y: ((y // 2 + k) % 2, y % 2, 2 * zh + co),
-            )
-            for k in range(2)
-        ]
-    )
-    lines = blocks.reshape(2, 96, 4, 2, 128)
-    before, after = halo(
-        lines[:, :, :, 1].reshape(2, 96, 512), lines[:, :, :, 0].reshape(2, 96, 512)
-    )
-    near = (blocks, before, after)
+    packed = lax.all_to_all(packed, ("zh", "co", "zl"), 0, 0, tiled=True)
+    packed = jnp.sum(packed, axis=0)
+    packed, near, pieces = lax.optimization_barrier((packed, near, pieces))
+    packed = jnp.concatenate(ring(packed, "x"), axis=0)
     far = [permute(v, ("co",), lambda i: (1 - i,)) for v in near]
-
-    packed = lax.all_to_all(packed, ("zh", "co", "zl", "x"), 0, 0, tiled=True)
-    packed, near, far = lax.optimization_barrier((packed, near, far))
     gated, hidden = pl.pallas_call(
         gate_kernel,
         out_shape=(jax.ShapeDtypeStruct((96, 1024), BF), jax.ShapeDtypeStruct((96, 1024), BF)),
@@ -429,12 +409,11 @@
     rows = gated.reshape(96, 4, 2, 128)
     above, below = halo(rows[:, :, 1].reshape(96, 512), rows[:, :, 0].reshape(96, 512))
     clips = ring(gated, "y")
-    kernels = conv_weight.transpose(0, 4, 1, 2, 3).reshape(3, 384, 864)
-    clips, above, below, kernels = lax.optimization_barrier((clips, above, below, kernels))
+    clips, above, below = lax.optimization_barrier((clips, above, below))
     table = pl.pallas_call(
         grad_kernel,
         out_shape=jax.ShapeDtypeStruct((128, 16, 128), BF),
-        in_specs=[scalars] + [whole] * 10,
+        in_specs=[scalars] + [whole] * 8,
         out_specs=whole,
         scratch_shapes=[
             pltpu.VMEM((896, 4096), BF),
@@ -447,19 +426,27 @@
         cost_estimate=cost(4 * 10**9, 20 * 10**6),
         name="weight_grad",
     )(jnp.stack([y, co, zh]).astype(jnp.int32), *clips, *near, *far)
-    table, above, below = lax.optimization_barrier((table, above, below))
+    table, conv_weight = lax.optimization_barrier((table, conv_weight))
+    kernels = conv_weight.transpose(0, 4, 1, 2, 3).reshape(3, 384, 864)
     shares = lax.all_to_all(table.reshape(16, 8, 16, 128), ("zl", "x"), 0, 0, tiled=True)
-    partial = pl.pallas_call(
+    keep, send = pl.pallas_call(
         conv_kernel,
-        out_shape=jax.ShapeDtypeStruct((4, 96, 1024), BF),
-        scratch_shapes=[pltpu.VMEM((864, 1536), BF)],
+        out_shape=(jax.ShapeDtypeStruct((2, 96, 1024), BF),) * 2,
+        in_specs=[scalars] + [whole] * 4,
+        out_specs=(whole, whole),
+        scratch_shapes=[pltpu.VMEM((864, 1536), BF), pltpu.VMEM((4, 96, 1024), BF)],
         compiler_params=params,
         cost_estimate=cost(3 * 10**9, 12 * 10**6),
         name="convolution",
-    )(clips[0], above, below, kernels)
-    shares, partial = lax.optimization_barrier((shares, partial))
+    )(co.astype(jnp.int32)[None], clips[0], above, below, kernels)
+    send = permute(send, ("co",), lambda i: (1 - i,))
+    summed = keep.astype(F32) + send.astype(F32)
+    near = lax.dynamic_index_in_dim(summed, zh, 0, keepdims=False)
+    far = lax.dynamic_index_in_dim(summed, 1 - zh, 0, keepdims=False).astype(BF)
+    shares, near, far = lax.optimization_barrier((shares, near, far))
     share = jnp.sum(shares.astype(F32), axis=0).astype(BF)
     table = spread(share, ("zl", "x"), 16).reshape(128, 16, 128)
+    table, near, far = lax.optimization_barrier((table, near, far))
     weight_grad = pl.pallas_call(
         join_kernel,
         out_shape=jax.ShapeDtypeStruct((2592, 384), F32),
@@ -472,13 +459,7 @@
     )(y.astype(jnp.int32)[None], *ring(table, "y"))
     weight_grad = weight_grad.reshape(3, 3, 3, 96, 384)
 
-    conv = lax.dynamic_index_in_dim(partial, ch, 0, keepdims=False).astype(F32)
-    for k in range(1, 4):
-        piece = lax.dynamic_index_in_dim(partial, ch ^ k, 0, keepdims=False)
-        piece = permute(
-            piece, ("zh", "co"), lambda zh, co, k=k: (zh ^ (k >> 1), co ^ (k & 1))
-        )
-        conv = conv + piece.astype(F32)
+    conv = near + permute(far, ("zh",), lambda i: (1 - i,)).astype(F32)
     mixed = hidden.astype(F32) + conv + conv_bias[:, None]
     mixed = (mixed.reshape(96, 4, 256) * mask[None, :, None]).astype(BF)
     return mixed.reshape(96, 1, 4, 2, 128), weight_grad

time: 222 us -> 214 us (0.964)
  waiting for transfers between devices: 60.5 us -> 52.5 us
    all_to_all x2, waiting for transfers between devices: 22.6 us -> 11.9 us  [the longest x1 11.9 us: body(): mine = lax.all_to_all(by_frame, ('zh', 'zl'), 0, 0, tiled=True)]
    ppermute x29 -> x30, waiting for transfers between devices: 31.7 us -> 40 us  [permute(): return lax.ppermute(value, axes, pairs)]
    all_to_all x1, waiting for transfers between devices: 6.27 us -> 0.64 us  [body(): lax.all_to_all(table.reshape(16, 8, 16, 128), ('zl', 'x'), 0, 0, tiled=True)]
    optimization_barrier x1 -> x0, local copies, waits for them, and re-layouts: 2.4 us -> none  [body(): lax.optimization_barrier((clips, above, below, kernels))]
    reshape x0 -> x1, local copies, waits for them, and re-layouts: none -> 2.4 us  [body(): kernels = conv_weight.transpose(0, 4, 1, 2, 3).reshape(3, 384, 864)]
    ppermute x29 -> x30, starting transfers between devices: 66.9 us -> 65.6 us  [permute(): return lax.ppermute(value, axes, pairs)]
  transfers between devices with their start and end apart: 32 -> 33, of which waited for: 10 -> 14; matrix products, arithmetic and copies ran while one was open for 6% -> 7% of each run, Pallas kernels for 7% -> 8%
where the time goes in v2:
time: 214 us; the launch traced here: 212 us
  starting transfers between devices  90.1 us (42%)
  waiting for transfers between devices  52.5 us (25%)
  Pallas kernels  28.1 us (13%)
  blocking collectives  20.7 us (10%)
  local copies, waits for them, and re-layouts  14.3 us (7%)
  other arithmetic  4.92 us (2%)
    ppermute x30, starting transfers between devices, permute(): return lax.ppermute(value, axes, pairs)  65.6 us
    ppermute x30, waiting for transfers between devices, permute(): return lax.ppermute(value, axes, pairs)  40 us
    all_to_all x1, blocking collectives, spread(): return lax.all_to_all(copies, axes, 0, 0, tiled=True)  20.7 us
    all_to_all x1, waiting for transfers between devices, body(): mine = lax.all_to_all(by_frame, ('zh', 'zl'), 0, 0, tiled=True)  11.9 us
    pallas_call x1, Pallas kernels, body(): pl.pallas_call(attend_kernel, out_shape=(jax.ShapeDtypeStruct((384, 256),...  9.14 us
    all_to_all x1, starting transfers between devices, body(): packed = lax.all_to_all(packed, ('zh', 'co', 'zl'), 0, 0, tiled=True)  8.99 us
    all_to_all x1, starting transfers between devices, body(): lax.all_to_all(table.reshape(16, 8, 16, 128), ('zl', 'x'), 0, 0, tiled=True)  7.9 us
    all_to_all x1, starting transfers between devices, body(): mine = lax.all_to_all(by_frame, ('zh', 'zl'), 0, 0, tiled=True)  7.55 us
  transfers between devices with their start and end apart: 33, of which 14 were waited for; matrix products, arithmetic and copies ran while one was open for 7% of the time, Pallas kernels for 8%

profile of v2, /device:TPU:65, one launch (start us, length us, event | category | flops | bytes accessed | tf_op | source)
XLA Modules:
  0.0 212.4 jit_solution(11873599361184186272)
XLA Ops:
  1.3 1.7 reshape.60.frames
  3.1 1.9 pack.1
  5.0 7.6 %all-to-all-start = ((bf16[8,112,256]{2,1,0:T(8,128)(2,1)}), bf16[8,112,256]{2,1,0:T(8,128)(2,1)S(1)}, u32[]{:S(2)}, u32[]{:S(2)}) async-start(bf16[8,112,256]{2,1,0:T(8,128)(2,1)} %pack.1), calls=%async_computation | async-start | bytes 917504 | tf_op jit(solution)/shard_map/all_to_all | solution.py:337
  12.5 11.9 %all-to-all-done.own0 = bf16[8,112,256]{2,1,0:T(8,128)(2,1)S(1)} async-done(((bf16[8,112,256]{2,1,0:T(8,128)(2,1)}), bf16[8,112,256]{2,1,0:T(8,128)(2,1)S(1)}, u32[]{:S(2)}, u32[]{:S(2)}) %all-to-all-start) | async-done | bytes 458784 | tf_op jit(solution)/shard_map/all_to_all | solution.py:337
  24.4 2.5 %collective-permute-start.2 = (bf16[8,112,256]{2,1,0:T(8,128)(2,1)S(1)}, bf16[8,112,256]{2,1,0:T(8,128)(2,1)S(1)}, u32[]{:S(2)}, u32[]{:S(2)}) collective-permute-start(bf16[8,112,256]{2,1,0:T(8,128)(2,1)S(1)} %all-to-all-done.own0), channel_id=1, source_target_pairs={{0,12},{4,0},{8,4},{12,8},{1,13},{5,1},{9,5},{13,9},{2,14},{6,2},{... | collective-permute-start | bytes 1376264 | tf_op jit(solution)/shard_map/ppermute | solution.py:29
  27.4 0.6 collective-permute-start
  28.2 1.1 slice_reduce_fusion.3
  29.3 4.1 %collective-permute-start.8 = (bf16[96,512]{1,0:T(8,128)(2,1)S(1)}, bf16[96,512]{1,0:T(8,128)(2,1)S(1)}, u32[]{:S(2)}, u32[]{:S(2)}) collective-permute-start(bf16[96,512]{1,0:T(8,128)(2,1)S(1)} %bitcast.60), channel_id=1, source_target_pairs={{4,0},{8,4},{12,8},{16,12},{20,16},{24,20},{28,24},{32,28},{36,32}... | collective-permute-start | bytes 294920 | tf_op jit(solution)/shard_map/ppermute | solution.py:29
  33.6 5.1 %collective-permute-start.3 = (bf16[8,112,256]{2,1,0:T(8,128)(2,1)S(1)}, bf16[8,112,256]{2,1,0:T(8,128)(2,1)S(1)}, u32[]{:S(2)}, u32[]{:S(2)}) collective-permute-start(bf16[8,112,256]{2,1,0:T(8,128)(2,1)S(1)} %all-to-all-done.own0), channel_id=1, source_target_pairs={{0,64},{64,0},{1,65},{65,1},{2,66},{66,2},{3,67},{67,3},{4,68},{68... | collective-permute-start | bytes 1376264 | tf_op jit(solution)/shard_map/ppermute | solution.py:29
  38.7 10.8 %collective-permute-start.6 = (bf16[8,112,256]{2,1,0:T(8,128)(2,1)S(1)}, bf16[8,112,256]{2,1,0:T(8,128)(2,1)}, u32[]{:S(2)}, u32[]{:S(2)}) collective-permute-start(bf16[8,112,256]{2,1,0:T(8,128)(2,1)S(1)} %collective-permute-done.2.own3), channel_id=1, source_target_pairs={{0,64},{64,0},{1,65},{65,1},{2,66},{66,2},{3,67},{67,3},{4,68},{68... | collective-permute-start | bytes 1376264 | tf_op jit(solution)/shard_map/ppermute | solution.py:29
  49.6 1.0 collective-permute-done.own1
  51.2 0.6 broadcast_in_dim.31.qkv_bias
  51.8 0.8 broadcast_in_dim.36.out_bias
  52.6 1.9 collective-permute-start.7
  54.5 0.6 pad_add_fusion.1.at
  55.1 5.8 %collective-permute-done.7 = bf16[96,512]{1,0:T(8,128)(2,1)S(1)} collective-permute-done((bf16[96,512]{1,0:T(8,128)(2,1)S(1)}, bf16[96,512]{1,0:T(8,128)(2,1)S(1)}, u32[]{:S(2)}, u32[]{:S(2)}) %collective-permute-start.7) | collective-permute-done | bytes 98336 | tf_op jit(solution)/shard_map/ppermute | solution.py:29
  61.0 5.4 %collective-permute-start.10 = (bf16[96,2048]{1,0:T(8,128)(2,1)S(1)}, bf16[96,2048]{1,0:T(8,128)(2,1)S(1)}, u32[]{:S(2)}, u32[]{:S(2)}) collective-permute-start(bf16[96,2048]{1,0:T(8,128)(2,1)S(1)} %pad_maximum_fusion), channel_id=1, source_target_pairs={{0,128},{1,192},{2,0},{3,64},{64,129},{65,193},{66,1},{67,65},{128... | collective-permute-start | bytes 1179656 | tf_op jit(solution)/shard_map/ppermute | solution.py:29
  66.4 2.1 collective-permute-start.9
  68.6 9.1 %attention.1 = (bf16[384,256]{1,0:T(8,128)(2,1)}, f32[16,1,128]{2,1,0:T(1,128)}) custom-call(s32[4]{0:T(128)} %pad_add_fusion.1.at, bf16[8,112,256]{2,1,0:T(8,128)(2,1)} %copy-done.6, bf16[8,112,256]{2,1,0:T(8,128)(2,1)} %copy-done.19, bf16[8,112,256]{2,1,0:T(8,128)(2,1)} %copy-done.18, bf16[8,112,256]{2,1,0:T(8,128)(2,1)} %copy-done.17, ...), custom_call_target="tpu_custom_call" | custom-call | flops 4000000000 | bytes 20000000 | tf_op jit(solution)/shard_map/attention/pallas_call | solution.py:355
  77.8 9.0 %all-to-all-start.1 = ((f32[16,1,128]{2,1,0:T(1,128)}), f32[16,1,128]{2,1,0:T(1,128)S(1)}, u32[]{:S(2)}, u32[]{:S(2)}) async-start(f32[16,1,128]{2,1,0:T(1,128)} %get-tuple-element.30), calls=%async_computation.1 | async-start | bytes 16384 | tf_op jit(solution)/shard_map/all_to_all | solution.py:387
  86.7 0.9 constant_dynamic-slice_fusion
  87.6 3.6 %collective-permute-start.14 = (bf16[96,256]{1,0:T(8,128)(2,1)S(1)}, bf16[96,256]{1,0:T(8,128)(2,1)S(1)}, u32[]{:S(2)}, u32[]{:S(2)}) collective-permute-start(bf16[96,256]{1,0:T(8,128)(2,1)S(1)} %get-tuple-element.62), channel_id=1, source_target_pairs={{0,192},{16,224},{32,128},{48,160},{64,208},{80,240},{96,144},{112... | collective-permute-start | bytes 147464 | tf_op jit(solution)/shard_map/ppermute | solution.py:29
  91.2 0.9 collective-permute-start.13
  92.2 5.4 %collective-permute-start.11 = (bf16[96,256]{1,0:T(8,128)(2,1)S(1)}, bf16[96,256]{1,0:T(8,128)(2,1)S(1)}, u32[]{:S(2)}, u32[]{:S(2)}) collective-permute-start(bf16[96,256]{1,0:T(8,128)(2,1)S(1)} %get-tuple-element.65), channel_id=1, source_target_pairs={{0,0},{16,32},{32,64},{48,96},{64,16},{80,48},{96,80},{112,112},{1... | collective-permute-start | bytes 147464 | tf_op jit(solution)/shard_map/ppermute | solution.py:29
  97.6 0.7 pad_add_fusion.at
  98.8 1.5 collective-permute-start.17
  100.3 0.6 collective-permute-start.15
  100.8 0.7 copy.22.gain
  101.6 0.7 copy.23.shift
  102.3 2.1 collective-permute-start.23
  104.4 0.6 pad_maximum_fusion.1.packed
  105.0 1.9 gate.1
  106.9 1.0 reshape.63
  107.9 1.1 slice_reduce_fusion
  109.1 4.3 %collective-permute-start.21 = (bf16[96,512]{1,0:T(8,128)(2,1)S(1)}, bf16[96,512]{1,0:T(8,128)(2,1)}, u32[]{:S(2)}, u32[]{:S(2)}) collective-permute-start(bf16[96,512]{1,0:T(8,128)(2,1)S(1)} %bitcast.63), channel_id=1, source_target_pairs={{0,4},{4,8},{8,12},{12,16},{16,20},{20,24},{24,28},{28,32},{32,36}... | collective-permute-start | bytes 294920 | tf_op jit(solution)/shard_map/ppermute | solution.py:29
  113.3 3.1 %collective-permute-start.22 = (bf16[96,512]{1,0:T(8,128)(2,1)S(1)}, bf16[96,512]{1,0:T(8,128)(2,1)S(1)}, u32[]{:S(2)}, u32[]{:S(2)}) collective-permute-start(bf16[96,512]{1,0:T(8,128)(2,1)S(1)} %bitcast.62), channel_id=1, source_target_pairs={{4,0},{8,4},{12,8},{16,12},{20,16},{24,20},{28,24},{32,28},{36,32}... | collective-permute-start | bytes 294920 | tf_op jit(solution)/shard_map/ppermute | solution.py:29
  116.5 1.0 collective-permute-start.20
  117.5 0.8 collective-permute-start.19
  118.3 0.8 collective-permute-done.22.after
  119.1 0.6 pad_add_fusion.2.at
  119.7 1.6 collective-permute-done.20.clip3
  121.3 2.5 %collective-permute-done.19.clip2 = bf16[96,1024]{1,0:T(8,128)(2,1)S(1)} collective-permute-done((bf16[96,1024]{1,0:T(8,128)(2,1)}, bf16[96,1024]{1,0:T(8,128)(2,1)S(1)}, u32[]{:S(2)}, u32[]{:S(2)}) %collective-permute-start.19) | collective-permute-done | bytes 196640 | tf_op jit(solution)/shard_map/ppermute | solution.py:29
  123.8 2.4 %collective-permute-done.18.clip1 = bf16[96,1024]{1,0:T(8,128)(2,1)S(1)} collective-permute-done((bf16[96,1024]{1,0:T(8,128)(2,1)}, bf16[96,1024]{1,0:T(8,128)(2,1)S(1)}, u32[]{:S(2)}, u32[]{:S(2)}) %collective-permute-start.18) | collective-permute-done | bytes 196640 | tf_op jit(solution)/shard_map/ppermute | solution.py:29
  126.3 0.6 copy-done.26
  127.1 0.7 copy-done.23
  127.9 5.4 %weight_grad.1 = bf16[128,16,128]{2,1,0:T(8,128)(2,1)} custom-call(s32[3]{0:T(128)} %pad_add_fusion.2.at, bf16[96,1024]{1,0:T(8,128)(2,1)} %get-tuple-element.40.clip0.clip, bf16[96,1024]{1,0:T(8,128)(2,1)} %copy-done.26, bf16[96,1024]{1,0:T(8,128)(2,1)} %copy-done.25, bf16[96,1024]{1,0:T(8,128)(2,1)} %copy-done.24, ...), custom_call_target="tpu_custom_call" | custom-call | flops 4000000000 | bytes 20000000 | tf_op jit(solution)/shard_map/weight_grad/pallas_call | solution.py:413
  133.3 7.9 %all-to-all-start.2 = ((bf16[16,8,16,128]{3,2,1,0:T(8,128)(2,1)}), bf16[16,8,16,128]{3,2,1,0:T(8,128)(2,1)S(1)}, u32[]{:S(2)}, u32[]{:S(2)}) async-start(bf16[16,8,16,128]{3,2,1,0:T(8,128)(2,1)} %bitcast.55), calls=%async_computation.2 | async-start | bytes 1048576 | tf_op jit(solution)/shard_map/all_to_all | solution.py:431
  141.2 2.4 %copy.26.weight = bf16[3,384,864]{2,1,0:T(8,128)(2,1)} copy(bf16[3,384,864]{1,2,0:T(8,128)(2,1)S(1)} %bitcast.54) | data formatting | bytes 3981312 | tf_op jit(solution)/shard_map/reshape | solution.py:430
  143.6 5.4 %convolution.1 = (bf16[2,96,1024]{2,1,0:T(8,128)(2,1)}, bf16[2,96,1024]{2,1,0:T(8,128)(2,1)}) custom-call(s32[1]{0:T(128)} %bitcast.1.at, bf16[96,1024]{1,0:T(8,128)(2,1)} %get-tuple-element.40.clip0.clip, bf16[96,512]{1,0:T(8,128)(2,1)} %collective-permute-done.21.before, bf16[96,512]{1,0:T(8,128)(2,1)} %copy-done.27, bf16[3,384,864]{2,1,0:T(8,128)(2,1)} %copy.26.weight), custom_call_target="tpu_custom_call" | custom-call | flops 3000000000 | bytes 12000000 | tf_op jit(solution)/shard_map/convolution/pallas_call | solution.py:432
  149.0 2.7 %collective-permute-start.25 = (bf16[2,96,1024]{2,1,0:T(8,128)(2,1)}, bf16[2,96,1024]{2,1,0:T(8,128)(2,1)S(1)}, u32[]{:S(2)}, u32[]{:S(2)}) collective-permute-start(bf16[2,96,1024]{2,1,0:T(8,128)(2,1)} %get-tuple-element.51), channel_id=1, source_target_pairs={{0,64},{64,0},{1,65},{65,1},{2,66},{66,2},{3,67},{67,3},{4,68},{68... | collective-permute-start | bytes 1179656 | tf_op jit(solution)/shard_map/ppermute | solution.py:29
  151.7 1.6 collective-permute-done.25
  153.3 1.1 convert_add_fusion
  154.5 0.6 all-to-all-done.2
  155.3 20.7 %all_to_all.20 = bf16[16,8,16,128]{3,2,1,0:T(8,128)(2,1)S(1)} all-to-all(bf16[16,8,16,128]{3,2,1,0:T(8,128)(2,1)S(1)} %broadcast_in_dim.35), channel_id=1, replica_groups=mesh['zh'=2,'co'=2,'zl'=4,'x'=4,'y'=4] {'zl','x'}, dimensions={0} | all-to-all | bytes 1048576 | tf_op jit(solution)/shard_map/all_to_all | solution.py:50
  176.0 4.6 %collective-permute-start.26 = (bf16[96,1024]{1,0:T(8,128)(2,1)S(1)}, bf16[96,1024]{1,0:T(8,128)(2,1)S(1)}, u32[]{:S(2)}, u32[]{:S(2)}) collective-permute-start(bf16[96,1024]{1,0:T(8,128)(2,1)S(1)} %fusion.1), channel_id=1, source_target_pairs={{0,128},{128,0},{1,129},{129,1},{2,130},{130,2},{3,131},{131,3},{4... | collective-permute-start | bytes 589832 | tf_op jit(solution)/shard_map/ppermute | solution.py:29
  180.6 0.8 collective-permute-start.28
  181.4 0.6 collective-permute-start.27
  182.1 8.1 %collective-permute-done.26 = bf16[96,1024]{1,0:T(8,128)(2,1)S(1)} collective-permute-done((bf16[96,1024]{1,0:T(8,128)(2,1)S(1)}, bf16[96,1024]{1,0:T(8,128)(2,1)S(1)}, u32[]{:S(2)}, u32[]{:S(2)}) %collective-permute-start.26) | collective-permute-done | bytes 196640 | tf_op jit(solution)/shard_map/ppermute | solution.py:29
  190.6 0.9 fusion
  191.5 1.1 collective-permute-done.29.table3
  192.6 1.5 collective-permute-done.28.table2
  194.0 13.1 %collective-permute-done.27.table1 = bf16[128,16,128]{2,1,0:T(8,128)(2,1)S(1)} collective-permute-done((bf16[128,16,128]{2,1,0:T(8,128)(2,1)S(1)}, bf16[128,16,128]{2,1,0:T(8,128)(2,1)S(1)}, u32[]{:S(2)}, u32[]{:S(2)}) %collective-permute-start.27) | collective-permute-done | bytes 524320 | tf_op jit(solution)/shard_map/ppermute | solution.py:29
  207.2 0.8 copy-done.5
  208.0 4.4 %join.1 = f32[2592,384]{1,0:T(8,128)} custom-call(s32[1]{0:T(128)} %bitcast.11.at, bf16[128,16,128]{2,1,0:T(8,128)(2,1)} %bitcast.53, bf16[128,16,128]{2,1,0:T(8,128)(2,1)} %copy-done.5, bf16[128,16,128]{2,1,0:T(8,128)(2,1)} %copy-done.4, bf16[128,16,128]{2,1,0:T(8,128)(2,1)} %copy-done.3), custom_call_target="tpu_custom_call" | custom-call | flops 1000000 | bytes 6000000 | tf_op jit(solution)/shard_map/join/pallas_call | solution.py:450
  (100 shorter events, 3.1 us)
Async XLA Ops:
  0.6 27.3 %copy-start.2 = (bf16[96,1,4,2,128]{4,3,2,1,0:T(2,128)(2,1)S(1)}, bf16[96,1,4,2,128]{4,3,2,1,0:T(2,128)(2,1)}, u32[]{:S(2)}) copy-start(bf16[96,1,4,2,128]{4,3,2,1,0:T(2,128)(2,1)} %param.25) | copy-start | bytes 589828
  0.6 50.6 %copy-start.12 = (f32[1152]{0:T(1024)S(1)}, f32[1152]{0:T(1024)}, u32[]{:S(2)}) copy-start(f32[1152]{0:T(1024)} %param.18) | copy-start | bytes 13828
  1.3 50.5 %copy-start.13 = (f32[384]{0:T(512)S(1)}, f32[384]{0:T(512)}, u32[]{:S(2)}) copy-start(f32[384]{0:T(512)} %param.20) | copy-start | bytes 4612
  5.0 19.4 %all-to-all-start = ((bf16[8,112,256]{2,1,0:T(8,128)(2,1)}), bf16[8,112,256]{2,1,0:T(8,128)(2,1)S(1)}, u32[]{:S(2)}, u32[]{:S(2)}) async-start(bf16[8,112,256]{2,1,0:T(8,128)(2,1)} %pack.1), calls=%async_computation | async-start | bytes 917504 | tf_op jit(solution)/shard_map/all_to_all | solution.py:337
  24.4 44.2 %copy-start.6 = (bf16[8,112,256]{2,1,0:T(8,128)(2,1)}, bf16[8,112,256]{2,1,0:T(8,128)(2,1)S(1)}, u32[]{:S(2)}) copy-start(bf16[8,112,256]{2,1,0:T(8,128)(2,1)S(1)} %all-to-all-done.own0) | copy-start | bytes 1376260
  24.4 14.3 %collective-permute-start.2 = (bf16[8,112,256]{2,1,0:T(8,128)(2,1)S(1)}, bf16[8,112,256]{2,1,0:T(8,128)(2,1)S(1)}, u32[]{:S(2)}, u32[]{:S(2)}) collective-permute-start(bf16[8,112,256]{2,1,0:T(8,128)(2,1)S(1)} %all-to-all-done.own0), channel_id=1, source_target_pairs={{0,12},{4,0},{8,4},{12,8},{1,13},{5,1},{9,5},{13,9},{2,14},{6,2},{... | collective-permute-start | bytes 1376264 | tf_op jit(solution)/shard_map/ppermute | solution.py:29
  26.8 22.7 %collective-permute-start.1 = (bf16[8,112,256]{2,1,0:T(8,128)(2,1)S(1)}, bf16[8,112,256]{2,1,0:T(8,128)(2,1)S(1)}, u32[]{:S(2)}, u32[]{:S(2)}) collective-permute-start(bf16[8,112,256]{2,1,0:T(8,128)(2,1)S(1)} %all-to-all-done.own0), channel_id=1, source_target_pairs={{0,8},{4,12},{8,0},{12,4},{1,9},{5,13},{9,1},{13,5},{2,10},{6,14},... | collective-permute-start | bytes 1376264 | tf_op jit(solution)/shard_map/ppermute | solution.py:29
  27.4 23.3 %collective-permute-start = (bf16[8,112,256]{2,1,0:T(8,128)(2,1)S(1)}, bf16[8,112,256]{2,1,0:T(8,128)(2,1)S(1)}, u32[]{:S(2)}, u32[]{:S(2)}) collective-permute-start(bf16[8,112,256]{2,1,0:T(8,128)(2,1)S(1)} %all-to-all-done.own0), channel_id=1, source_target_pairs={{0,4},{4,8},{8,12},{12,0},{1,5},{5,9},{9,13},{13,1},{2,6},{6,10},{... | collective-permute-start | bytes 1376264 | tf_op jit(solution)/shard_map/ppermute | solution.py:29
  29.3 23.3 %collective-permute-start.8 = (bf16[96,512]{1,0:T(8,128)(2,1)S(1)}, bf16[96,512]{1,0:T(8,128)(2,1)S(1)}, u32[]{:S(2)}, u32[]{:S(2)}) collective-permute-start(bf16[96,512]{1,0:T(8,128)(2,1)S(1)} %bitcast.60), channel_id=1, source_target_pairs={{4,0},{8,4},{12,8},{16,12},{20,16},{24,20},{28,24},{32,28},{36,32}... | collective-permute-start | bytes 294920 | tf_op jit(solution)/shard_map/ppermute | solution.py:29
  33.6 32.8 %collective-permute-start.3 = (bf16[8,112,256]{2,1,0:T(8,128)(2,1)S(1)}, bf16[8,112,256]{2,1,0:T(8,128)(2,1)S(1)}, u32[]{:S(2)}, u32[]{:S(2)}) collective-permute-start(bf16[8,112,256]{2,1,0:T(8,128)(2,1)S(1)} %all-to-all-done.own0), channel_id=1, source_target_pairs={{0,64},{64,0},{1,65},{65,1},{2,66},{66,2},{3,67},{67,3},{4,68},{68... | collective-permute-start | bytes 1376264 | tf_op jit(solution)/shard_map/ppermute | solution.py:29
  38.7 29.9 %copy-start.17 = (bf16[8,112,256]{2,1,0:T(8,128)(2,1)}, bf16[8,112,256]{2,1,0:T(8,128)(2,1)S(1)}, u32[]{:S(2)}) copy-start(bf16[8,112,256]{2,1,0:T(8,128)(2,1)S(1)} %collective-permute-done.2.own3) | copy-start | bytes 1376260
  38.7 29.8 %collective-permute-start.6 = (bf16[8,112,256]{2,1,0:T(8,128)(2,1)S(1)}, bf16[8,112,256]{2,1,0:T(8,128)(2,1)}, u32[]{:S(2)}, u32[]{:S(2)}) collective-permute-start(bf16[8,112,256]{2,1,0:T(8,128)(2,1)S(1)} %collective-permute-done.2.own3), channel_id=1, source_target_pairs={{0,64},{64,0},{1,65},{65,1},{2,66},{66,2},{3,67},{67,3},{4,68},{68... | collective-permute-start | bytes 1376264 | tf_op jit(solution)/shard_map/ppermute | solution.py:29
  49.5 19.1 %copy-start.18 = (bf16[8,112,256]{2,1,0:T(8,128)(2,1)}, bf16[8,112,256]{2,1,0:T(8,128)(2,1)S(1)}, u32[]{:S(2)}) copy-start(bf16[8,112,256]{2,1,0:T(8,128)(2,1)S(1)} %collective-permute-done.1.own2) | copy-start | bytes 1376260
  49.5 19.0 %collective-permute-start.5 = (bf16[8,112,256]{2,1,0:T(8,128)(2,1)S(1)}, bf16[8,112,256]{2,1,0:T(8,128)(2,1)}, u32[]{:S(2)}, u32[]{:S(2)}) collective-permute-start(bf16[8,112,256]{2,1,0:T(8,128)(2,1)S(1)} %collective-permute-done.1.own2), channel_id=1, source_target_pairs={{0,64},{64,0},{1,65},{65,1},{2,66},{66,2},{3,67},{67,3},{4,68},{68... | collective-permute-start | bytes 1376264 | tf_op jit(solution)/shard_map/ppermute | solution.py:29
  50.6 18.0 %copy-start.19 = (bf16[8,112,256]{2,1,0:T(8,128)(2,1)}, bf16[8,112,256]{2,1,0:T(8,128)(2,1)S(1)}, u32[]{:S(2)}) copy-start(bf16[8,112,256]{2,1,0:T(8,128)(2,1)S(1)} %collective-permute-done.own1) | copy-start | bytes 1376260
  50.6 17.9 %collective-permute-start.4 = (bf16[8,112,256]{2,1,0:T(8,128)(2,1)S(1)}, bf16[8,112,256]{2,1,0:T(8,128)(2,1)}, u32[]{:S(2)}, u32[]{:S(2)}) collective-permute-start(bf16[8,112,256]{2,1,0:T(8,128)(2,1)S(1)} %collective-permute-done.own1), channel_id=1, source_target_pairs={{0,64},{64,0},{1,65},{65,1},{2,66},{66,2},{3,67},{67,3},{4,68},{68... | collective-permute-start | bytes 1376264 | tf_op jit(solution)/shard_map/ppermute | solution.py:29
  52.6 8.3 %collective-permute-start.7 = (bf16[96,512]{1,0:T(8,128)(2,1)S(1)}, bf16[96,512]{1,0:T(8,128)(2,1)S(1)}, u32[]{:S(2)}, u32[]{:S(2)}) collective-permute-start(bf16[96,512]{1,0:T(8,128)(2,1)S(1)} %bitcast.61), channel_id=1, source_target_pairs={{0,4},{4,8},{8,12},{12,16},{16,20},{20,24},{24,28},{28,32},{32,36}... | collective-permute-start | bytes 294920 | tf_op jit(solution)/shard_map/ppermute | solution.py:29
  61.0 39.8 %copy-start.14 = (f32[96]{0:T(128)S(1)}, f32[96]{0:T(128)}, u32[]{:S(2)}) copy-start(f32[96]{0:T(128)} %param.21) | copy-start | bytes 1156
  61.0 40.5 %copy-start.15 = (f32[96]{0:T(128)S(1)}, f32[96]{0:T(128)}, u32[]{:S(2)}) copy-start(f32[96]{0:T(128)} %param.22) | copy-start | bytes 1156
  61.0 31.2 %collective-permute-start.10 = (bf16[96,2048]{1,0:T(8,128)(2,1)S(1)}, bf16[96,2048]{1,0:T(8,128)(2,1)S(1)}, u32[]{:S(2)}, u32[]{:S(2)}) collective-permute-start(bf16[96,2048]{1,0:T(8,128)(2,1)S(1)} %pad_maximum_fusion), channel_id=1, source_target_pairs={{0,128},{1,192},{2,0},{3,64},{64,129},{65,193},{66,1},{67,65},{128... | collective-permute-start | bytes 1179656 | tf_op jit(solution)/shard_map/ppermute | solution.py:29
  66.4 2.2 %copy-start.20 = (bf16[8,112,256]{2,1,0:T(8,128)(2,1)}, bf16[8,112,256]{2,1,0:T(8,128)(2,1)S(1)}, u32[]{:S(2)}) copy-start(bf16[8,112,256]{2,1,0:T(8,128)(2,1)S(1)} %collective-permute-done.3.other0) | copy-start | bytes 1376260
  66.4 31.9 %collective-permute-start.9 = (bf16[96,2048]{1,0:T(8,128)(2,1)S(1)}, bf16[96,2048]{1,0:T(8,128)(2,1)}, u32[]{:S(2)}, u32[]{:S(2)}) collective-permute-start(bf16[96,2048]{1,0:T(8,128)(2,1)S(1)} %pad_maximum_fusion), channel_id=1, source_target_pairs={{0,0},{1,64},{2,128},{3,192},{64,1},{65,65},{66,129},{67,193},{128... | collective-permute-start | bytes 1179656 | tf_op jit(solution)/shard_map/ppermute | solution.py:29
  77.8 20.5 %all-to-all-start.1 = ((f32[16,1,128]{2,1,0:T(1,128)}), f32[16,1,128]{2,1,0:T(1,128)S(1)}, u32[]{:S(2)}, u32[]{:S(2)}) async-start(f32[16,1,128]{2,1,0:T(1,128)} %get-tuple-element.30), calls=%async_computation.1 | async-start | bytes 16384 | tf_op jit(solution)/shard_map/all_to_all | solution.py:387
  87.6 10.7 %collective-permute-start.14 = (bf16[96,256]{1,0:T(8,128)(2,1)S(1)}, bf16[96,256]{1,0:T(8,128)(2,1)S(1)}, u32[]{:S(2)}, u32[]{:S(2)}) collective-permute-start(bf16[96,256]{1,0:T(8,128)(2,1)S(1)} %get-tuple-element.62), channel_id=1, source_target_pairs={{0,192},{16,224},{32,128},{48,160},{64,208},{80,240},{96,144},{112... | collective-permute-start | bytes 147464 | tf_op jit(solution)/shard_map/ppermute | solution.py:29
  91.2 7.1 %collective-permute-start.13 = (bf16[96,256]{1,0:T(8,128)(2,1)S(1)}, bf16[96,256]{1,0:T(8,128)(2,1)S(1)}, u32[]{:S(2)}, u32[]{:S(2)}) collective-permute-start(bf16[96,256]{1,0:T(8,128)(2,1)S(1)} %get-tuple-element.63), channel_id=1, source_target_pairs={{0,128},{16,160},{32,192},{48,224},{64,144},{80,176},{96,208},{112... | collective-permute-start | bytes 147464 | tf_op jit(solution)/shard_map/ppermute | solution.py:29
  92.2 6.2 %collective-permute-start.12 = (bf16[96,256]{1,0:T(8,128)(2,1)S(1)}, bf16[96,256]{1,0:T(8,128)(2,1)S(1)}, u32[]{:S(2)}, u32[]{:S(2)}) collective-permute-start(bf16[96,256]{1,0:T(8,128)(2,1)S(1)} %get-tuple-element.64), channel_id=1, source_target_pairs={{0,64},{16,96},{32,0},{48,32},{64,80},{80,112},{96,16},{112,48},{1... | collective-permute-start | bytes 147464 | tf_op jit(solution)/shard_map/ppermute | solution.py:29
  92.2 34.1 %copy-start.21 = (bf16[96,2048]{1,0:T(8,128)(2,1)}, bf16[96,2048]{1,0:T(8,128)(2,1)S(1)}, u32[]{:S(2)}) copy-start(bf16[96,2048]{1,0:T(8,128)(2,1)S(1)} %collective-permute-done.10.near1) | copy-start | bytes 1179652
  92.2 6.6 %collective-permute-start.11 = (bf16[96,256]{1,0:T(8,128)(2,1)S(1)}, bf16[96,256]{1,0:T(8,128)(2,1)S(1)}, u32[]{:S(2)}, u32[]{:S(2)}) collective-permute-start(bf16[96,256]{1,0:T(8,128)(2,1)S(1)} %get-tuple-element.65), channel_id=1, source_target_pairs={{0,0},{16,32},{32,64},{48,96},{64,16},{80,48},{96,80},{112,112},{1... | collective-permute-start | bytes 147464 | tf_op jit(solution)/shard_map/ppermute | solution.py:29
  98.3 6.7 %copy-start.8 = (bf16[96,256]{1,0:T(8,128)(2,1)}, bf16[96,256]{1,0:T(8,128)(2,1)S(1)}, u32[]{:S(2)}) copy-start(bf16[96,256]{1,0:T(8,128)(2,1)S(1)} %collective-permute-done.14.piece3) | copy-start | bytes 147460
  98.3 6.6 %copy-start.9 = (bf16[96,256]{1,0:T(8,128)(2,1)}, bf16[96,256]{1,0:T(8,128)(2,1)S(1)}, u32[]{:S(2)}) copy-start(bf16[96,256]{1,0:T(8,128)(2,1)S(1)} %collective-permute-done.13.piece2) | copy-start | bytes 147460
  98.4 6.6 %copy-start.10 = (bf16[96,256]{1,0:T(8,128)(2,1)}, bf16[96,256]{1,0:T(8,128)(2,1)S(1)}, u32[]{:S(2)}) copy-start(bf16[96,256]{1,0:T(8,128)(2,1)S(1)} %collective-permute-done.12.piece1) | copy-start | bytes 147460
  98.8 6.2 %copy-start.11 = (bf16[96,256]{1,0:T(8,128)(2,1)}, bf16[96,256]{1,0:T(8,128)(2,1)S(1)}, u32[]{:S(2)}) copy-start(bf16[96,256]{1,0:T(8,128)(2,1)S(1)} %collective-permute-done.11.piece0) | copy-start | bytes 147460
  98.8 5.6 %collective-permute-start.17 = (f32[1,128]{1,0:T(1,128)S(1)}, f32[1,128]{1,0:T(1,128)S(1)}, u32[]{:S(2)}, u32[]{:S(2)}) collective-permute-start(f32[1,128]{1,0:T(1,128)S(1)} %bitcast.65), channel_id=1, source_target_pairs={{0,12},{4,0},{8,4},{12,8},{1,13},{5,1},{9,5},{13,9},{2,14},{6,2},{... | collective-permute-start | bytes 1544 | tf_op jit(solution)/shard_map/ppermute | solution.py:29
  100.2 4.1 %collective-permute-start.16 = (f32[1,128]{1,0:T(1,128)S(1)}, f32[1,128]{1,0:T(1,128)S(1)}, u32[]{:S(2)}, u32[]{:S(2)}) collective-permute-start(f32[1,128]{1,0:T(1,128)S(1)} %bitcast.66), channel_id=1, source_target_pairs={{0,8},{4,12},{8,0},{12,4},{1,9},{5,13},{9,1},{13,5},{2,10},{6,14},... | collective-permute-start | bytes 1544 | tf_op jit(solution)/shard_map/ppermute | solution.py:29
  100.3 4.1 %collective-permute-start.15 = (f32[1,128]{1,0:T(1,128)S(1)}, f32[1,128]{1,0:T(1,128)S(1)}, u32[]{:S(2)}, u32[]{:S(2)}) collective-permute-start(f32[1,128]{1,0:T(1,128)S(1)} %bitcast.67), channel_id=1, source_target_pairs={{0,4},{4,8},{8,12},{12,0},{1,5},{5,9},{9,13},{13,1},{2,6},{6,10},{... | collective-permute-start | bytes 1544 | tf_op jit(solution)/shard_map/ppermute | solution.py:29
  102.3 24.0 %collective-permute-start.23 = (bf16[96,2048]{1,0:T(8,128)(2,1)}, bf16[96,2048]{1,0:T(8,128)(2,1)S(1)}, u32[]{:S(2)}, u32[]{:S(2)}) collective-permute-start(bf16[96,2048]{1,0:T(8,128)(2,1)} %collective-permute-done.9.near0), channel_id=1, source_target_pairs={{0,64},{64,0},{1,65},{65,1},{2,66},{66,2},{3,67},{67,3},{4,68},{68... | collective-permute-start | bytes 1179656 | tf_op jit(solution)/shard_map/ppermute | solution.py:29
  104.4 22.0 %collective-permute-start.24 = (bf16[96,2048]{1,0:T(8,128)(2,1)S(1)}, bf16[96,2048]{1,0:T(8,128)(2,1)S(1)}, u32[]{:S(2)}, u32[]{:S(2)}) collective-permute-start(bf16[96,2048]{1,0:T(8,128)(2,1)S(1)} %collective-permute-done.10.near1), channel_id=1, source_target_pairs={{0,64},{64,0},{1,65},{65,1},{2,66},{66,2},{3,67},{67,3},{4,68},{68... | collective-permute-start | bytes 1179656 | tf_op jit(solution)/shard_map/ppermute | solution.py:29
  109.1 8.4 %collective-permute-start.21 = (bf16[96,512]{1,0:T(8,128)(2,1)S(1)}, bf16[96,512]{1,0:T(8,128)(2,1)}, u32[]{:S(2)}, u32[]{:S(2)}) collective-permute-start(bf16[96,512]{1,0:T(8,128)(2,1)S(1)} %bitcast.63), channel_id=1, source_target_pairs={{0,4},{4,8},{8,12},{12,16},{16,20},{20,24},{24,28},{28,32},{32,36}... | collective-permute-start | bytes 294920 | tf_op jit(solution)/shard_map/ppermute | solution.py:29
  113.3 5.8 %collective-permute-start.22 = (bf16[96,512]{1,0:T(8,128)(2,1)S(1)}, bf16[96,512]{1,0:T(8,128)(2,1)S(1)}, u32[]{:S(2)}, u32[]{:S(2)}) collective-permute-start(bf16[96,512]{1,0:T(8,128)(2,1)S(1)} %bitcast.62), channel_id=1, source_target_pairs={{4,0},{8,4},{12,8},{16,12},{20,16},{24,20},{28,24},{32,28},{36,32}... | collective-permute-start | bytes 294920 | tf_op jit(solution)/shard_map/ppermute | solution.py:29
  116.5 4.8 %collective-permute-start.20 = (bf16[96,1024]{1,0:T(8,128)(2,1)}, bf16[96,1024]{1,0:T(8,128)(2,1)S(1)}, u32[]{:S(2)}, u32[]{:S(2)}) collective-permute-start(bf16[96,1024]{1,0:T(8,128)(2,1)} %get-tuple-element.40.clip0.clip), channel_id=1, source_target_pairs={{0,3},{1,0},{2,1},{3,2},{4,7},{5,4},{6,5},{7,6},{8,11},{9,8},{10,9... | collective-permute-start | bytes 589832 | tf_op jit(solution)/shard_map/ppermute | solution.py:29
  117.5 6.3 %collective-permute-start.19 = (bf16[96,1024]{1,0:T(8,128)(2,1)}, bf16[96,1024]{1,0:T(8,128)(2,1)S(1)}, u32[]{:S(2)}, u32[]{:S(2)}) collective-permute-start(bf16[96,1024]{1,0:T(8,128)(2,1)} %get-tuple-element.40.clip0.clip), channel_id=1, source_target_pairs={{0,2},{1,3},{2,0},{3,1},{4,6},{5,7},{6,4},{7,5},{8,10},{9,11},{10,... | collective-permute-start | bytes 589832 | tf_op jit(solution)/shard_map/ppermute | solution.py:29
  119.1 7.2 %copy-start.27 = (bf16[96,512]{1,0:T(8,128)(2,1)}, bf16[96,512]{1,0:T(8,128)(2,1)S(1)}, u32[]{:S(2)}) copy-start(bf16[96,512]{1,0:T(8,128)(2,1)S(1)} %collective-permute-done.22.after) | copy-start | bytes 294916
  119.1 7.2 %collective-permute-start.18 = (bf16[96,1024]{1,0:T(8,128)(2,1)}, bf16[96,1024]{1,0:T(8,128)(2,1)S(1)}, u32[]{:S(2)}, u32[]{:S(2)}) collective-permute-start(bf16[96,1024]{1,0:T(8,128)(2,1)} %get-tuple-element.40.clip0.clip), channel_id=1, source_target_pairs={{0,1},{1,2},{2,3},{3,0},{4,5},{5,6},{6,7},{7,4},{8,9},{9,10},{10,1... | collective-permute-start | bytes 589832 | tf_op jit(solution)/shard_map/ppermute | solution.py:29
  121.3 5.0 %copy-start.24 = (bf16[96,1024]{1,0:T(8,128)(2,1)}, bf16[96,1024]{1,0:T(8,128)(2,1)S(1)}, u32[]{:S(2)}) copy-start(bf16[96,1024]{1,0:T(8,128)(2,1)S(1)} %collective-permute-done.20.clip3) | copy-start | bytes 589828
  123.8 2.5 %copy-start.25 = (bf16[96,1024]{1,0:T(8,128)(2,1)}, bf16[96,1024]{1,0:T(8,128)(2,1)S(1)}, u32[]{:S(2)}) copy-start(bf16[96,1024]{1,0:T(8,128)(2,1)S(1)} %collective-permute-done.19.clip2) | copy-start | bytes 589828
  126.3 0.7 copy-start.26
  126.3 0.8 copy-start.22
  127.1 0.7 copy-start.23
  127.9 13.3 %copy-start.1 = (bf16[3,3,3,96,384]{4,3,2,1,0:T(8,128)(2,1)S(1)}, bf16[3,3,3,96,384]{4,3,2,1,0:T(8,128)(2,1)}, u32[]{:S(2)}) copy-start(bf16[3,3,3,96,384]{4,3,2,1,0:T(8,128)(2,1)} %param.23) | copy-start | bytes 5971972
  133.3 21.8 %all-to-all-start.2 = ((bf16[16,8,16,128]{3,2,1,0:T(8,128)(2,1)}), bf16[16,8,16,128]{3,2,1,0:T(8,128)(2,1)S(1)}, u32[]{:S(2)}, u32[]{:S(2)}) async-start(bf16[16,8,16,128]{3,2,1,0:T(8,128)(2,1)} %bitcast.55), calls=%async_computation.2 | async-start | bytes 1048576 | tf_op jit(solution)/shard_map/all_to_all | solution.py:431
  149.0 4.3 %collective-permute-start.25 = (bf16[2,96,1024]{2,1,0:T(8,128)(2,1)}, bf16[2,96,1024]{2,1,0:T(8,128)(2,1)S(1)}, u32[]{:S(2)}, u32[]{:S(2)}) collective-permute-start(bf16[2,96,1024]{2,1,0:T(8,128)(2,1)} %get-tuple-element.51), channel_id=1, source_target_pairs={{0,64},{64,0},{1,65},{65,1},{2,66},{66,2},{3,67},{67,3},{4,68},{68... | collective-permute-start | bytes 1179656 | tf_op jit(solution)/shard_map/ppermute | solution.py:29
  154.4 35.8 %copy-start.7 = (bf16[96,1024]{1,0:T(8,128)(2,1)S(1)}, bf16[96,1024]{1,0:T(8,128)(2,1)}, u32[]{:S(2)}) copy-start(bf16[96,1024]{1,0:T(8,128)(2,1)} %get-tuple-element.38) | copy-start | bytes 589828
  154.4 35.8 %copy-start.16 = (f32[96]{0:T(128)S(1)}, f32[96]{0:T(128)}, u32[]{:S(2)}) copy-start(f32[96]{0:T(128)} %param.24) | copy-start | bytes 1156
  176.0 31.1 %copy-start = (bf16[16,8,16,128]{3,2,1,0:T(8,128)(2,1)}, bf16[16,8,16,128]{3,2,1,0:T(8,128)(2,1)S(1)}, u32[]{:S(2)}) copy-start(bf16[16,8,16,128]{3,2,1,0:T(8,128)(2,1)S(1)} %all_to_all.20) | copy-start | bytes 1572868
  176.0 14.2 %collective-permute-start.26 = (bf16[96,1024]{1,0:T(8,128)(2,1)S(1)}, bf16[96,1024]{1,0:T(8,128)(2,1)S(1)}, u32[]{:S(2)}, u32[]{:S(2)}) collective-permute-start(bf16[96,1024]{1,0:T(8,128)(2,1)S(1)} %fusion.1), channel_id=1, source_target_pairs={{0,128},{128,0},{1,129},{129,1},{2,130},{130,2},{3,131},{131,3},{4... | collective-permute-start | bytes 589832 | tf_op jit(solution)/shard_map/ppermute | solution.py:29
  180.6 12.0 %collective-permute-start.29 = (bf16[128,16,128]{2,1,0:T(8,128)(2,1)S(1)}, bf16[128,16,128]{2,1,0:T(8,128)(2,1)S(1)}, u32[]{:S(2)}, u32[]{:S(2)}) collective-permute-start(bf16[128,16,128]{2,1,0:T(8,128)(2,1)S(1)} %bitcast.50), channel_id=1, source_target_pairs={{0,3},{1,0},{2,1},{3,2},{4,7},{5,4},{6,5},{7,6},{8,11},{9,8},{10,9... | collective-permute-start | bytes 1572872 | tf_op jit(solution)/shard_map/ppermute | solution.py:29
  180.6 13.4 %collective-permute-start.28 = (bf16[128,16,128]{2,1,0:T(8,128)(2,1)S(1)}, bf16[128,16,128]{2,1,0:T(8,128)(2,1)S(1)}, u32[]{:S(2)}, u32[]{:S(2)}) collective-permute-start(bf16[128,16,128]{2,1,0:T(8,128)(2,1)S(1)} %bitcast.51), channel_id=1, source_target_pairs={{0,2},{1,3},{2,0},{3,1},{4,6},{5,7},{6,4},{7,5},{8,10},{9,11},{10,... | collective-permute-start | bytes 1572872 | tf_op jit(solution)/shard_map/ppermute | solution.py:29
  181.4 25.8 %collective-permute-start.27 = (bf16[128,16,128]{2,1,0:T(8,128)(2,1)S(1)}, bf16[128,16,128]{2,1,0:T(8,128)(2,1)S(1)}, u32[]{:S(2)}, u32[]{:S(2)}) collective-permute-start(bf16[128,16,128]{2,1,0:T(8,128)(2,1)S(1)} %bitcast.52), channel_id=1, source_target_pairs={{0,1},{1,2},{2,3},{3,0},{4,5},{5,6},{6,7},{7,4},{8,9},{9,10},{10,1... | collective-permute-start | bytes 1572872 | tf_op jit(solution)/shard_map/ppermute | solution.py:29
  192.6 14.6 %copy-start.3 = (bf16[128,16,128]{2,1,0:T(8,128)(2,1)}, bf16[128,16,128]{2,1,0:T(8,128)(2,1)S(1)}, u32[]{:S(2)}) copy-start(bf16[128,16,128]{2,1,0:T(8,128)(2,1)S(1)} %collective-permute-done.29.table3) | copy-start | bytes 1572868
  194.0 13.2 %copy-start.4 = (bf16[128,16,128]{2,1,0:T(8,128)(2,1)}, bf16[128,16,128]{2,1,0:T(8,128)(2,1)S(1)}, u32[]{:S(2)}) copy-start(bf16[128,16,128]{2,1,0:T(8,128)(2,1)S(1)} %collective-permute-done.28.table2) | copy-start | bytes 1572868
  207.2 0.8 copy-start.5

commit v3 on v2

--- a/solution.py
+++ b/solution.py
@@ -103,10 +103,14 @@
     qkv_bias,
     out_weight,
     out_bias,
-    hidden,
+    piece0,
+    piece1,
+    piece2,
+    piece3,
     sums,
     tokens,
     scores,
+    hidden,
 ):
     co, slot, valid, frame = at[0], at[1], at[2], at[3]
     count = valid.astype(F32) * (12 * 32 * 128)
@@ -177,6 +181,8 @@
             rows = pl.ds(pl.multiple_of((2 * zh + which) * 96, 32), 96)
             raw = part[zh * 4 + slot, :96].astype(F32)
             hidden[rows, :] = (raw + hidden[rows, :].astype(F32)).astype(BF)
+    for k, piece in enumerate((piece0, piece1, piece2, piece3)):
+        piece[...] = hidden[pl.ds(pl.multiple_of((frame ^ k) * 96, 32), 96), :]
     data = jnp.where(frame < valid, hidden[...].astype(F32), 0.0)
     first = jnp.sum(data, axis=1, keepdims=True)
     second = jnp.sum(data * data, axis=1, keepdims=True)
@@ -184,24 +190,32 @@
     lane = lax.broadcasted_iota(jnp.int32, (384, 128), 1)
     table = jnp.where(row == lane, first, jnp.where(row + 32 == lane, second, 0.0))
     table = jnp.sum(table, axis=0, keepdims=True)
+    table = table + jnp.where(lane[0:1] == 64, valid.astype(F32) / 64.0, 0.0)
     sums[...] = jnp.broadcast_to(table[None], sums.shape)
 
 
-def gate_kernel(at, packed, piece0, piece1, piece2, piece3, gain, shift, gated, hidden, held):
-    ch, valid = at[0], at[1]
-    count = valid.astype(F32) * (12 * 32 * 128)
-    table = jnp.sum(packed[...], axis=0, keepdims=True)
+def arrange_kernel(at, piece0, piece1, piece2, piece3, whole, last, leading, held):
+    for k, piece in enumerate((piece0, piece1, piece2, piece3)):
+        held[at[0] ^ k] = piece[...]
+    for f in range(4):
+        data = held[f]
+        whole[:, f * 256 : f * 256 + 256] = data
+        leading[:, f * 128 : f * 128 + 128] = data[:, :128]
+        last[:, f * 128 : f * 128 + 128] = data[:, 128:]
+
+
+def clip_columns(table, ch):
     group = lax.broadcasted_iota(jnp.int32, (96, 128), 0) // 12 + ch * 8
+    count = column(table, 64) * (12 * 32 * 128)
     mean = column(table, group) / count
     var = column(table, group + 32) / count - mean * mean
-    scale = lax.rsqrt(var + EPS)
-    for k, piece in enumerate((piece0, piece1, piece2, piece3)):
-        held[ch ^ k] = piece[...]
-    for f in range(4):
-        data = held[f]
-        hidden[:, f * 256 : f * 256 + 256] = data
-        u = (data.astype(F32) - mean) * scale * gain[...] + shift[...]
-        gated[:, f * 256 : f * 256 + 256] = (u / (1.0 + jnp.exp(-u))).astype(BF)
+    return mean, lax.rsqrt(var + EPS)
+
+
+def gate(data, columns, gain, shift):
+    mean, scale = columns
+    u = (data.astype(F32) - mean) * scale * gain[...] + shift[...]
+    return u / (1.0 + jnp.exp(-u))
 
 
 def shifted(g, kx):
@@ -214,20 +228,38 @@
 
 
 def grad_kernel(
-    at, clip0, clip1, clip2, clip3, near0, near1, far0, far1, out, gs, cs, cot, before, after
+    at,
+    table,
+    clip0,
+    clip1,
+    clip2,
+    clip3,
+    near0,
+    near1,
+    far0,
+    far1,
+    gain,
+    shift,
+    out,
+    gs,
+    cs,
+    cot,
+    before,
+    after,
 ):
     for i, part in enumerate((near0, near1, far0, far1)):
         cot[i] = part[:, :1024]
         before[i] = part[:, 1024:1536]
         after[i] = part[:, 1536:]
     gs[864:, :] = jnp.zeros((32, 4096), BF)
-    for s, gated in enumerate((clip0, clip1, clip2, clip3)):
+    for s, hidden in enumerate((clip0, clip1, clip2, clip3)):
+        columns = clip_columns(table[s : s + 1], at[3])
         for kt in range(2):
             gs[kt * 288 : kt * 288 + 288, s * 1024 : s * 1024 + (2 - kt) * 256] = jnp.zeros(
                 (288, (2 - kt) * 256), BF
             )
         for b in range(8):
-            g = gated[:, b * 128 : b * 128 + 128].astype(F32)
+            g = gate(hidden[:, b * 128 : b * 128 + 128], columns, gain, shift)
             for kx in range(3):
                 piece = shifted(g, kx).astype(BF)
                 for kt in range(3):
@@ -244,12 +276,12 @@
             cs[0:96, to + 128 : to + 256] = after[k, :, f * 128 : f * 128 + 128]
             cs[192:288, to : to + 128] = before[k, :, f * 128 : f * 128 + 128]
             cs[192:288, to + 128 : to + 256] = cot[k, :, f * 256 : f * 256 + 128]
-    table = lax.dot_general(
+    grads = lax.dot_general(
         cs[...], gs[...], (((1,), (1,)), ((), ())), preferred_element_type=F32
     ).astype(BF)
     for t in range(18):
         for l in range(7):
-            out[t * 7 + l] = table[t * 16 : t * 16 + 16, l * 128 : l * 128 + 128]
+            out[t * 7 + l] = grads[t * 16 : t * 16 + 16, l * 128 : l * 128 + 128]
     out[126:] = jnp.zeros((2, 16, 128), BF)
 
 
@@ -271,8 +303,9 @@
                 lane = end
 
 
-def conv_kernel(at, clip, before, after, weight, keep, send, stack, held):
+def conv_kernel(at, table, clip, before, after, weight, gain, shift, keep, send, stack, held):
     stack[:, :512] = jnp.zeros((864, 512), BF)
+    columns = clip_columns(table[0:1], at[1])
     for f in range(4):
         for p in range(4):
             if p == 0:
@@ -281,7 +314,11 @@
                 g = after[:, f * 128 : f * 128 + 128]
             else:
                 g = clip[:, f * 256 + p * 128 - 128 : f * 256 + p * 128]
-            g = g.astype(F32)
+            g = gate(g, columns, gain, shift)
+            if p == 0:
+                g = jnp.where(at[2] > 0, g, 0.0)
+            elif p == 3:
+                g = jnp.where(at[2] < 15, g, 0.0)
             for kx in range(3):
                 piece = shifted(g, kx).astype(BF)
                 for ky in range(3):
@@ -335,13 +372,14 @@
         name="pack",
     )(frame_count, features.reshape(96, 1024), norm1_gain[None], norm1_shift[None])
     mine = lax.all_to_all(by_frame, ("zh", "zl"), 0, 0, tiled=True)
-    parts = ring(mine, "x")
-    others = [permute(p, ("co",), lambda i: (1 - i,)) for p in parts]
-
     masked = (cotangent.reshape(96, 4, 256) * mask.astype(BF)[None, :, None]).reshape(96, 1024)
     lines = masked.reshape(96, 4, 2, 128)
     before, after = halo(lines[:, :, 1].reshape(96, 512), lines[:, :, 0].reshape(96, 512))
     bundle = jnp.concatenate([masked, before, after], axis=1)
+    mine, bundle = lax.optimization_barrier((mine, bundle))
+    parts = ring(mine, "x")
+    others = [permute(p, ("co",), lambda i: (1 - i,)) for p in parts]
+
     bundle, _ = lax.optimization_barrier((bundle, parts[1]))
     near = [
         permute(
@@ -352,15 +390,17 @@
 
     frame = 2 * zh + zl // 2
     at = jnp.stack([co, 2 * (zl % 2) + co, valid, frame]).astype(jnp.int32)
-    hidden_q, packed = pl.pallas_call(
+    *pieces, packed = pl.pallas_call(
         attend_kernel,
-        out_shape=(
-            jax.ShapeDtypeStruct((384, 256), BF),
-            jax.ShapeDtypeStruct((16, 1, 128), F32),
-        ),
+        out_shape=(jax.ShapeDtypeStruct((96, 256), BF),) * 4
+        + (jax.ShapeDtypeStruct((64, 1, 128), F32),),
         in_specs=[scalars] + [whole] * 12,
-        out_specs=(whole, whole),
-        scratch_shapes=[pltpu.VMEM((384, 4096), BF), pltpu.VMEM((256, 4096), F32)],
+        out_specs=(whole,) * 5,
+        scratch_shapes=[
+            pltpu.VMEM((384, 4096), BF),
+            pltpu.VMEM((256, 4096), F32),
+            pltpu.VMEM((384, 256), BF),
+        ],
         compiler_params=params,
         cost_estimate=cost(4 * 10**9, 20 * 10**6),
         name="attention",
@@ -374,46 +414,43 @@
         out_bias[:, None],
     )
 
-    pieces = []
+    near, pieces = lax.optimization_barrier((near, pieces))
+    far = [permute(v, ("co",), lambda i: (1 - i,)) for v in near]
+
     for k in range(4):
-        piece = lax.dynamic_slice(hidden_q, ((frame ^ k) * 96, 0), (96, 256))
 
         def to_channels(zh, co, zl, k=k):
             c = (2 * zh + zl // 2) ^ k
             return (c // 2, c % 2, 2 * (zl % 2) + co)
 
-        pieces.append(permute(piece, ("zh", "co", "zl"), to_channels))
-
-    packed = lax.all_to_all(packed, ("zh", "co", "zl"), 0, 0, tiled=True)
+        pieces[k] = permute(pieces[k], ("zh", "co", "zl"), to_channels)
+    packed = lax.all_to_all(packed, ("zh", "co", "zl", "x"), 0, 0, tiled=True)
     packed = jnp.sum(packed, axis=0)
-    packed, near, pieces = lax.optimization_barrier((packed, near, pieces))
-    packed = jnp.concatenate(ring(packed, "x"), axis=0)
-    far = [permute(v, ("co",), lambda i: (1 - i,)) for v in near]
-    gated, hidden = pl.pallas_call(
-        gate_kernel,
-        out_shape=(jax.ShapeDtypeStruct((96, 1024), BF), jax.ShapeDtypeStruct((96, 1024), BF)),
-        in_specs=[scalars] + [whole] * 7,
-        out_specs=(whole, whole),
+    packed, far, pieces = lax.optimization_barrier((packed, far, pieces))
+    hidden, last, leading = pl.pallas_call(
+        arrange_kernel,
+        out_shape=(
+            jax.ShapeDtypeStruct((96, 1024), BF),
+            jax.ShapeDtypeStruct((96, 512), BF),
+            jax.ShapeDtypeStruct((96, 512), BF),
+        ),
+        in_specs=[scalars] + [whole] * 4,
+        out_specs=(whole,) * 3,
         scratch_shapes=[pltpu.VMEM((4, 96, 256), BF)],
         compiler_params=params,
-        cost_estimate=cost(10**7, 10**6),
-        name="gate",
-    )(
-        jnp.stack([ch, valid]).astype(jnp.int32),
-        packed,
-        *pieces,
-        norm2_gain[:, None],
-        norm2_shift[:, None],
-    )
-
-    rows = gated.reshape(96, 4, 2, 128)
-    above, below = halo(rows[:, :, 1].reshape(96, 512), rows[:, :, 0].reshape(96, 512))
-    clips = ring(gated, "y")
-    clips, above, below = lax.optimization_barrier((clips, above, below))
+        cost_estimate=cost(10**6, 10**6),
+        name="arrange",
+    )(ch.astype(jnp.int32)[None], *pieces)
+    packed, hidden = lax.optimization_barrier((packed, hidden))
+    clips = ring(hidden, "y")
+
+    table2 = jnp.concatenate(ring(packed, "y"), axis=0)
+    gain, shift = norm2_gain[:, None], norm2_shift[:, None]
+
     table = pl.pallas_call(
         grad_kernel,
         out_shape=jax.ShapeDtypeStruct((128, 16, 128), BF),
-        in_specs=[scalars] + [whole] * 8,
+        in_specs=[scalars] + [whole] * 11,
         out_specs=whole,
         scratch_shapes=[
             pltpu.VMEM((896, 4096), BF),
@@ -425,20 +462,30 @@
         compiler_params=params,
         cost_estimate=cost(4 * 10**9, 20 * 10**6),
         name="weight_grad",
-    )(jnp.stack([y, co, zh]).astype(jnp.int32), *clips, *near, *far)
-    table, conv_weight = lax.optimization_barrier((table, conv_weight))
+    )(jnp.stack([y, co, zh, ch]).astype(jnp.int32), table2, *clips, *near, *far, gain, shift)
+    table, conv_weight, last, leading = lax.optimization_barrier((table, conv_weight, last, leading))
+    above, below = halo(last, leading)
     kernels = conv_weight.transpose(0, 4, 1, 2, 3).reshape(3, 384, 864)
     shares = lax.all_to_all(table.reshape(16, 8, 16, 128), ("zl", "x"), 0, 0, tiled=True)
     keep, send = pl.pallas_call(
         conv_kernel,
         out_shape=(jax.ShapeDtypeStruct((2, 96, 1024), BF),) * 2,
-        in_specs=[scalars] + [whole] * 4,
+        in_specs=[scalars] + [whole] * 7,
         out_specs=(whole, whole),
         scratch_shapes=[pltpu.VMEM((864, 1536), BF), pltpu.VMEM((4, 96, 1024), BF)],
         compiler_params=params,
         cost_estimate=cost(3 * 10**9, 12 * 10**6),
         name="convolution",
-    )(co.astype(jnp.int32)[None], clips[0], above, below, kernels)
+    )(
+        jnp.stack([co, ch, zl * 4 + x]).astype(jnp.int32),
+        table2,
+        clips[0],
+        above,
+        below,
+        kernels,
+        gain,
+        shift,
+    )
     send = permute(send, ("co",), lambda i: (1 - i,))
     summed = keep.astype(F32) + send.astype(F32)
     near = lax.dynamic_index_in_dim(summed, zh, 0, keepdims=False)

time: 214 us -> 216 us (level)
  waiting for transfers between devices: 52.5 us -> 55 us
    ppermute x30, waiting for transfers between devices: 40 us -> 53.2 us  [permute(): return lax.ppermute(value, axes, pairs)]
    all_to_all x1, waiting for transfers between devices: 11.9 us -> 0.01 us  [body(): mine = lax.all_to_all(by_frame, ('zh', 'zl'), 0, 0, tiled=True)]
    all_to_all x1, starting transfers between devices: 8.99 us -> 16.7 us  [body(): packed = lax.all_to_all(packed, ('zh', 'co', 'zl', 'x'), 0, 0, tiled=True)]
    ppermute x30, starting transfers between devices: 65.6 us -> 58.6 us  [permute(): return lax.ppermute(value, axes, pairs)]
    all_to_all x1, starting transfers between devices: 7.9 us -> 5.31 us  [body(): lax.all_to_all(table.reshape(16, 8, 16, 128), ('zl', 'x'), 0, 0, tiled=True)]
    unnamed x62, local copies, waits for them, and re-layouts: 2.59 us -> 4.93 us
  transfers between devices with their start and end apart: 33 -> 33, of which waited for: 14 -> 14; matrix products, arithmetic and copies ran while one was open for 7% -> 6% of each run, Pallas kernels for 8% -> 7%
where the time goes in v3:
time: 216 us; the launch traced here: 214 us
  starting transfers between devices  88.3 us (41%)
  waiting for transfers between devices  55 us (25%)
  Pallas kernels  29.4 us (14%)
  blocking collectives  21.4 us (10%)
  local copies, waits for them, and re-layouts  13.6 us (6%)
  other arithmetic  5.03 us (2%)
    ppermute x30, starting transfers between devices, permute(): return lax.ppermute(value, axes, pairs)  58.6 us
    ppermute x30, waiting for transfers between devices, permute(): return lax.ppermute(value, axes, pairs)  53.2 us
    all_to_all x1, blocking collectives, spread(): return lax.all_to_all(copies, axes, 0, 0, tiled=True)  21.4 us
    all_to_all x1, starting transfers between devices, body(): packed = lax.all_to_all(packed, ('zh', 'co', 'zl', 'x'), 0, 0, tiled=True)  16.7 us
    pallas_call x1, Pallas kernels, body(): pl.pallas_call(attend_kernel, out_shape=(jax.ShapeDtypeStruct((96, 256),...  9.13 us
    all_to_all x1, starting transfers between devices, body(): mine = lax.all_to_all(by_frame, ('zh', 'zl'), 0, 0, tiled=True)  7.69 us
    pallas_call x1, Pallas kernels, body(): pl.pallas_call(grad_kernel, out_shape=jax.ShapeDtypeStruct((128, 16, 128)...  6.5 us
    pallas_call x1, Pallas kernels, body(): pl.pallas_call(conv_kernel, out_shape=(jax.ShapeDtypeStruct((2, 96, 1024)...  5.84 us
  transfers between devices with their start and end apart: 33, of which 14 were waited for; matrix products, arithmetic and copies ran while one was open for 6% of the time, Pallas kernels for 7%

profile of v3, /device:TPU:65, one launch (start us, length us, event | category | flops | bytes accessed | tf_op | source)
XLA Modules:
  0.0 214.4 jit_solution(15265716774308577696)
XLA Ops:
  1.3 1.7 reshape.57.frames
  3.0 1.9 pack.1
  4.9 7.7 %all-to-all-start = ((bf16[8,112,256]{2,1,0:T(8,128)(2,1)}), bf16[8,112,256]{2,1,0:T(8,128)(2,1)S(1)}, u32[]{:S(2)}, u32[]{:S(2)}) async-start(bf16[8,112,256]{2,1,0:T(8,128)(2,1)} %pack.1), calls=%async_computation | async-start | bytes 917504 | tf_op jit(solution)/shard_map/all_to_all | solution.py:374
  12.9 1.1 slice_reduce_fusion.1
  14.0 4.4 %collective-permute-start.1 = (bf16[96,512]{1,0:T(8,128)(2,1)S(1)}, bf16[96,512]{1,0:T(8,128)(2,1)S(1)}, u32[]{:S(2)}, u32[]{:S(2)}) collective-permute-start(bf16[96,512]{1,0:T(8,128)(2,1)S(1)} %bitcast.51), channel_id=1, source_target_pairs={{4,0},{8,4},{12,8},{16,12},{20,16},{24,20},{28,24},{32,28},{36,32}... | collective-permute-start | bytes 294920 | tf_op jit(solution)/shard_map/ppermute | solution.py:29
  18.4 1.9 collective-permute-start
  20.6 2.2 %collective-permute-done.1 = bf16[96,512]{1,0:T(8,128)(2,1)S(1)} collective-permute-done((bf16[96,512]{1,0:T(8,128)(2,1)S(1)}, bf16[96,512]{1,0:T(8,128)(2,1)S(1)}, u32[]{:S(2)}, u32[]{:S(2)}) %collective-permute-start.1) | collective-permute-done | bytes 98336 | tf_op jit(solution)/shard_map/ppermute | solution.py:29
  22.8 3.6 %collective-permute-done = bf16[96,512]{1,0:T(8,128)(2,1)S(1)} collective-permute-done((bf16[96,512]{1,0:T(8,128)(2,1)S(1)}, bf16[96,512]{1,0:T(8,128)(2,1)S(1)}, u32[]{:S(2)}, u32[]{:S(2)}) %collective-permute-start) | collective-permute-done | bytes 98336 | tf_op jit(solution)/shard_map/ppermute | solution.py:29
  26.5 1.9 collective-permute-start.4
  28.4 0.7 collective-permute-start.2
  29.1 2.2 %collective-permute-start.5 = (bf16[8,112,256]{2,1,0:T(8,128)(2,1)S(1)}, bf16[8,112,256]{2,1,0:T(8,128)(2,1)S(1)}, u32[]{:S(2)}, u32[]{:S(2)}) collective-permute-start(bf16[8,112,256]{2,1,0:T(8,128)(2,1)S(1)} %all-to-all-done.own0), channel_id=1, source_target_pairs={{0,64},{64,0},{1,65},{65,1},{2,66},{66,2},{3,67},{67,3},{4,68},{68... | collective-permute-start | bytes 1376264 | tf_op jit(solution)/shard_map/ppermute | solution.py:29
  31.3 7.6 %collective-permute-done.4.own3 = bf16[8,112,256]{2,1,0:T(8,128)(2,1)S(1)} collective-permute-done((bf16[8,112,256]{2,1,0:T(8,128)(2,1)S(1)}, bf16[8,112,256]{2,1,0:T(8,128)(2,1)S(1)}, u32[]{:S(2)}, u32[]{:S(2)}) %collective-permute-start.4) | collective-permute-done | bytes 458784 | tf_op jit(solution)/shard_map/ppermute | solution.py:29
  38.9 10.1 %collective-permute-start.8 = (bf16[8,112,256]{2,1,0:T(8,128)(2,1)S(1)}, bf16[8,112,256]{2,1,0:T(8,128)(2,1)S(1)}, u32[]{:S(2)}, u32[]{:S(2)}) collective-permute-start(bf16[8,112,256]{2,1,0:T(8,128)(2,1)S(1)} %collective-permute-done.4.own3), channel_id=1, source_target_pairs={{0,64},{64,0},{1,65},{65,1},{2,66},{66,2},{3,67},{67,3},{4,68},{68... | collective-permute-start | bytes 1376264 | tf_op jit(solution)/shard_map/ppermute | solution.py:29
  49.1 2.4 %collective-permute-done.2.own1 = bf16[8,112,256]{2,1,0:T(8,128)(2,1)S(1)} collective-permute-done((bf16[8,112,256]{2,1,0:T(8,128)(2,1)S(1)}, bf16[8,112,256]{2,1,0:T(8,128)(2,1)S(1)}, u32[]{:S(2)}, u32[]{:S(2)}) %collective-permute-start.2) | collective-permute-done | bytes 458784 | tf_op jit(solution)/shard_map/ppermute | solution.py:29
  51.5 0.8 collective-permute-start.6
  52.4 6.2 %collective-permute-start.10 = (bf16[96,2048]{1,0:T(8,128)(2,1)S(1)}, bf16[96,2048]{1,0:T(8,128)(2,1)}, u32[]{:S(2)}, u32[]{:S(2)}) collective-permute-start(bf16[96,2048]{1,0:T(8,128)(2,1)S(1)} %pad_maximum_fusion), channel_id=1, source_target_pairs={{0,128},{1,192},{2,0},{3,64},{64,129},{65,193},{66,1},{67,65},{128... | collective-permute-start | bytes 1179656 | tf_op jit(solution)/shard_map/ppermute | solution.py:29
  58.6 2.6 %collective-permute-start.9 = (bf16[96,2048]{1,0:T(8,128)(2,1)S(1)}, bf16[96,2048]{1,0:T(8,128)(2,1)}, u32[]{:S(2)}, u32[]{:S(2)}) collective-permute-start(bf16[96,2048]{1,0:T(8,128)(2,1)S(1)} %pad_maximum_fusion), channel_id=1, source_target_pairs={{0,0},{1,64},{2,128},{3,192},{64,1},{65,65},{66,129},{67,193},{128... | collective-permute-start | bytes 1179656 | tf_op jit(solution)/shard_map/ppermute | solution.py:29
  61.2 0.6 pad_add_fusion.at
  61.8 0.6 broadcast_in_dim.33.qkv_bias
  62.4 0.8 broadcast_in_dim.39.out_bias
  63.3 0.7 copy-done.21
  64.0 9.1 %attention.1 = (bf16[96,256]{1,0:T(8,128)(2,1)}, bf16[96,256]{1,0:T(8,128)(2,1)}, bf16[96,256]{1,0:T(8,128)(2,1)}, bf16[96,256]{1,0:T(8,128)(2,1)}, f32[64,1,128]{2,1,0:T(1,128)}) custom-call(s32[4]{0:T(128)} %pad_add_fusion.at, bf16[8,112,256]{2,1,0:T(8,128)(2,1)} %copy-done.6, bf16[8,112,256]{2,1,0:T(8,128)(2,1)} %copy-done.19, ...), custom_call_target="tpu_custom_call" | custom-call | flops 4000000000 | bytes 20000000 | tf_op jit(solution)/shard_map/attention/pallas_call | solution.py:393
  73.2 1.8 collective-permute-done.10.near1
  75.4 1.9 collective-permute-start.13
  77.3 16.7 %all-to-all-start.1 = ((f32[64,1,128]{2,1,0:T(1,128)}), f32[64,1,128]{2,1,0:T(1,128)S(1)}, u32[]{:S(2)}, u32[]{:S(2)}) async-start(f32[64,1,128]{2,1,0:T(1,128)} %get-tuple-element.41), calls=%async_computation.1 | async-start | bytes 65536 | tf_op jit(solution)/shard_map/all_to_all | solution.py:427
  94.1 0.6 collective-permute-start.14
  94.7 3.3 %collective-permute-start.15 = (bf16[96,256]{1,0:T(8,128)(2,1)}, bf16[96,256]{1,0:T(8,128)(2,1)S(1)}, u32[]{:S(2)}, u32[]{:S(2)}) collective-permute-start(bf16[96,256]{1,0:T(8,128)(2,1)} %get-tuple-element.52), channel_id=1, source_target_pairs={{0,128},{16,160},{32,192},{48,224},{64,144},{80,176},{96,208},{112... | collective-permute-start | bytes 147464 | tf_op jit(solution)/shard_map/ppermute | solution.py:29
  98.0 1.6 collective-permute-start.16
  99.6 1.8 all-to-all-done.1
  101.7 3.3 %collective-permute-done.16.piece3 = bf16[96,256]{1,0:T(8,128)(2,1)S(1)} collective-permute-done((bf16[96,256]{1,0:T(8,128)(2,1)}, bf16[96,256]{1,0:T(8,128)(2,1)S(1)}, u32[]{:S(2)}, u32[]{:S(2)}) %collective-permute-start.16) | collective-permute-done | bytes 49184 | tf_op jit(solution)/shard_map/ppermute | solution.py:29
  105.1 0.6 copy-done.11
  105.7 1.7 arrange.1
  107.3 2.1 collective-permute-start.21
  109.4 2.7 %collective-permute-start.19 = (f32[1,128]{1,0:T(1,128)S(1)}, f32[1,128]{1,0:T(1,128)S(1)}, u32[]{:S(2)}, u32[]{:S(2)}) collective-permute-start(f32[1,128]{1,0:T(1,128)S(1)} %bitcast.54), channel_id=1, source_target_pairs={{0,3},{1,0},{2,1},{3,2},{4,7},{5,4},{6,5},{7,6},{8,11},{9,8},{10,9... | collective-permute-start | bytes 1544 | tf_op jit(solution)/shard_map/ppermute | solution.py:29
  112.1 0.7 pad_add_fusion.1.at
  113.0 4.6 %collective-permute-done.19 = f32[1,128]{1,0:T(1,128)S(1)} collective-permute-done((f32[1,128]{1,0:T(1,128)S(1)}, f32[1,128]{1,0:T(1,128)S(1)}, u32[]{:S(2)}, u32[]{:S(2)}) %collective-permute-start.19) | collective-permute-done | bytes 544 | tf_op jit(solution)/shard_map/ppermute | solution.py:29
  117.6 0.7 copy.22.gain
  118.3 0.7 copy.23.shift
  119.0 2.2 %collective-permute-done.17 = f32[1,128]{1,0:T(1,128)S(1)} collective-permute-done((f32[1,128]{1,0:T(1,128)S(1)}, f32[1,128]{1,0:T(1,128)S(1)}, u32[]{:S(2)}, u32[]{:S(2)}) %collective-permute-start.17) | collective-permute-done | bytes 544 | tf_op jit(solution)/shard_map/ppermute | solution.py:29
  121.2 0.6 pad_maximum_fusion.1.table
  121.8 0.6 copy-done.24
  122.5 0.7 copy-done.26
  123.2 6.5 %weight_grad.1 = bf16[128,16,128]{2,1,0:T(8,128)(2,1)} custom-call(s32[4]{0:T(128)} %pad_add_fusion.1.at, f32[4,128]{1,0:T(4,128)} %pad_maximum_fusion.1.table, bf16[96,1024]{1,0:T(8,128)(2,1)} %get-tuple-element.60.clip0.clip, bf16[96,1024]{1,0:T(8,128)(2,1)} %copy-done.26, bf16[96,1024]{1,0:T(8,128)(2,1)} %copy-done.25, bf16[96,1024]{1,0:T(8,128)(2,1)} %copy-done.24, ...), custom_call_target="tpu_custom_call" | custom-call | flops 4000000000 | bytes 20000000 | tf_op jit(solution)/shard_map/weight_grad/pallas_call | solution.py:450
  129.7 3.1 %collective-permute-start.23 = (bf16[96,512]{1,0:T(8,128)(2,1)}, bf16[96,512]{1,0:T(8,128)(2,1)S(1)}, u32[]{:S(2)}, u32[]{:S(2)}) collective-permute-start(bf16[96,512]{1,0:T(8,128)(2,1)} %get-tuple-element.67), channel_id=1, source_target_pairs={{0,4},{4,8},{8,12},{12,16},{16,20},{20,24},{24,28},{28,32},{32,36}... | collective-permute-start | bytes 294920 | tf_op jit(solution)/shard_map/ppermute | solution.py:29
  132.8 4.3 %collective-permute-start.24 = (bf16[96,512]{1,0:T(8,128)(2,1)}, bf16[96,512]{1,0:T(8,128)(2,1)S(1)}, u32[]{:S(2)}, u32[]{:S(2)}) collective-permute-start(bf16[96,512]{1,0:T(8,128)(2,1)} %get-tuple-element.68), channel_id=1, source_target_pairs={{4,0},{8,4},{12,8},{16,12},{20,16},{24,20},{28,24},{32,28},{36,32}... | collective-permute-start | bytes 294920 | tf_op jit(solution)/shard_map/ppermute | solution.py:29
  137.1 0.7 pad_add_fusion.2.at
  137.8 5.3 %all-to-all-start.2 = ((bf16[16,8,16,128]{3,2,1,0:T(8,128)(2,1)}), bf16[16,8,16,128]{3,2,1,0:T(8,128)(2,1)S(1)}, u32[]{:S(2)}, u32[]{:S(2)}) async-start(bf16[16,8,16,128]{3,2,1,0:T(8,128)(2,1)} %bitcast.48), calls=%async_computation.2 | async-start | bytes 1048576 | tf_op jit(solution)/shard_map/all_to_all | solution.py:469
  143.1 2.4 %copy.24.weight = bf16[3,384,864]{2,1,0:T(8,128)(2,1)} copy(bf16[3,384,864]{1,2,0:T(8,128)(2,1)S(1)} %bitcast.47) | data formatting | bytes 3981312 | tf_op jit(solution)/shard_map/reshape | solution.py:468
  145.5 0.6 copy-done.27
  146.1 0.6 copy-done.28
  146.7 5.8 %convolution.1 = (bf16[2,96,1024]{2,1,0:T(8,128)(2,1)}, bf16[2,96,1024]{2,1,0:T(8,128)(2,1)}) custom-call(s32[3]{0:T(128)} %pad_add_fusion.2.at, f32[4,128]{1,0:T(4,128)} %pad_maximum_fusion.1.table, bf16[96,1024]{1,0:T(8,128)(2,1)} %get-tuple-element.60.clip0.clip, bf16[96,512]{1,0:T(8,128)(2,1)} %copy-done.27, bf16[96,512]{1,0:T(8,128)(2,1)} %copy-done.28, ...), custom_call_target="tpu_custom_call" | custom-call | flops 3000000000 | bytes 12000000 | tf_op jit(solution)/shard_map/convolution/pallas_call | solution.py:470
  152.6 2.5 %collective-permute-start.25 = (bf16[2,96,1024]{2,1,0:T(8,128)(2,1)}, bf16[2,96,1024]{2,1,0:T(8,128)(2,1)S(1)}, u32[]{:S(2)}, u32[]{:S(2)}) collective-permute-start(bf16[2,96,1024]{2,1,0:T(8,128)(2,1)} %get-tuple-element.71), channel_id=1, source_target_pairs={{0,64},{64,0},{1,65},{65,1},{2,66},{66,2},{3,67},{67,3},{4,68},{68... | collective-permute-start | bytes 1179656 | tf_op jit(solution)/shard_map/ppermute | solution.py:29
  155.1 1.6 collective-permute-done.25
  156.6 1.1 convert_add_fusion
  158.0 21.4 %all_to_all.20 = bf16[16,8,16,128]{3,2,1,0:T(8,128)(2,1)S(1)} all-to-all(bf16[16,8,16,128]{3,2,1,0:T(8,128)(2,1)S(1)} %broadcast_in_dim.38), channel_id=1, replica_groups=mesh['zh'=2,'co'=2,'zl'=4,'x'=4,'y'=4] {'zl','x'}, dimensions={0} | all-to-all | bytes 1048576 | tf_op jit(solution)/shard_map/all_to_all | solution.py:50
  179.4 3.2 %collective-permute-start.26 = (bf16[96,1024]{1,0:T(8,128)(2,1)S(1)}, bf16[96,1024]{1,0:T(8,128)(2,1)S(1)}, u32[]{:S(2)}, u32[]{:S(2)}) collective-permute-start(bf16[96,1024]{1,0:T(8,128)(2,1)S(1)} %fusion.1), channel_id=1, source_target_pairs={{0,128},{128,0},{1,129},{129,1},{2,130},{130,2},{3,131},{131,3},{4... | collective-permute-start | bytes 589832 | tf_op jit(solution)/shard_map/ppermute | solution.py:29
  182.6 1.0 collective-permute-start.28
  183.6 0.5 collective-permute-start.27
  184.1 9.5 %collective-permute-done.26 = bf16[96,1024]{1,0:T(8,128)(2,1)S(1)} collective-permute-done((bf16[96,1024]{1,0:T(8,128)(2,1)S(1)}, bf16[96,1024]{1,0:T(8,128)(2,1)S(1)}, u32[]{:S(2)}, u32[]{:S(2)}) %collective-permute-start.26) | collective-permute-done | bytes 196640 | tf_op jit(solution)/shard_map/ppermute | solution.py:29
  194.0 0.9 fusion
  194.9 1.2 collective-permute-done.28.table2
  196.1 13.0 %collective-permute-done.27.table1 = bf16[128,16,128]{2,1,0:T(8,128)(2,1)S(1)} collective-permute-done((bf16[128,16,128]{2,1,0:T(8,128)(2,1)S(1)}, bf16[128,16,128]{2,1,0:T(8,128)(2,1)S(1)}, u32[]{:S(2)}, u32[]{:S(2)}) %collective-permute-start.27) | collective-permute-done | bytes 524320 | tf_op jit(solution)/shard_map/ppermute | solution.py:29
  209.2 0.8 copy-done.5
  210.0 4.4 %join.1 = f32[2592,384]{1,0:T(8,128)} custom-call(s32[1]{0:T(128)} %bitcast.9.at, bf16[128,16,128]{2,1,0:T(8,128)(2,1)} %bitcast.46, bf16[128,16,128]{2,1,0:T(8,128)(2,1)} %copy-done.5, bf16[128,16,128]{2,1,0:T(8,128)(2,1)} %copy-done.4, bf16[128,16,128]{2,1,0:T(8,128)(2,1)} %copy-done.3), custom_call_target="tpu_custom_call" | custom-call | flops 1000000 | bytes 6000000 | tf_op jit(solution)/shard_map/join/pallas_call | solution.py:497
  (97 shorter events, 2.6 us)
Async XLA Ops:
  0.6 12.0 %copy-start.2 = (bf16[96,1,4,2,128]{4,3,2,1,0:T(2,128)(2,1)S(1)}, bf16[96,1,4,2,128]{4,3,2,1,0:T(2,128)(2,1)}, u32[]{:S(2)}) copy-start(bf16[96,1,4,2,128]{4,3,2,1,0:T(2,128)(2,1)} %param.25) | copy-start | bytes 589828
  4.9 56.9 %copy-start.12 = (f32[1152]{0:T(1024)S(1)}, f32[1152]{0:T(1024)}, u32[]{:S(2)}) copy-start(f32[1152]{0:T(1024)} %param.18) | copy-start | bytes 13828
  4.9 57.5 %copy-start.13 = (f32[384]{0:T(512)S(1)}, f32[384]{0:T(512)}, u32[]{:S(2)}) copy-start(f32[384]{0:T(512)} %param.20) | copy-start | bytes 4612
  4.9 21.5 %all-to-all-start = ((bf16[8,112,256]{2,1,0:T(8,128)(2,1)}), bf16[8,112,256]{2,1,0:T(8,128)(2,1)S(1)}, u32[]{:S(2)}, u32[]{:S(2)}) async-start(bf16[8,112,256]{2,1,0:T(8,128)(2,1)} %pack.1), calls=%async_computation | async-start | bytes 917504 | tf_op jit(solution)/shard_map/all_to_all | solution.py:374
  14.0 8.8 %collective-permute-start.1 = (bf16[96,512]{1,0:T(8,128)(2,1)S(1)}, bf16[96,512]{1,0:T(8,128)(2,1)S(1)}, u32[]{:S(2)}, u32[]{:S(2)}) collective-permute-start(bf16[96,512]{1,0:T(8,128)(2,1)S(1)} %bitcast.51), channel_id=1, source_target_pairs={{4,0},{8,4},{12,8},{16,12},{20,16},{24,20},{28,24},{32,28},{36,32}... | collective-permute-start | bytes 294920 | tf_op jit(solution)/shard_map/ppermute | solution.py:29
  18.4 8.0 %collective-permute-start = (bf16[96,512]{1,0:T(8,128)(2,1)S(1)}, bf16[96,512]{1,0:T(8,128)(2,1)S(1)}, u32[]{:S(2)}, u32[]{:S(2)}) collective-permute-start(bf16[96,512]{1,0:T(8,128)(2,1)S(1)} %bitcast.52), channel_id=1, source_target_pairs={{0,4},{4,8},{8,12},{12,16},{16,20},{20,24},{24,28},{28,32},{32,36}... | collective-permute-start | bytes 294920 | tf_op jit(solution)/shard_map/ppermute | solution.py:29
  26.5 36.8 %copy-start.6 = (bf16[8,112,256]{2,1,0:T(8,128)(2,1)}, bf16[8,112,256]{2,1,0:T(8,128)(2,1)S(1)}, u32[]{:S(2)}) copy-start(bf16[8,112,256]{2,1,0:T(8,128)(2,1)S(1)} %all-to-all-done.own0) | copy-start | bytes 1376260
  26.5 12.4 %collective-permute-start.4 = (bf16[8,112,256]{2,1,0:T(8,128)(2,1)S(1)}, bf16[8,112,256]{2,1,0:T(8,128)(2,1)S(1)}, u32[]{:S(2)}, u32[]{:S(2)}) collective-permute-start(bf16[8,112,256]{2,1,0:T(8,128)(2,1)S(1)} %all-to-all-done.own0), channel_id=1, source_target_pairs={{0,12},{4,0},{8,4},{12,8},{1,13},{5,1},{9,5},{13,9},{2,14},{6,2},{... | collective-permute-start | bytes 1376264 | tf_op jit(solution)/shard_map/ppermute | solution.py:29
  28.4 20.6 %collective-permute-start.3 = (bf16[8,112,256]{2,1,0:T(8,128)(2,1)S(1)}, bf16[8,112,256]{2,1,0:T(8,128)(2,1)S(1)}, u32[]{:S(2)}, u32[]{:S(2)}) collective-permute-start(bf16[8,112,256]{2,1,0:T(8,128)(2,1)S(1)} %all-to-all-done.own0), channel_id=1, source_target_pairs={{0,8},{4,12},{8,0},{12,4},{1,9},{5,13},{9,1},{13,5},{2,10},{6,14},... | collective-permute-start | bytes 1376264 | tf_op jit(solution)/shard_map/ppermute | solution.py:29
  28.4 23.1 %collective-permute-start.2 = (bf16[8,112,256]{2,1,0:T(8,128)(2,1)S(1)}, bf16[8,112,256]{2,1,0:T(8,128)(2,1)S(1)}, u32[]{:S(2)}, u32[]{:S(2)}) collective-permute-start(bf16[8,112,256]{2,1,0:T(8,128)(2,1)S(1)} %all-to-all-done.own0), channel_id=1, source_target_pairs={{0,4},{4,8},{8,12},{12,0},{1,5},{5,9},{9,13},{13,1},{2,6},{6,10},{... | collective-permute-start | bytes 1376264 | tf_op jit(solution)/shard_map/ppermute | solution.py:29
  29.1 29.5 %collective-permute-start.5 = (bf16[8,112,256]{2,1,0:T(8,128)(2,1)S(1)}, bf16[8,112,256]{2,1,0:T(8,128)(2,1)S(1)}, u32[]{:S(2)}, u32[]{:S(2)}) collective-permute-start(bf16[8,112,256]{2,1,0:T(8,128)(2,1)S(1)} %all-to-all-done.own0), channel_id=1, source_target_pairs={{0,64},{64,0},{1,65},{65,1},{2,66},{66,2},{3,67},{67,3},{4,68},{68... | collective-permute-start | bytes 1376264 | tf_op jit(solution)/shard_map/ppermute | solution.py:29
  38.9 24.4 %copy-start.17 = (bf16[8,112,256]{2,1,0:T(8,128)(2,1)}, bf16[8,112,256]{2,1,0:T(8,128)(2,1)S(1)}, u32[]{:S(2)}) copy-start(bf16[8,112,256]{2,1,0:T(8,128)(2,1)S(1)} %collective-permute-done.4.own3) | copy-start | bytes 1376260
  38.9 24.3 %collective-permute-start.8 = (bf16[8,112,256]{2,1,0:T(8,128)(2,1)S(1)}, bf16[8,112,256]{2,1,0:T(8,128)(2,1)S(1)}, u32[]{:S(2)}, u32[]{:S(2)}) collective-permute-start(bf16[8,112,256]{2,1,0:T(8,128)(2,1)S(1)} %collective-permute-done.4.own3), channel_id=1, source_target_pairs={{0,64},{64,0},{1,65},{65,1},{2,66},{66,2},{3,67},{67,3},{4,68},{68... | collective-permute-start | bytes 1376264 | tf_op jit(solution)/shard_map/ppermute | solution.py:29
  49.0 14.3 %copy-start.18 = (bf16[8,112,256]{2,1,0:T(8,128)(2,1)}, bf16[8,112,256]{2,1,0:T(8,128)(2,1)S(1)}, u32[]{:S(2)}) copy-start(bf16[8,112,256]{2,1,0:T(8,128)(2,1)S(1)} %collective-permute-done.3.own2) | copy-start | bytes 1376260
  49.0 14.2 %collective-permute-start.7 = (bf16[8,112,256]{2,1,0:T(8,128)(2,1)S(1)}, bf16[8,112,256]{2,1,0:T(8,128)(2,1)}, u32[]{:S(2)}, u32[]{:S(2)}) collective-permute-start(bf16[8,112,256]{2,1,0:T(8,128)(2,1)S(1)} %collective-permute-done.3.own2), channel_id=1, source_target_pairs={{0,64},{64,0},{1,65},{65,1},{2,66},{66,2},{3,67},{67,3},{4,68},{68... | collective-permute-start | bytes 1376264 | tf_op jit(solution)/shard_map/ppermute | solution.py:29
  51.5 11.8 %copy-start.19 = (bf16[8,112,256]{2,1,0:T(8,128)(2,1)}, bf16[8,112,256]{2,1,0:T(8,128)(2,1)S(1)}, u32[]{:S(2)}) copy-start(bf16[8,112,256]{2,1,0:T(8,128)(2,1)S(1)} %collective-permute-done.2.own1) | copy-start | bytes 1376260
  51.5 11.7 %collective-permute-start.6 = (bf16[8,112,256]{2,1,0:T(8,128)(2,1)S(1)}, bf16[8,112,256]{2,1,0:T(8,128)(2,1)}, u32[]{:S(2)}, u32[]{:S(2)}) collective-permute-start(bf16[8,112,256]{2,1,0:T(8,128)(2,1)S(1)} %collective-permute-done.2.own1), channel_id=1, source_target_pairs={{0,64},{64,0},{1,65},{65,1},{2,66},{66,2},{3,67},{67,3},{4,68},{68... | collective-permute-start | bytes 1376264 | tf_op jit(solution)/shard_map/ppermute | solution.py:29
  52.4 22.5 %collective-permute-start.10 = (bf16[96,2048]{1,0:T(8,128)(2,1)S(1)}, bf16[96,2048]{1,0:T(8,128)(2,1)}, u32[]{:S(2)}, u32[]{:S(2)}) collective-permute-start(bf16[96,2048]{1,0:T(8,128)(2,1)S(1)} %pad_maximum_fusion), channel_id=1, source_target_pairs={{0,128},{1,192},{2,0},{3,64},{64,129},{65,193},{66,1},{67,65},{128... | collective-permute-start | bytes 1179656 | tf_op jit(solution)/shard_map/ppermute | solution.py:29
  58.6 4.7 %copy-start.20 = (bf16[8,112,256]{2,1,0:T(8,128)(2,1)}, bf16[8,112,256]{2,1,0:T(8,128)(2,1)S(1)}, u32[]{:S(2)}) copy-start(bf16[8,112,256]{2,1,0:T(8,128)(2,1)S(1)} %collective-permute-done.5.other0) | copy-start | bytes 1376260
  58.6 16.3 %collective-permute-start.9 = (bf16[96,2048]{1,0:T(8,128)(2,1)S(1)}, bf16[96,2048]{1,0:T(8,128)(2,1)}, u32[]{:S(2)}, u32[]{:S(2)}) collective-permute-start(bf16[96,2048]{1,0:T(8,128)(2,1)S(1)} %pad_maximum_fusion), channel_id=1, source_target_pairs={{0,0},{1,64},{2,128},{3,192},{64,1},{65,65},{66,129},{67,193},{128... | collective-permute-start | bytes 1179656 | tf_op jit(solution)/shard_map/ppermute | solution.py:29
  63.2 54.3 %copy-start.14 = (f32[96]{0:T(128)S(1)}, f32[96]{0:T(128)}, u32[]{:S(2)}) copy-start(f32[96]{0:T(128)} %param.21) | copy-start | bytes 1156
  63.2 55.1 %copy-start.15 = (f32[96]{0:T(128)S(1)}, f32[96]{0:T(128)}, u32[]{:S(2)}) copy-start(f32[96]{0:T(128)} %param.22) | copy-start | bytes 1156
  63.2 0.8 copy-start.21
  74.9 30.1 %collective-permute-start.11 = (bf16[96,2048]{1,0:T(8,128)(2,1)}, bf16[96,2048]{1,0:T(8,128)(2,1)S(1)}, u32[]{:S(2)}, u32[]{:S(2)}) collective-permute-start(bf16[96,2048]{1,0:T(8,128)(2,1)} %collective-permute-done.9.near0), channel_id=1, source_target_pairs={{0,64},{64,0},{1,65},{65,1},{2,66},{66,2},{3,67},{67,3},{4,68},{68... | collective-permute-start | bytes 1179656 | tf_op jit(solution)/shard_map/ppermute | solution.py:29
  75.2 29.8 %collective-permute-start.12 = (bf16[96,2048]{1,0:T(8,128)(2,1)}, bf16[96,2048]{1,0:T(8,128)(2,1)S(1)}, u32[]{:S(2)}, u32[]{:S(2)}) collective-permute-start(bf16[96,2048]{1,0:T(8,128)(2,1)} %collective-permute-done.10.near1), channel_id=1, source_target_pairs={{0,64},{64,0},{1,65},{65,1},{2,66},{66,2},{3,67},{67,3},{4,68},{68... | collective-permute-start | bytes 1179656 | tf_op jit(solution)/shard_map/ppermute | solution.py:29
  75.4 22.6 %collective-permute-start.13 = (bf16[96,256]{1,0:T(8,128)(2,1)}, bf16[96,256]{1,0:T(8,128)(2,1)S(1)}, u32[]{:S(2)}, u32[]{:S(2)}) collective-permute-start(bf16[96,256]{1,0:T(8,128)(2,1)} %get-tuple-element.50), channel_id=1, source_target_pairs={{0,0},{16,32},{32,64},{48,96},{64,16},{80,48},{96,80},{112,112},{1... | collective-permute-start | bytes 147464 | tf_op jit(solution)/shard_map/ppermute | solution.py:29
  77.3 24.1 %all-to-all-start.1 = ((f32[64,1,128]{2,1,0:T(1,128)}), f32[64,1,128]{2,1,0:T(1,128)S(1)}, u32[]{:S(2)}, u32[]{:S(2)}) async-start(f32[64,1,128]{2,1,0:T(1,128)} %get-tuple-element.41), calls=%async_computation.1 | async-start | bytes 65536 | tf_op jit(solution)/shard_map/all_to_all | solution.py:427
  94.1 7.4 %collective-permute-start.14 = (bf16[96,256]{1,0:T(8,128)(2,1)}, bf16[96,256]{1,0:T(8,128)(2,1)S(1)}, u32[]{:S(2)}, u32[]{:S(2)}) collective-permute-start(bf16[96,256]{1,0:T(8,128)(2,1)} %get-tuple-element.51), channel_id=1, source_target_pairs={{0,64},{16,96},{32,0},{48,32},{64,80},{80,112},{96,16},{112,48},{1... | collective-permute-start | bytes 147464 | tf_op jit(solution)/shard_map/ppermute | solution.py:29
  94.7 7.0 %collective-permute-start.15 = (bf16[96,256]{1,0:T(8,128)(2,1)}, bf16[96,256]{1,0:T(8,128)(2,1)S(1)}, u32[]{:S(2)}, u32[]{:S(2)}) collective-permute-start(bf16[96,256]{1,0:T(8,128)(2,1)} %get-tuple-element.52), channel_id=1, source_target_pairs={{0,128},{16,160},{32,192},{48,224},{64,144},{80,176},{96,208},{112... | collective-permute-start | bytes 147464 | tf_op jit(solution)/shard_map/ppermute | solution.py:29
  98.0 7.1 %copy-start.8 = (bf16[96,256]{1,0:T(8,128)(2,1)}, bf16[96,256]{1,0:T(8,128)(2,1)S(1)}, u32[]{:S(2)}) copy-start(bf16[96,256]{1,0:T(8,128)(2,1)S(1)} %collective-permute-done.13.piece0) | copy-start | bytes 147460
  98.0 7.0 %collective-permute-start.16 = (bf16[96,256]{1,0:T(8,128)(2,1)}, bf16[96,256]{1,0:T(8,128)(2,1)S(1)}, u32[]{:S(2)}, u32[]{:S(2)}) collective-permute-start(bf16[96,256]{1,0:T(8,128)(2,1)} %get-tuple-element.53), channel_id=1, source_target_pairs={{0,192},{16,224},{32,128},{48,160},{64,208},{80,240},{96,144},{112... | collective-permute-start | bytes 147464 | tf_op jit(solution)/shard_map/ppermute | solution.py:29
  101.5 3.5 %copy-start.9 = (bf16[96,256]{1,0:T(8,128)(2,1)}, bf16[96,256]{1,0:T(8,128)(2,1)S(1)}, u32[]{:S(2)}) copy-start(bf16[96,256]{1,0:T(8,128)(2,1)S(1)} %collective-permute-done.14.piece1) | copy-start | bytes 147460
  101.7 3.4 %copy-start.10 = (bf16[96,256]{1,0:T(8,128)(2,1)}, bf16[96,256]{1,0:T(8,128)(2,1)S(1)}, u32[]{:S(2)}) copy-start(bf16[96,256]{1,0:T(8,128)(2,1)S(1)} %collective-permute-done.15.piece2) | copy-start | bytes 147460
  105.0 0.6 copy-start.11
  105.0 16.7 %copy-start.22 = (bf16[96,2048]{1,0:T(8,128)(2,1)}, bf16[96,2048]{1,0:T(8,128)(2,1)S(1)}, u32[]{:S(2)}) copy-start(bf16[96,2048]{1,0:T(8,128)(2,1)S(1)} %collective-permute-done.11.far0) | copy-start | bytes 1179652
  105.1 16.7 %copy-start.23 = (bf16[96,2048]{1,0:T(8,128)(2,1)}, bf16[96,2048]{1,0:T(8,128)(2,1)S(1)}, u32[]{:S(2)}) copy-start(bf16[96,2048]{1,0:T(8,128)(2,1)S(1)} %collective-permute-done.12.far1) | copy-start | bytes 1179652
  107.3 14.4 %collective-permute-start.22 = (bf16[96,1024]{1,0:T(8,128)(2,1)}, bf16[96,1024]{1,0:T(8,128)(2,1)S(1)}, u32[]{:S(2)}, u32[]{:S(2)}) collective-permute-start(bf16[96,1024]{1,0:T(8,128)(2,1)} %get-tuple-element.60.clip0.clip), channel_id=1, source_target_pairs={{0,3},{1,0},{2,1},{3,2},{4,7},{5,4},{6,5},{7,6},{8,11},{9,8},{10,9... | collective-permute-start | bytes 589832 | tf_op jit(solution)/shard_map/ppermute | solution.py:29
  107.3 14.4 %collective-permute-start.21 = (bf16[96,1024]{1,0:T(8,128)(2,1)}, bf16[96,1024]{1,0:T(8,128)(2,1)S(1)}, u32[]{:S(2)}, u32[]{:S(2)}) collective-permute-start(bf16[96,1024]{1,0:T(8,128)(2,1)} %get-tuple-element.60.clip0.clip), channel_id=1, source_target_pairs={{0,2},{1,3},{2,0},{3,1},{4,6},{5,7},{6,4},{7,5},{8,10},{9,11},{10,... | collective-permute-start | bytes 589832 | tf_op jit(solution)/shard_map/ppermute | solution.py:29
  109.4 12.4 %collective-permute-start.20 = (bf16[96,1024]{1,0:T(8,128)(2,1)}, bf16[96,1024]{1,0:T(8,128)(2,1)S(1)}, u32[]{:S(2)}, u32[]{:S(2)}) collective-permute-start(bf16[96,1024]{1,0:T(8,128)(2,1)} %get-tuple-element.60.clip0.clip), channel_id=1, source_target_pairs={{0,1},{1,2},{2,3},{3,0},{4,5},{5,6},{6,7},{7,4},{8,9},{9,10},{10,1... | collective-permute-start | bytes 589832 | tf_op jit(solution)/shard_map/ppermute | solution.py:29
  109.4 8.1 %collective-permute-start.19 = (f32[1,128]{1,0:T(1,128)S(1)}, f32[1,128]{1,0:T(1,128)S(1)}, u32[]{:S(2)}, u32[]{:S(2)}) collective-permute-start(f32[1,128]{1,0:T(1,128)S(1)} %bitcast.54), channel_id=1, source_target_pairs={{0,3},{1,0},{2,1},{3,2},{4,7},{5,4},{6,5},{7,6},{8,11},{9,8},{10,9... | collective-permute-start | bytes 1544 | tf_op jit(solution)/shard_map/ppermute | solution.py:29
  112.8 6.3 %collective-permute-start.18 = (f32[1,128]{1,0:T(1,128)S(1)}, f32[1,128]{1,0:T(1,128)S(1)}, u32[]{:S(2)}, u32[]{:S(2)}) collective-permute-start(f32[1,128]{1,0:T(1,128)S(1)} %bitcast.55), channel_id=1, source_target_pairs={{0,2},{1,3},{2,0},{3,1},{4,6},{5,7},{6,4},{7,5},{8,10},{9,11},{10,... | collective-permute-start | bytes 1544 | tf_op jit(solution)/shard_map/ppermute | solution.py:29
  117.6 3.6 %collective-permute-start.17 = (f32[1,128]{1,0:T(1,128)S(1)}, f32[1,128]{1,0:T(1,128)S(1)}, u32[]{:S(2)}, u32[]{:S(2)}) collective-permute-start(f32[1,128]{1,0:T(1,128)S(1)} %bitcast.56), channel_id=1, source_target_pairs={{0,1},{1,2},{2,3},{3,0},{4,5},{5,6},{6,7},{7,4},{8,9},{9,10},{10,1... | collective-permute-start | bytes 1544 | tf_op jit(solution)/shard_map/ppermute | solution.py:29
  121.8 0.7 copy-start.24
  121.8 0.8 copy-start.25
  122.5 0.7 copy-start.26
  123.2 19.9 %copy-start.1 = (bf16[3,3,3,96,384]{4,3,2,1,0:T(8,128)(2,1)S(1)}, bf16[3,3,3,96,384]{4,3,2,1,0:T(8,128)(2,1)}, u32[]{:S(2)}) copy-start(bf16[3,3,3,96,384]{4,3,2,1,0:T(8,128)(2,1)} %param.23) | copy-start | bytes 5971972
  129.7 15.8 %collective-permute-start.23 = (bf16[96,512]{1,0:T(8,128)(2,1)}, bf16[96,512]{1,0:T(8,128)(2,1)S(1)}, u32[]{:S(2)}, u32[]{:S(2)}) collective-permute-start(bf16[96,512]{1,0:T(8,128)(2,1)} %get-tuple-element.67), channel_id=1, source_target_pairs={{0,4},{4,8},{8,12},{12,16},{16,20},{20,24},{24,28},{28,32},{32,36}... | collective-permute-start | bytes 294920 | tf_op jit(solution)/shard_map/ppermute | solution.py:29
  132.8 12.7 %collective-permute-start.24 = (bf16[96,512]{1,0:T(8,128)(2,1)}, bf16[96,512]{1,0:T(8,128)(2,1)S(1)}, u32[]{:S(2)}, u32[]{:S(2)}) collective-permute-start(bf16[96,512]{1,0:T(8,128)(2,1)} %get-tuple-element.68), channel_id=1, source_target_pairs={{4,0},{8,4},{12,8},{16,12},{20,16},{24,20},{28,24},{32,28},{36,32}... | collective-permute-start | bytes 294920 | tf_op jit(solution)/shard_map/ppermute | solution.py:29
  137.8 20.1 %all-to-all-start.2 = ((bf16[16,8,16,128]{3,2,1,0:T(8,128)(2,1)}), bf16[16,8,16,128]{3,2,1,0:T(8,128)(2,1)S(1)}, u32[]{:S(2)}, u32[]{:S(2)}) async-start(bf16[16,8,16,128]{3,2,1,0:T(8,128)(2,1)} %bitcast.48), calls=%async_computation.2 | async-start | bytes 1048576 | tf_op jit(solution)/shard_map/all_to_all | solution.py:469
  145.5 0.6 copy-start.27
  146.1 0.6 copy-start.28
  152.6 4.0 %collective-permute-start.25 = (bf16[2,96,1024]{2,1,0:T(8,128)(2,1)}, bf16[2,96,1024]{2,1,0:T(8,128)(2,1)S(1)}, u32[]{:S(2)}, u32[]{:S(2)}) collective-permute-start(bf16[2,96,1024]{2,1,0:T(8,128)(2,1)} %get-tuple-element.71), channel_id=1, source_target_pairs={{0,64},{64,0},{1,65},{65,1},{2,66},{66,2},{3,67},{67,3},{4,68},{68... | collective-permute-start | bytes 1179656 | tf_op jit(solution)/shard_map/ppermute | solution.py:29
  157.7 35.9 %copy-start.7 = (bf16[96,1024]{1,0:T(8,128)(2,1)S(1)}, bf16[96,1024]{1,0:T(8,128)(2,1)}, u32[]{:S(2)}) copy-start(bf16[96,1024]{1,0:T(8,128)(2,1)} %get-tuple-element.60.clip0.clip) | copy-start | bytes 589828
  157.7 35.8 %copy-start.16 = (f32[96]{0:T(128)S(1)}, f32[96]{0:T(128)}, u32[]{:S(2)}) copy-start(f32[96]{0:T(128)} %param.24) | copy-start | bytes 1156
  179.4 29.8 %copy-start = (bf16[16,8,16,128]{3,2,1,0:T(8,128)(2,1)}, bf16[16,8,16,128]{3,2,1,0:T(8,128)(2,1)S(1)}, u32[]{:S(2)}) copy-start(bf16[16,8,16,128]{3,2,1,0:T(8,128)(2,1)S(1)} %all_to_all.20) | copy-start | bytes 1572868
  179.4 14.2 %collective-permute-start.26 = (bf16[96,1024]{1,0:T(8,128)(2,1)S(1)}, bf16[96,1024]{1,0:T(8,128)(2,1)S(1)}, u32[]{:S(2)}, u32[]{:S(2)}) collective-permute-start(bf16[96,1024]{1,0:T(8,128)(2,1)S(1)} %fusion.1), channel_id=1, source_target_pairs={{0,128},{128,0},{1,129},{129,1},{2,130},{130,2},{3,131},{131,3},{4... | collective-permute-start | bytes 589832 | tf_op jit(solution)/shard_map/ppermute | solution.py:29
  182.6 12.3 %collective-permute-start.29 = (bf16[128,16,128]{2,1,0:T(8,128)(2,1)S(1)}, bf16[128,16,128]{2,1,0:T(8,128)(2,1)S(1)}, u32[]{:S(2)}, u32[]{:S(2)}) collective-permute-start(bf16[128,16,128]{2,1,0:T(8,128)(2,1)S(1)} %bitcast.43), channel_id=1, source_target_pairs={{0,3},{1,0},{2,1},{3,2},{4,7},{5,4},{6,5},{7,6},{8,11},{9,8},{10,9... | collective-permute-start | bytes 1572872 | tf_op jit(solution)/shard_map/ppermute | solution.py:29
  182.6 13.5 %collective-permute-start.28 = (bf16[128,16,128]{2,1,0:T(8,128)(2,1)S(1)}, bf16[128,16,128]{2,1,0:T(8,128)(2,1)S(1)}, u32[]{:S(2)}, u32[]{:S(2)}) collective-permute-start(bf16[128,16,128]{2,1,0:T(8,128)(2,1)S(1)} %bitcast.44), channel_id=1, source_target_pairs={{0,2},{1,3},{2,0},{3,1},{4,6},{5,7},{6,4},{7,5},{8,10},{9,11},{10,... | collective-permute-start | bytes 1572872 | tf_op jit(solution)/shard_map/ppermute | solution.py:29
  183.6 25.6 %collective-permute-start.27 = (bf16[128,16,128]{2,1,0:T(8,128)(2,1)S(1)}, bf16[128,16,128]{2,1,0:T(8,128)(2,1)S(1)}, u32[]{:S(2)}, u32[]{:S(2)}) collective-permute-start(bf16[128,16,128]{2,1,0:T(8,128)(2,1)S(1)} %bitcast.45), channel_id=1, source_target_pairs={{0,1},{1,2},{2,3},{3,0},{4,5},{5,6},{6,7},{7,4},{8,9},{9,10},{10,1... | collective-permute-start | bytes 1572872 | tf_op jit(solution)/shard_map/ppermute | solution.py:29
  194.9 14.3 %copy-start.3 = (bf16[128,16,128]{2,1,0:T(8,128)(2,1)}, bf16[128,16,128]{2,1,0:T(8,128)(2,1)S(1)}, u32[]{:S(2)}) copy-start(bf16[128,16,128]{2,1,0:T(8,128)(2,1)S(1)} %collective-permute-done.29.table3) | copy-start | bytes 1572868
  196.1 13.1 %copy-start.4 = (bf16[128,16,128]{2,1,0:T(8,128)(2,1)}, bf16[128,16,128]{2,1,0:T(8,128)(2,1)S(1)}, u32[]{:S(2)}) copy-start(bf16[128,16,128]{2,1,0:T(8,128)(2,1)S(1)} %collective-permute-done.28.table2) | copy-start | bytes 1572868
  209.2 0.8 copy-start.5
